TPU v7x, 768 devices: a whole 4x8x12 slice. The times are simulated.
768 devices in a mesh: grp: 16 (over y, core), shard: 48 (over x, z).
Axes of the slice: x: 4, y: 8, z: 12, core: 2. Of those that a mesh axis runs over, the one named last changes fastest.
Arguments:
- points: bfloat16 [786432, 768], P(('grp', 'shard'))
- serve_new: int32 [36864, 16], P(('grp', 'shard')), may hold values from 0 to 1023
- serve_old: int32 [12288, 32], P(('grp', 'shard')), may hold values from 0 to 1023
- count_new: int32 [36864, 1], P(('grp', 'shard')), may hold values from 0 to 16, as said below
- count_old: int32 [12288, 1], P(('grp', 'shard')), may hold values from 0 to 32, as said below
Outputs:
- nearest: float32 [786432, 16], P(('grp', 'shard'))
- reverse: float32 [786432], P(('grp', 'shard'))
Inputs may be any that keep to these rules, and one draw needn't show every extreme that they name: `serve_new`: entries past a slot list's count are filler rows that take no part. `serve_old`: entries past a slot list's count are filler rows that take no part. `count_new`: each device has one owner of its row group, drawn from the seed, whose count is 16. `count_old`: each device has one owner among the devices of its member index, drawn from the seed, whose count is 32.
All inputs are finite; a program needn't handle non-finite values.
Results may differ from a plain program's by a relative error of at most 0.00069.
Values may be sent and summed in bfloat16 or wider, within the bound.
No kernel may reach another device: no remote copies, remote signals or barrier semaphores. Data moves between devices by JAX's collectives and lax.ppermute only.
A program may use at most 32 MiB of HBM per device.

v0:
```python
import jax
import jax.numpy as jnp
from jax import lax
from jax.sharding import PartitionSpec as P

NEAR = 16


cap_value = 8.0
far_value = 1000000000.0


def distance_block(candidates, points, own_sq):
    cand_sq = jnp.sum(jnp.square(candidates.astype(jnp.float32)), axis=1)
    inner_products = lax.dot_general(
        candidates, points, (((1,), (1,)), ((), ())), preferred_element_type=jnp.float32
    )
    return cand_sq[:, None] + own_sq[None, :] - 2.0 * inner_products


def body(points, serve_new, serve_old, count_new, count_old):
    row_count, features = points.shape
    peer_count, slot_count = serve_new.shape
    group_count, group_slots = serve_old.shape
    split_at = peer_count * slot_count
    own_sq = jnp.sum(jnp.square(points.astype(jnp.float32)), axis=1)
    offered_new = jnp.take(points, serve_new, axis=0)
    offered_old = jnp.take(points, serve_old, axis=0)
    pulled_new = lax.all_to_all(offered_new, "shard", split_axis=0, concat_axis=0, tiled=True)
    pulled_old = lax.all_to_all(offered_old, "grp", split_axis=0, concat_axis=0, tiled=True)
    candidates = jnp.concatenate(
        [
            pulled_new.reshape(split_at, features),
            pulled_old.reshape(group_count * group_slots, features),
        ],
        axis=0,
    )
    distances = distance_block(candidates, points, own_sq)
    usable_new = jnp.arange(slot_count, dtype=jnp.int32)[None, :] < count_new
    usable_old = jnp.arange(group_slots, dtype=jnp.int32)[None, :] < count_old
    usable = jnp.concatenate([usable_new.reshape(-1), usable_old.reshape(-1)])
    masked = jnp.where(usable[:, None], distances, far_value)
    nearest = jnp.sort(masked.T, axis=1)[:, :NEAR]
    tiles = jnp.where(usable[:, None], distances, cap_value).astype(jnp.bfloat16)
    slot_minima = jnp.min(tiles, axis=1)
    first_minima = slot_minima[:split_at].reshape(peer_count, slot_count)
    second_minima = slot_minima[split_at:].reshape(group_count, group_slots)
    back_new = lax.all_to_all(
        first_minima, "shard", split_axis=0, concat_axis=0, tiled=True
    ).astype(jnp.float32)
    back_old = lax.all_to_all(second_minima, "grp", split_axis=0, concat_axis=0, tiled=True).astype(
        jnp.float32
    )
    served = jnp.concatenate([serve_new.reshape(-1), serve_old.reshape(-1)])
    minima = jnp.concatenate([back_new.reshape(-1), back_old.reshape(-1)])
    matches = served[None, :] == jnp.arange(row_count, dtype=jnp.int32)[:, None]
    reverse = jnp.minimum(
        cap_value, jnp.min(jnp.where(matches, minima[None, :], cap_value), axis=1)
    )
    return (nearest, reverse)


def solution(mesh):
    placed = (
        P(("grp", "shard"), None),
        P(("grp", "shard"), None),
        P(("grp", "shard"), None),
        P(("grp", "shard"), None),
        P(("grp", "shard"), None),
    )
    return jax.shard_map(
        body,
        mesh=mesh,
        in_specs=placed,
        out_specs=(P(("grp", "shard"), None), P(("grp", "shard"))),
        check_vma=False,
    )
```

profile of v0, /device:TPU:1, one launch (start us, length us, event | category | flops | bytes accessed | tf_op | source)
XLA Modules:
  0.0 498.8 jit_solution(14865738368117742065)
XLA Ops:
  0.6 0.7 compare_select_fusion
  1.3 0.7 compare_and_fusion
  2.0 0.1 reshape.85
  2.1 0.0 copy-start.2
  2.1 0.0 copy-start
  2.1 4.1 gather_fusion.1
  6.3 1.1 broadcast_select_fusion.1
  7.3 13.9 %all-to-all-start.1 = ((bf16[16,32,768]{2,1,0:T(8,128)(2,1)}), bf16[16,32,768]{2,1,0:T(8,128)(2,1)S(1)}, u32[]{:S(2)}, u32[]{:S(2)}) async-start(bf16[16,32,768]{2,1,0:T(8,128)(2,1)} %broadcast_select_fusion.1), calls=%async_computation.1 | async-start | bytes 1572864 | tf_op jit(solution)/shard_map/all_to_all | solution.py:30
  21.3 0.0 copy-done.2
  21.3 0.1 copy.19
  21.4 0.1 reshape.77
  21.4 0.0 copy-done
  21.5 2.8 gather_fusion
  24.2 0.0 copy-start.4
  24.2 0.7 copy.18
  24.9 1.9 broadcast_select_fusion
  26.8 17.1 %all-to-all-done.1 = bf16[16,32,768]{2,1,0:T(8,128)(2,1)S(1)} async-done(((bf16[16,32,768]{2,1,0:T(8,128)(2,1)}), bf16[16,32,768]{2,1,0:T(8,128)(2,1)S(1)}, u32[]{:S(2)}, u32[]{:S(2)}) %all-to-all-start.1) | async-done | bytes 786464 | tf_op jit(solution)/shard_map/all_to_all | solution.py:30
  44.0 12.7 %all-to-all-start = ((bf16[48,16,768]{2,1,0:T(8,128)(2,1)}), bf16[48,16,768]{2,1,0:T(8,128)(2,1)S(1)}, u32[]{:S(2)}, u32[]{:S(2)}) async-start(bf16[48,16,768]{2,1,0:T(8,128)(2,1)} %broadcast_select_fusion), calls=%async_computation | async-start | bytes 2359296 | tf_op jit(solution)/shard_map/all_to_all | solution.py:29
  56.6 0.0 copy-done.4
  56.7 0.7 iota_compare_fusion.1
  57.3 0.8 lt.58
  58.1 0.7 iota_compare_fusion.2
  58.8 0.6 lt.63
  59.4 1.4 dynamic-update-slice
  60.8 1.4 dynamic-update-slice.1
  62.3 0.4 multiply_reduce_fusion.1
  62.6 37.9 %all-to-all-done = bf16[48,16,768]{2,1,0:T(8,128)(2,1)S(1)} async-done(((bf16[48,16,768]{2,1,0:T(8,128)(2,1)}), bf16[48,16,768]{2,1,0:T(8,128)(2,1)S(1)}, u32[]{:S(2)}, u32[]{:S(2)}) %all-to-all-start) | async-done | bytes 1179680 | tf_op jit(solution)/shard_map/all_to_all | solution.py:29
  100.5 0.5 multiply_reduce_fusion
  101.0 0.0 copy-start.3
  101.0 5.4 %fusion = (f32[1024,1280]{1,0:T(8,128)}, f32[1280,1024]{0,1:T(8,128)S(1)}) fusion(f32[1024]{0:T(1024)S(1)} %multiply_reduce_fusion.1, f32[1280]{0:T(1024)S(1)} %multiply_reduce_fusion, pred[1280]{0:T(1024)(128)(4,1)} %dynamic-update-slice.1, bf16[1024,768]{1,0:T(8,128)(2,1)S(1)} %copy-done, bf16[512,768]{1,0:T(8,128)(2,1)S(1)} %bitcast.15, ...), kind=kOutput, calls=%fused_computation.3 | convolution fusion | flops 2022440960 | bytes 14035200 | tf_op jit(solution)/shard_map/dot_general | solution.py:15
  106.4 0.0 copy-start.1
  106.4 0.0 copy-done.3
  106.4 0.9 fusion.1
  107.3 0.7 all_to_all.25
  108.0 4.7 all-to-all-start.3
  112.7 0.1 copy.20
  112.8 0.0 copy-done.1
  112.8 0.1 reshape.74
  112.8 0.1 reshape.73
  112.9 0.7 all_to_all.24
  113.6 6.0 %all-to-all-done.3 = bf16[16,1,32]{2,1,0:T(2,128)(2,1)S(1)} async-done(((bf16[16,1,32]{2,1,0:T(2,128)(2,1)}), bf16[16,1,32]{2,1,0:T(2,128)(2,1)S(1)}, u32[]{:S(2)}, u32[]{:S(2)}) %all-to-all-start.3) | async-done | bytes 1056 | tf_op jit(solution)/shard_map/all_to_all | solution.py:51
  119.6 7.4 %all-to-all-start.2 = ((bf16[48,1,16]{2,1,0:T(2,128)(2,1)}), bf16[48,1,16]{2,1,0:T(2,128)(2,1)S(1)}, u32[]{:S(2)}, u32[]{:S(2)}) async-start(bf16[48,1,16]{2,1,0:T(2,128)(2,1)} %all_to_all.24), calls=%async_computation.2 | async-start | bytes 49152 | tf_op jit(solution)/shard_map/all_to_all | solution.py:48
  127.1 5.9 %copy.24 = f32[1024,1280]{0,1:T(8,128)} copy(f32[1024,1280]{1,0:T(8,128)} %get-tuple-element.13) | data formatting | bytes 10485760
  133.0 2.7 iota.15.clone
  135.7 353.8 %sort.15 = (f32[1024,1280]{0,1:T(8,128)}, s32[1024,1280]{0,1:T(8,128)}) sort(f32[1024,1280]{0,1:T(8,128)} %copy.24, s32[1024,1280]{0,1:T(8,128)} %iota.15.clone), dimensions={1}, to_apply=%region_2.3 | sort | flops 27525120 | bytes 20971520 | tf_op jit(solution)/shard_map/jit(sort)/sort | solution.py:43
  489.5 6.0 %copy.26 = f32[1024,1280]{1,0:T(8,128)} copy(f32[1024,1280]{0,1:T(8,128)} %get-tuple-element.11) | data formatting | bytes 10485760 | tf_op jit(solution)/shard_map/jit(sort)/sort | solution.py:43
  495.4 1.1 slice.32
  496.5 0.8 copy.23
  497.3 0.1 convert_element_type.23
  497.4 0.0 all-to-all-done.2
  497.4 0.1 reduce
  497.5 0.1 convert_element_type.22
  497.6 0.6 select_reduce_fusion
  498.2 0.6 broadcast_minimum_fusion
  (10 shorter events, 0.1 us)
Async XLA Ops:
  2.1 19.1 %copy-start.2 = (s32[48,16]{0,1:T(8,128)S(1)}, s32[48,16]{0,1:T(8,128)}, u32[]{:S(2)}) copy-start(s32[48,16]{0,1:T(8,128)} %param.6) | copy-start | bytes 9220
  2.1 19.3 %copy-start = (bf16[1024,768]{1,0:T(8,128)(2,1)S(1)}, bf16[1024,768]{1,0:T(8,128)(2,1)}, u32[]{:S(2)}) copy-start(bf16[1024,768]{1,0:T(8,128)(2,1)} %param.5) | copy-start | bytes 4718596
  7.3 36.6 %all-to-all-start.1 = ((bf16[16,32,768]{2,1,0:T(8,128)(2,1)}), bf16[16,32,768]{2,1,0:T(8,128)(2,1)S(1)}, u32[]{:S(2)}, u32[]{:S(2)}) async-start(bf16[16,32,768]{2,1,0:T(8,128)(2,1)} %broadcast_select_fusion.1), calls=%async_computation.1 | async-start | bytes 1572864 | tf_op jit(solution)/shard_map/all_to_all | solution.py:30
  24.2 32.4 %copy-start.4 = (s32[48,1]{0,1:T(1,128)S(1)}, s32[48,1]{0,1:T(1,128)}, u32[]{:S(2)}) copy-start(s32[48,1]{0,1:T(1,128)} %param.8) | copy-start | bytes 580
  44.0 56.6 %all-to-all-start = ((bf16[48,16,768]{2,1,0:T(8,128)(2,1)}), bf16[48,16,768]{2,1,0:T(8,128)(2,1)S(1)}, u32[]{:S(2)}, u32[]{:S(2)}) async-start(bf16[48,16,768]{2,1,0:T(8,128)(2,1)} %broadcast_select_fusion), calls=%async_computation | async-start | bytes 2359296 | tf_op jit(solution)/shard_map/all_to_all | solution.py:29
  101.0 5.4 %copy-start.3 = (pred[1280]{0:T(1024)(128)(4,1)S(1)}, pred[1280]{0:T(1024)(128)(4,1)}, u32[]{:S(2)}) copy-start(pred[1280]{0:T(1024)(128)(4,1)} %dynamic-update-slice.1) | copy-start | bytes 3844
  106.4 6.4 %copy-start.1 = (s32[16,32]{1,0:T(8,128)S(1)}, s32[16,32]{1,0:T(8,128)}, u32[]{:S(2)}) copy-start(s32[16,32]{1,0:T(8,128)} %param.7) | copy-start | bytes 6148
  108.0 11.6 %all-to-all-start.3 = ((bf16[16,1,32]{2,1,0:T(2,128)(2,1)}), bf16[16,1,32]{2,1,0:T(2,128)(2,1)S(1)}, u32[]{:S(2)}, u32[]{:S(2)}) async-start(bf16[16,1,32]{2,1,0:T(2,128)(2,1)} %all_to_all.25), calls=%async_computation.3 | async-start | bytes 16384 | tf_op jit(solution)/shard_map/all_to_all | solution.py:51
  119.6 377.8 %all-to-all-start.2 = ((bf16[48,1,16]{2,1,0:T(2,128)(2,1)}), bf16[48,1,16]{2,1,0:T(2,128)(2,1)S(1)}, u32[]{:S(2)}, u32[]{:S(2)}) async-start(bf16[48,1,16]{2,1,0:T(2,128)(2,1)} %all_to_all.24), calls=%async_computation.2 | async-start | bytes 49152 | tf_op jit(solution)/shard_map/all_to_all | solution.py:48
where the time goes:
time: 501 us; the launch traced here: 499 us
  other arithmetic  363 us (72%)
  waiting for transfers between devices  61.1 us (12%)
  starting transfers between devices  38.7 us (8%)
  local copies, waits for them, and re-layouts  30.3 us (6%)
  matrix products  5.38 us (1%)
    sort x1, other arithmetic, body(): nearest = jnp.sort(masked.T, axis=1)[:, :NEAR]  354 us
    all_to_all x1, waiting for transfers between devices, body(): lax.all_to_all(offered_new, 'shard', split_axis=0, concat_axis=0, tiled=T...  37.9 us
    all_to_all x1, waiting for transfers between devices, body(): lax.all_to_all(offered_old, 'grp', split_axis=0, concat_axis=0, tiled=True)  17.1 us
    all_to_all x1, starting transfers between devices, body(): lax.all_to_all(offered_old, 'grp', split_axis=0, concat_axis=0, tiled=True)  13.9 us
    all_to_all x1, starting transfers between devices, body(): lax.all_to_all(offered_new, 'shard', split_axis=0, concat_axis=0, tiled=T...  12.7 us
  transfers between devices with their start and end apart: 4, of which 3 were waited for; matrix products, arithmetic and copies ran while one was open for 77% of the time, Pallas kernels for 0%

commit v1 on v0

v1 whole, which is shorter than its diff:
```python
import functools

import jax
import jax.numpy as jnp
from jax import lax
from jax.experimental import pallas as pl
from jax.experimental.pallas import tpu as pltpu
from jax.sharding import PartitionSpec as P

NEAR = 16
LANES = 128
SUBLANES = 8

cap_value = 8.0
far_value = 1000000000.0

VMEM_LIMIT = 48 * 1024 * 1024

SORT16 = (
    (0, 13), (1, 12), (2, 15), (3, 14), (4, 8), (5, 6), (7, 11), (9, 10),
    (0, 5), (1, 7), (2, 9), (3, 4), (6, 13), (8, 14), (10, 15), (11, 12),
    (0, 1), (2, 3), (4, 5), (6, 8), (7, 9), (10, 11), (12, 13), (14, 15),
    (0, 2), (1, 3), (4, 10), (5, 11), (6, 7), (8, 9), (12, 14), (13, 15),
    (1, 2), (3, 12), (4, 6), (5, 7), (8, 10), (9, 11), (13, 14),
    (1, 4), (2, 6), (5, 8), (7, 10), (9, 13), (11, 14),
    (2, 4), (3, 6), (9, 12), (11, 13),
    (3, 5), (6, 8), (7, 9), (10, 12),
    (3, 4), (5, 6), (7, 8), (9, 10), (11, 12),
    (6, 7), (8, 9),
)


def iota(shape, dim):
    return lax.broadcasted_iota(jnp.int32, shape, dim)


def onehot(condition, dtype=jnp.bfloat16):
    return jnp.where(condition, 1.0, 0.0).astype(dtype)


def dot(a, b):
    return lax.dot_general(a, b, (((1,), (0,)), ((), ())), preferred_element_type=jnp.float32)


def flat_parts(start, count, peers, slots, flipped):
    shape = lambda n: (count, n)
    peer = lambda n: iota(shape(n), 1) == (iota(shape(n), 0) + start) // slots
    slot = lambda n: iota(shape(n), 1) == (iota(shape(n), 0) + start) % slots
    return (slot(slots), peer(peers)) if flipped else (peer(peers), slot(slots))


def column(rows_of, lane_of, values):
    picked = dot(onehot(rows_of), values)
    return jnp.sum(jnp.where(lane_of, picked, 0.0), axis=1, keepdims=True)


def index_column(lists, start, count, peers, slots, flipped):
    rows_of, lane_of = flat_parts(start, count, peers, slots, flipped)
    high = column(rows_of, lane_of, (lists // 32).astype(jnp.bfloat16))
    low = column(rows_of, lane_of, (lists % 32).astype(jnp.bfloat16))
    return high.astype(jnp.int32) * 32 + low.astype(jnp.int32)


def gather_kernel(peers, slots, flipped, chunk, points_ref, lists_ref, out_ref):
    rows = points_ref.shape[0]
    for start in range(0, peers * slots, chunk):
        index = index_column(lists_ref[...], start, chunk, peers, slots, flipped)
        picks = onehot(index == iota((chunk, rows), 1))
        out_ref[start : start + chunk, :] = dot(picks, points_ref[...]).astype(jnp.bfloat16)


def gather(points, lists, peers, slots, flipped):
    total = peers * slots
    rows, features = points.shape
    return pl.pallas_call(
        functools.partial(gather_kernel, peers, slots, flipped, 256),
        out_shape=jax.ShapeDtypeStruct((total, features), jnp.bfloat16),
        compiler_params=pltpu.CompilerParams(vmem_limit_bytes=VMEM_LIMIT),
        cost_estimate=pl.CostEstimate(
            flops=2 * total * rows * features, bytes_accessed=2 * (total + rows) * features, transcendentals=0
        ),
    )(points, lists)


def exchange(values, low, high):
    a, b = values[low], values[high]
    values[low], values[high] = jnp.minimum(a, b), jnp.maximum(a, b)


def sort16(values):
    values = list(values)
    for low, high in SORT16:
        exchange(values, low, high)
    return values


def merge16(first, second):
    values = [jnp.minimum(first[k], second[15 - k]) for k in range(16)]
    for gap in (8, 4, 2, 1):
        for k in range(16):
            if not k & gap:
                exchange(values, k, k + gap)
    return values


def block16(ref, start, lanes):
    return [ref[pl.ds(start + SUBLANES * k, SUBLANES), lanes] for k in range(16)]


def smallest16(ref, lanes, held):
    step = 16 * SUBLANES
    first = 0
    if held is None:
        held, first = sort16(block16(ref, 0, lanes)), 1

    def body(t, held):
        start = pl.multiple_of(t * step, step)
        return tuple(merge16(held, sort16(block16(ref, start, lanes))))

    return list(lax.fori_loop(first, ref.shape[0] // step, body, tuple(held)))


def distances_into(dist_ref, minima_ref, cand_ref, points_ref, own_sq_ref, counts_ref, peers, slots, chunk):
    total = peers * slots
    back = jnp.zeros((peers, slots), jnp.float32)
    for start in range(0, total, chunk):
        cand = cand_ref[start : start + chunk, :]
        wide = cand.astype(jnp.float32)
        cand_sq = jnp.sum(wide * wide, axis=1, keepdims=True)
        inner = lax.dot_general(
            cand, points_ref[...], (((1,), (1,)), ((), ())), preferred_element_type=jnp.float32
        )
        dist = cand_sq + own_sq_ref[...] - 2.0 * inner
        peer = iota((chunk, peers), 1) == (iota((chunk, peers), 0) + start) // slots
        count = jnp.sum(jnp.where(peer, counts_ref[...], 0), axis=1, keepdims=True)
        usable = (iota((chunk, 1), 0) + start) % slots < count
        minima = jnp.where(usable, jnp.min(dist, axis=1, keepdims=True), cap_value)
        dist_ref[start : start + chunk, :] = jnp.where(usable, dist, far_value)
        slot = iota((chunk, slots), 1) == (iota((chunk, slots), 0) + start) % slots
        spread = jnp.where(slot, minima, 0.0).astype(jnp.bfloat16)
        owner = iota((peers, chunk), 0) == (iota((peers, chunk), 1) + start) // slots
        back = back + dot(onehot(owner), spread)
    minima_ref[...] = back.astype(jnp.bfloat16)


def near_kernel(peers, slots, chunk, cand_ref, points_ref, own_sq_ref, counts_ref, held_ref, minima_ref, dist_ref):
    distances_into(dist_ref, minima_ref, cand_ref, points_ref, own_sq_ref, counts_ref, peers, slots, chunk)

    def block(t, _):
        lanes = pl.ds(pl.multiple_of(t * LANES, LANES), LANES)
        for k, value in enumerate(smallest16(dist_ref, lanes, None)):
            held_ref[SUBLANES * k : SUBLANES * (k + 1), lanes] = value
        return 0

    lax.fori_loop(0, dist_ref.shape[1] // LANES, block, 0)


def dist_kernel(peers, slots, chunk, cand_ref, points_ref, own_sq_ref, counts_ref, dist_ref, minima_ref):
    distances_into(dist_ref, minima_ref, cand_ref, points_ref, own_sq_ref, counts_ref, peers, slots, chunk)


def select_kernel(dist_ref, held_ref, out_ref):
    held = smallest16(dist_ref, slice(None), block16(held_ref, 0, slice(None)))
    for shift in (4, 2, 1):
        held = merge16(held, [pltpu.roll(value, shift, 0) for value in held])
    sublane = iota((SUBLANES, LANES), 0)
    for half in range(2):
        rows = held[SUBLANES * half]
        for k in range(1, SUBLANES):
            rows = jnp.where(sublane == k, held[SUBLANES * half + k], rows)
        out_ref[SUBLANES * half : SUBLANES * (half + 1), :] = rows


def reverse_kernel(new_lists_ref, old_lists_ref, new_back_ref, old_back_ref, out_ref):
    slots_new, peers_new = new_lists_ref.shape
    peers_old, slots_old = old_lists_ref.shape
    rows = SUBLANES * LANES
    best = jnp.full((1, rows), cap_value, jnp.float32)
    for lists_ref, back_ref, peers, slots, flipped in (
        (new_lists_ref, new_back_ref, peers_new, slots_new, True),
        (old_lists_ref, old_back_ref, peers_old, slots_old, False),
    ):
        chunk = 256
        for start in range(0, peers * slots, chunk):
            index = index_column(lists_ref[...], start, chunk, peers, slots, flipped)
            back = column(*flat_parts(start, chunk, peers, slots, False), back_ref[...])
            matches = index == iota((chunk, rows), 1)
            best = jnp.minimum(best, jnp.min(jnp.where(matches, back, cap_value), axis=0, keepdims=True))
    for k in range(SUBLANES):
        out_ref[k : k + 1, :] = best[:, LANES * k : LANES * (k + 1)]


def body(points, serve_new, serve_old, count_new, count_old):
    rows, features = points.shape
    peers, slots = serve_new.shape
    groups, group_slots = serve_old.shape
    lists_new = serve_new.T
    counts_new, counts_old = count_new.T, count_old.T
    params = pltpu.CompilerParams(vmem_limit_bytes=VMEM_LIMIT)

    offered_old = gather(points, serve_old, groups, group_slots, False)
    offered_new = gather(points, lists_new, peers, slots, True)
    pulled_new = lax.all_to_all(
        offered_new.reshape(peers, slots, features), "shard", split_axis=0, concat_axis=0, tiled=True
    ).reshape(peers * slots, features)
    pulled_old = lax.all_to_all(
        offered_old.reshape(groups, group_slots, features), "grp", split_axis=0, concat_axis=0, tiled=True
    ).reshape(groups * group_slots, features)

    own_sq = jnp.sum(jnp.square(points.astype(jnp.float32)), axis=1)[None, :]

    total_old = groups * group_slots
    held, minima_old = pl.pallas_call(
        functools.partial(near_kernel, groups, group_slots, 256),
        out_shape=(
            jax.ShapeDtypeStruct((16 * SUBLANES, rows), jnp.float32),
            jax.ShapeDtypeStruct((groups, group_slots), jnp.bfloat16),
        ),
        scratch_shapes=[pltpu.VMEM((total_old, rows), jnp.float32)],
        compiler_params=params,
        cost_estimate=pl.CostEstimate(
            flops=8 * total_old * rows * features, bytes_accessed=2 * (total_old + rows) * features, transcendentals=0
        ),
    )(pulled_old, points, own_sq, counts_old)
    back_old = lax.all_to_all(minima_old, "grp", split_axis=0, concat_axis=0, tiled=True)

    total_new = peers * slots
    dist, minima_new = pl.pallas_call(
        functools.partial(dist_kernel, peers, slots, 256),
        out_shape=(
            jax.ShapeDtypeStruct((total_new, rows), jnp.float32),
            jax.ShapeDtypeStruct((peers, slots), jnp.bfloat16),
        ),
        compiler_params=params,
        cost_estimate=pl.CostEstimate(
            flops=2 * total_new * rows * features, bytes_accessed=4 * total_new * rows, transcendentals=0
        ),
    )(pulled_new, points, own_sq, counts_new)
    back_new = lax.all_to_all(minima_new, "shard", split_axis=0, concat_axis=0, tiled=True)

    nearest = pl.pallas_call(
        select_kernel,
        grid=(rows // LANES,),
        in_specs=[
            pl.BlockSpec((total_new, LANES), lambda t: (0, t)),
            pl.BlockSpec((16 * SUBLANES, LANES), lambda t: (0, t)),
        ],
        out_specs=pl.BlockSpec((NEAR, LANES), lambda t: (0, t)),
        out_shape=jax.ShapeDtypeStruct((NEAR, rows), jnp.float32),
        compiler_params=params,
        cost_estimate=pl.CostEstimate(
            flops=8 * total_new * rows * features, bytes_accessed=4 * total_new * rows, transcendentals=0
        ),
    )(dist, held)

    reverse = pl.pallas_call(
        reverse_kernel,
        out_shape=jax.ShapeDtypeStruct((SUBLANES, LANES), jnp.float32),
        compiler_params=params,
    )(lists_new, serve_old, back_new, back_old)
    return nearest.T, reverse.reshape(rows)


def solution(mesh):
    placed = (P(("grp", "shard"), None),) * 5
    return jax.shard_map(
        body,
        mesh=mesh,
        in_specs=placed,
        out_specs=(P(("grp", "shard"), None), P(("grp", "shard"))),
        check_vma=False,
    )
```

time: 501 us -> 139 us (0.28)
  other arithmetic: 363 us -> 0.38 us
  local copies, waits for them, and re-layouts: 30.3 us -> 7.92 us
  Pallas kernels: 0 us -> 15.4 us
  waiting for transfers between devices: 61.1 us -> 72.6 us
  matrix products: 5.38 us -> 0 us
    sort x1 -> x0, other arithmetic: 354 us -> none  [body(): nearest = jnp.sort(masked.T, axis=1)[:, :NEAR]]
    pallas_call x0 -> x6, Pallas kernels: none -> 15.4 us  [the longest x2 4.53 us: gather(): pl.pallas_call(functools.partial(gather_kernel, peers, slots, flipped, 25...]
    all_to_all x4, waiting for transfers between devices: 61.1 us -> 72.6 us  [the longest x1 41.5 us: body(): lax.all_to_all(offered_new.reshape(peers, slots, features), 'shard', spli...]
    gather x2 -> x0, local copies, waits for them, and re-layouts: 6.89 us -> none  [the longest x1 4.12 us: body(): offered_old = jnp.take(points, serve_old, axis=0)]
    sort x1 -> x0, local copies, waits for them, and re-layouts: 5.96 us -> none  [body(): nearest = jnp.sort(masked.T, axis=1)[:, :NEAR]]
    dot_general x1 -> x0, matrix products: 5.38 us -> none  [distance_block(): lax.dot_general(candidates, points, (((1,), (1,)), ((), ())), preferred_e...]
  transfers between devices with their start and end apart: 4 -> 4, of which waited for: 3 -> 4; matrix products, arithmetic and copies ran while one was open for 77% -> 0% of each run, Pallas kernels for 0% -> 4%
where the time goes in v1:
time: 139 us; the launch traced here: 138 us
  waiting for transfers between devices  72.6 us (52%)
  starting transfers between devices  41.1 us (30%)
  Pallas kernels  15.4 us (11%)
  local copies, waits for them, and re-layouts  7.92 us (6%)
    all_to_all x1, waiting for transfers between devices, body(): lax.all_to_all(offered_new.reshape(peers, slots, features), 'shard', spli...  41.5 us
    all_to_all x1, waiting for transfers between devices, body(): lax.all_to_all(offered_old.reshape(groups, group_slots, features), 'grp',...  22.3 us
    all_to_all x1, starting transfers between devices, body(): lax.all_to_all(offered_old.reshape(groups, group_slots, features), 'grp',...  14 us
    all_to_all x1, starting transfers between devices, body(): lax.all_to_all(offered_new.reshape(peers, slots, features), 'shard', spli...  12.7 us
    all_to_all x1, starting transfers between devices, body(): lax.all_to_all(minima_new, 'shard', split_axis=0, concat_axis=0, tiled=True)  11 us
    unnamed x21, local copies, waits for them, and re-layouts  6.7 us
    all_to_all x1, waiting for transfers between devices, body(): lax.all_to_all(minima_new, 'shard', split_axis=0, concat_axis=0, tiled=True)  5.27 us
    pallas_call x2, Pallas kernels, gather(): pl.pallas_call(functools.partial(gather_kernel, peers, slots, flipped, 25...  4.53 us
  transfers between devices with their start and end apart: 4, of which 4 were waited for; matrix products, arithmetic and copies ran while one was open for 0% of the time, Pallas kernels for 4%

profile of v1, /device:TPU:1, one launch (start us, length us, event | category | flops | bytes accessed | tf_op | source)
XLA Modules:
  0.0 138.1 jit_solution(7551344247847645798)
XLA Ops:
  0.6 0.0 copy-start
  0.6 1.4 %copy-done = bf16[1024,768]{1,0:T(8,128)(2,1)S(1)} copy-done((bf16[1024,768]{1,0:T(8,128)(2,1)S(1)}, bf16[1024,768]{1,0:T(8,128)(2,1)}, u32[]{:S(2)}) %copy-start) | copy-done | bytes 1572888
  2.0 0.0 copy-start.4
  2.0 0.7 copy-done.4
  2.7 0.0 copy-start.1
  2.7 2.4 %shard_map.70 = bf16[512,768]{1,0:T(8,128)(2,1)} custom-call(bf16[1024,768]{1,0:T(8,128)(2,1)S(1)} %copy-done, s32[16,32]{1,0:T(8,128)S(1)} %copy-done.4), custom_call_target="tpu_custom_call" | custom-call | flops 805306368 | bytes 2359296 | tf_op jit(solution)/shard_map/pallas_call | solution.py:75
  5.1 0.0 copy-start.6
  5.1 14.0 %all-to-all-start.1 = ((bf16[16,32,768]{2,1,0:T(8,128)(2,1)}), bf16[16,32,768]{2,1,0:T(8,128)(2,1)S(1)}, u32[]{:S(2)}, u32[]{:S(2)}) async-start(bf16[16,32,768]{2,1,0:T(8,128)(2,1)} %bitcast.5), calls=%async_computation.1 | async-start | bytes 1572864 | tf_op jit(solution)/shard_map/all_to_all | solution.py:206
  19.1 0.0 copy-done.1
  19.2 0.4 multiply_reduce_fusion
  19.5 22.3 %all-to-all-done.1 = bf16[16,32,768]{2,1,0:T(8,128)(2,1)S(1)} async-done(((bf16[16,32,768]{2,1,0:T(8,128)(2,1)}), bf16[16,32,768]{2,1,0:T(8,128)(2,1)S(1)}, u32[]{:S(2)}, u32[]{:S(2)}) %all-to-all-start.1) | async-done | bytes 786464 | tf_op jit(solution)/shard_map/all_to_all | solution.py:206
  41.9 0.0 copy-done.6
  41.9 0.0 copy-start.3
  41.9 2.9 %shard_map.71 = (f32[128,1024]{1,0:T(8,128)S(1)}, bf16[16,32]{1,0:T(8,128)(2,1)S(1)}) custom-call(bf16[512,768]{1,0:T(8,128)(2,1)S(1)} %bitcast.21, bf16[1024,768]{1,0:T(8,128)(2,1)S(1)} %copy-done.1, f32[1,1024]{1,0:T(1,128)S(1)} %bitcast.27, s32[1,16]{1,0:T(1,128)S(1)} %bitcast.30), custom_call_target="tpu_custom_call" | custom-call | flops 3221225472 | bytes 2359296 | tf_op jit(solution)/shard_map/pallas_call | solution.py:213
  44.7 0.6 copy.11
  45.4 3.4 %all-to-all-start.3 = ((bf16[16,1,32]{2,1,0:T(2,128)(2,1)}), bf16[16,1,32]{2,1,0:T(2,128)(2,1)S(1)}, u32[]{:S(2)}, u32[]{:S(2)}) async-start(bf16[16,1,32]{2,1,0:T(2,128)(2,1)} %copy.11), calls=%async_computation.3 | async-start | bytes 16384 | tf_op jit(solution)/shard_map/all_to_all | solution.py:225
  48.7 0.0 copy-done.3
  48.7 2.2 %shard_map.68 = bf16[768,768]{1,0:T(8,128)(2,1)S(1)} custom-call(bf16[1024,768]{1,0:T(8,128)(2,1)S(1)} %copy-done.1, s32[16,48]{1,0:T(8,128)S(1)} %bitcast.25), custom_call_target="tpu_custom_call" | custom-call | flops 1207959552 | bytes 2752512 | tf_op jit(solution)/shard_map/pallas_call | solution.py:75
  50.9 0.0 copy-start.2
  50.9 1.0 copy-done.2
  52.0 0.0 copy-start.7
  52.0 3.5 %all-to-all-done.3 = bf16[16,1,32]{2,1,0:T(2,128)(2,1)S(1)} async-done(((bf16[16,1,32]{2,1,0:T(2,128)(2,1)}), bf16[16,1,32]{2,1,0:T(2,128)(2,1)S(1)}, u32[]{:S(2)}, u32[]{:S(2)}) %all-to-all-start.3) | async-done | bytes 1056 | tf_op jit(solution)/shard_map/all_to_all | solution.py:225
  55.5 12.7 %all-to-all-start = ((bf16[48,16,768]{2,1,0:T(8,128)(2,1)}), bf16[48,16,768]{2,1,0:T(8,128)(2,1)S(1)}, u32[]{:S(2)}, u32[]{:S(2)}) async-start(bf16[48,16,768]{2,1,0:T(8,128)(2,1)} %bitcast.20), calls=%async_computation | async-start | bytes 2359296 | tf_op jit(solution)/shard_map/all_to_all | solution.py:203
  68.2 41.5 %all-to-all-done = bf16[48,16,768]{2,1,0:T(8,128)(2,1)S(1)} async-done(((bf16[48,16,768]{2,1,0:T(8,128)(2,1)}), bf16[48,16,768]{2,1,0:T(8,128)(2,1)S(1)}, u32[]{:S(2)}, u32[]{:S(2)}) %all-to-all-start) | async-done | bytes 1179680 | tf_op jit(solution)/shard_map/all_to_all | solution.py:203
  109.6 0.0 copy-done.7
  109.6 2.1 %shard_map.69 = (f32[768,1024]{1,0:T(8,128)S(1)}, bf16[48,16]{1,0:T(8,128)(2,1)S(1)}) custom-call(bf16[768,768]{1,0:T(8,128)(2,1)S(1)} %bitcast.19, bf16[1024,768]{1,0:T(8,128)(2,1)S(1)} %copy-done.1, f32[1,1024]{1,0:T(1,128)S(1)} %bitcast.28, s32[1,48]{1,0:T(1,128)S(1)} %bitcast.31), custom_call_target="tpu_custom_call" | custom-call | flops 1207959552 | bytes 3145728 | tf_op jit(solution)/shard_map/pallas_call | solution.py:228
  111.8 0.0 copy-start.8
  111.8 1.7 %copy-done.8 = f32[768,1024]{1,0:T(8,128)} copy-done((f32[768,1024]{1,0:T(8,128)}, f32[768,1024]{1,0:T(8,128)S(1)}, u32[]{:S(2)}) %copy-start.8) | copy-done | bytes 3145752
  113.4 0.6 copy.9
  114.1 11.0 %all-to-all-start.2 = ((bf16[48,1,16]{2,1,0:T(2,128)(2,1)}), bf16[48,1,16]{2,1,0:T(2,128)(2,1)S(1)}, u32[]{:S(2)}, u32[]{:S(2)}) async-start(bf16[48,1,16]{2,1,0:T(2,128)(2,1)} %copy.9), calls=%async_computation.2 | async-start | bytes 49152 | tf_op jit(solution)/shard_map/all_to_all | solution.py:239
  125.1 0.0 copy-start.9
  125.1 1.9 %copy-done.9 = f32[768,1024]{1,0:T(8,128)S(1)} copy-done((f32[768,1024]{1,0:T(8,128)S(1)}, f32[768,1024]{1,0:T(8,128)}, u32[]{:S(2)}) %copy-start.9) | copy-done | bytes 3145752
  127.0 0.0 copy-start.5
  127.0 3.9 %shard_map.72 = f32[16,1024]{1,0:T(8,128)} custom-call(f32[768,1024]{1,0:T(8,128)S(1)} %copy-done.9, f32[128,1024]{1,0:T(8,128)S(1)} %get-tuple-element.7.held_ref), custom_call_target="tpu_custom_call" | custom-call | flops 4831838208 | bytes 3145728 | tf_op jit(solution)/shard_map/pallas_call | solution.py:241
  130.9 5.3 %all-to-all-done.2 = bf16[48,1,16]{2,1,0:T(2,128)(2,1)S(1)} async-done(((bf16[48,1,16]{2,1,0:T(2,128)(2,1)}), bf16[48,1,16]{2,1,0:T(2,128)(2,1)S(1)}, u32[]{:S(2)}, u32[]{:S(2)}) %all-to-all-start.2) | async-done | bytes 1568 | tf_op jit(solution)/shard_map/all_to_all | solution.py:239
  136.2 0.0 copy-done.5
  136.2 1.9 %shard_map.73 = f32[8,128]{1,0:T(8,128)} custom-call(s32[16,48]{1,0:T(8,128)S(1)} %bitcast.26, s32[16,32]{1,0:T(8,128)S(1)} %copy-done.5, bf16[48,16]{1,0:T(8,128)(2,1)S(1)} %bitcast.22, bf16[16,32]{1,0:T(8,128)(2,1)S(1)} %bitcast.23), custom_call_target="tpu_custom_call" | custom-call | tf_op jit(solution)/shard_map/pallas_call | solution.py:256
  (2 shorter events, 0.0 us)
Async XLA Ops:
  0.6 1.4 %copy-start = (bf16[1024,768]{1,0:T(8,128)(2,1)S(1)}, bf16[1024,768]{1,0:T(8,128)(2,1)}, u32[]{:S(2)}) copy-start(bf16[1024,768]{1,0:T(8,128)(2,1)} %points_ref.7) | copy-start | bytes 4718596
  2.0 0.7 copy-start.4
  2.7 16.4 %copy-start.1 = (bf16[1024,768]{1,0:T(8,128)(2,1)S(1)}, bf16[1024,768]{1,0:T(8,128)(2,1)}, u32[]{:S(2)}) copy-start(bf16[1024,768]{1,0:T(8,128)(2,1)} %points_ref.7) | copy-start | bytes 4718596
  5.1 36.8 %copy-start.6 = (s32[16,1]{0,1:T(1,128)S(1)}, s32[16,1]{0,1:T(1,128)}, u32[]{:S(2)}) copy-start(s32[16,1]{0,1:T(1,128)} %param.9) | copy-start | bytes 196
  5.1 36.8 %all-to-all-start.1 = ((bf16[16,32,768]{2,1,0:T(8,128)(2,1)}), bf16[16,32,768]{2,1,0:T(8,128)(2,1)S(1)}, u32[]{:S(2)}, u32[]{:S(2)}) async-start(bf16[16,32,768]{2,1,0:T(8,128)(2,1)} %bitcast.5), calls=%async_computation.1 | async-start | bytes 1572864 | tf_op jit(solution)/shard_map/all_to_all | solution.py:206
  41.9 6.9 %copy-start.3 = (s32[48,16]{0,1:T(8,128)S(1)}, s32[48,16]{0,1:T(8,128)}, u32[]{:S(2)}) copy-start(s32[48,16]{0,1:T(8,128)} %param.6) | copy-start | bytes 9220
  45.4 10.1 %all-to-all-start.3 = ((bf16[16,1,32]{2,1,0:T(2,128)(2,1)}), bf16[16,1,32]{2,1,0:T(2,128)(2,1)S(1)}, u32[]{:S(2)}, u32[]{:S(2)}) async-start(bf16[16,1,32]{2,1,0:T(2,128)(2,1)} %copy.11), calls=%async_computation.3 | async-start | bytes 16384 | tf_op jit(solution)/shard_map/all_to_all | solution.py:225
  50.9 1.0 copy-start.2
  52.0 57.7 %copy-start.7 = (s32[48,1]{0,1:T(1,128)S(1)}, s32[48,1]{0,1:T(1,128)}, u32[]{:S(2)}) copy-start(s32[48,1]{0,1:T(1,128)} %param.8) | copy-start | bytes 580
  55.5 54.2 %all-to-all-start = ((bf16[48,16,768]{2,1,0:T(8,128)(2,1)}), bf16[48,16,768]{2,1,0:T(8,128)(2,1)S(1)}, u32[]{:S(2)}, u32[]{:S(2)}) async-start(bf16[48,16,768]{2,1,0:T(8,128)(2,1)} %bitcast.20), calls=%async_computation | async-start | bytes 2359296 | tf_op jit(solution)/shard_map/all_to_all | solution.py:203
  111.8 1.7 %copy-start.8 = (f32[768,1024]{1,0:T(8,128)}, f32[768,1024]{1,0:T(8,128)S(1)}, u32[]{:S(2)}) copy-start(f32[768,1024]{1,0:T(8,128)S(1)} %get-tuple-element.6.dist_ref) | copy-start | bytes 9437188
  114.1 22.2 %all-to-all-start.2 = ((bf16[48,1,16]{2,1,0:T(2,128)(2,1)}), bf16[48,1,16]{2,1,0:T(2,128)(2,1)S(1)}, u32[]{:S(2)}, u32[]{:S(2)}) async-start(bf16[48,1,16]{2,1,0:T(2,128)(2,1)} %copy.9), calls=%async_computation.2 | async-start | bytes 49152 | tf_op jit(solution)/shard_map/all_to_all | solution.py:239
  125.1 1.9 %copy-start.9 = (f32[768,1024]{1,0:T(8,128)S(1)}, f32[768,1024]{1,0:T(8,128)}, u32[]{:S(2)}) copy-start(f32[768,1024]{1,0:T(8,128)} %copy-done.8) | copy-start | bytes 9437188
  127.0 9.2 %copy-start.5 = (s32[16,32]{1,0:T(8,128)S(1)}, s32[16,32]{1,0:T(8,128)}, u32[]{:S(2)}) copy-start(s32[16,32]{1,0:T(8,128)} %old_lists_ref.1) | copy-start | bytes 6148

commit v2 on v1

v2 whole, which is shorter than its diff:
```python
import functools

import jax
import jax.numpy as jnp
from jax import lax
from jax.experimental import pallas as pl
from jax.experimental.pallas import tpu as pltpu
from jax.sharding import PartitionSpec as P

NEAR = 16
LANES = 128
SUBLANES = 8

cap_value = 8.0
far_value = 1000000000.0

VMEM_LIMIT = 20 * 1024 * 1024

SORT16 = (
    (0, 13), (1, 12), (2, 15), (3, 14), (4, 8), (5, 6), (7, 11), (9, 10),
    (0, 5), (1, 7), (2, 9), (3, 4), (6, 13), (8, 14), (10, 15), (11, 12),
    (0, 1), (2, 3), (4, 5), (6, 8), (7, 9), (10, 11), (12, 13), (14, 15),
    (0, 2), (1, 3), (4, 10), (5, 11), (6, 7), (8, 9), (12, 14), (13, 15),
    (1, 2), (3, 12), (4, 6), (5, 7), (8, 10), (9, 11), (13, 14),
    (1, 4), (2, 6), (5, 8), (7, 10), (9, 13), (11, 14),
    (2, 4), (3, 6), (9, 12), (11, 13),
    (3, 5), (6, 8), (7, 9), (10, 12),
    (3, 4), (5, 6), (7, 8), (9, 10), (11, 12),
    (6, 7), (8, 9),
)


def iota(shape, dim):
    return lax.broadcasted_iota(jnp.int32, shape, dim)


def onehot(condition, dtype=jnp.bfloat16):
    return jnp.where(condition, 1.0, 0.0).astype(dtype)


def dot(a, b):
    return lax.dot_general(a, b, (((1,), (0,)), ((), ())), preferred_element_type=jnp.float32)


def flat_parts(start, count, peers, slots, order, flipped=False):
    def peer(n):
        return iota((count, n), 1) == order((iota((count, n), 0) + start) // slots)

    def slot(n):
        return iota((count, n), 1) == (iota((count, n), 0) + start) % slots

    return (slot(slots), peer(peers)) if flipped else (peer(peers), slot(slots))


def straight(block):
    return block


def column(rows_of, lane_of, values):
    picked = dot(onehot(rows_of), values)
    return jnp.sum(jnp.where(lane_of, picked, 0.0), axis=1, keepdims=True)


def index_column(lists, parts):
    high = column(*parts, (lists // 32).astype(jnp.bfloat16))
    low = column(*parts, (lists % 32).astype(jnp.bfloat16))
    return high.astype(jnp.int32) * 32 + low.astype(jnp.int32)


def gather_kernel(peers, slots, flipped, chunk, *refs):
    points_ref, lists_ref, place_ref = refs[:3]
    outs = refs[3:]
    rows = points_ref.shape[0]
    order = straight if flipped else lambda block: block ^ place_ref[0]
    size = outs[0].shape[0]
    for start in range(0, peers * slots, chunk):
        index = index_column(lists_ref[...], flat_parts(start, chunk, peers, slots, order, flipped))
        picked = dot(onehot(index == iota((chunk, rows), 1)), points_ref[...]).astype(jnp.bfloat16)
        for at in range(start, start + chunk, min(size, chunk)):
            piece = min(size, chunk)
            outs[at // size][at % size : at % size + piece, :] = picked[at - start : at - start + piece, :]


def gather(points, lists, place, peers, slots, flipped, pieces):
    total = peers * slots
    rows, features = points.shape
    vmem = pl.BlockSpec(memory_space=pltpu.VMEM)
    return pl.pallas_call(
        functools.partial(gather_kernel, peers, slots, flipped, 256),
        in_specs=[vmem, vmem, pl.BlockSpec(memory_space=pltpu.SMEM)],
        out_shape=(jax.ShapeDtypeStruct((total // pieces, features), jnp.bfloat16),) * pieces,
        compiler_params=pltpu.CompilerParams(vmem_limit_bytes=VMEM_LIMIT),
        cost_estimate=pl.CostEstimate(
            flops=2 * total * rows * features, bytes_accessed=2 * (total + rows) * features, transcendentals=0
        ),
    )(points, lists, place)


def exchange(values, low, high):
    a, b = values[low], values[high]
    values[low], values[high] = jnp.minimum(a, b), jnp.maximum(a, b)


def sort16(values):
    values = list(values)
    for low, high in SORT16:
        exchange(values, low, high)
    return values


def merge16(first, second):
    values = [jnp.minimum(first[k], second[15 - k]) for k in range(16)]
    for gap in (8, 4, 2, 1):
        for k in range(16):
            if not k & gap:
                exchange(values, k, k + gap)
    return values


def block16(ref, start, lanes):
    return [ref[pl.ds(start + SUBLANES * k, SUBLANES), lanes] for k in range(16)]


def smallest16(ref, lanes, held):
    step = 16 * SUBLANES
    first = 0
    if held is None:
        held, first = sort16(block16(ref, 0, lanes)), 1

    def body(t, held):
        start = pl.multiple_of(t * step, step)
        return tuple(merge16(held, sort16(block16(ref, start, lanes))))

    return list(lax.fori_loop(first, ref.shape[0] // step, body, tuple(held)))


def distances(cand, points_ref, own_sq_ref):
    wide = cand.astype(jnp.float32)
    cand_sq = jnp.sum(wide * wide, axis=1, keepdims=True)
    inner = lax.dot_general(
        cand, points_ref[...], (((1,), (1,)), ((), ())), preferred_element_type=jnp.float32
    )
    return cand_sq + own_sq_ref[...] - 2.0 * inner


def judge(dist, counts_ref, start, peers, slots, order):
    chunk = dist.shape[0]
    peer_of, slot_of = flat_parts(start, chunk, peers, slots, order)
    count = jnp.sum(jnp.where(peer_of, counts_ref[...], 0), axis=1, keepdims=True)
    usable = (iota((chunk, 1), 0) + start) % slots < count
    minima = jnp.where(usable, jnp.min(dist, axis=1, keepdims=True), cap_value)
    spread = jnp.where(slot_of, minima, 0.0).astype(jnp.bfloat16)
    owner = iota((peers, chunk), 0) == order((iota((peers, chunk), 1) + start) // slots)
    return jnp.where(usable, dist, far_value), dot(onehot(owner), spread)


def near_kernel(groups, slots, *refs):
    count = groups // 2
    evens, (odd_ref, points_ref, own_sq_ref, counts_ref, place_ref) = refs[:count], refs[count : count + 5]
    held_ref, minima_ref, dist_ref = refs[count + 5 :]

    def order(block):
        return jnp.where(block < count, 2 * block, 2 * (block - count) + 1) ^ place_ref[0]

    half = count * slots
    even = jnp.concatenate([ref[:slots, :] for ref in evens], axis=0)
    back = jnp.zeros((groups, slots), jnp.float32)
    for start, cand in ((0, even), (half, odd_ref[...])):
        dist, term = judge(distances(cand, points_ref, own_sq_ref), counts_ref, start, groups, slots, order)
        dist_ref[start : start + half, :] = dist
        back = back + term
    minima_ref[...] = back.astype(jnp.bfloat16)

    def block(t, _):
        lanes = pl.ds(pl.multiple_of(t * LANES, LANES), LANES)
        for k, value in enumerate(smallest16(dist_ref, lanes, None)):
            held_ref[SUBLANES * k : SUBLANES * (k + 1), lanes] = value
        return 0

    lax.fori_loop(0, dist_ref.shape[1] // LANES, block, 0)


def minima_kernel(peers, slots, chunk, cand_ref, points_ref, own_sq_ref, counts_ref, minima_ref):
    back = jnp.zeros((peers, slots), jnp.float32)
    for start in range(0, peers * slots, chunk):
        dist = distances(cand_ref[start : start + chunk, :], points_ref, own_sq_ref)
        back = back + judge(dist, counts_ref, start, peers, slots, straight)[1]
    minima_ref[...] = back.astype(jnp.bfloat16)


def select_kernel(peers, slots, chunk, cand_ref, points_ref, own_sq_ref, counts_ref, held_ref, out_ref, dist_ref):
    for start in range(0, peers * slots, chunk):
        dist = distances(cand_ref[start : start + chunk, :], points_ref, own_sq_ref)
        dist_ref[start : start + chunk, :] = judge(dist, counts_ref, start, peers, slots, straight)[0]
    sublane = iota((SUBLANES, LANES), 0)

    def block(t, _):
        lanes = pl.ds(pl.multiple_of(t * LANES, LANES), LANES)
        held = smallest16(dist_ref, lanes, block16(held_ref, 0, lanes))
        for shift in (4, 2, 1):
            held = merge16(held, [pltpu.roll(value, shift, 0) for value in held])
        for half in range(2):
            rows = held[SUBLANES * half]
            for k in range(1, SUBLANES):
                rows = jnp.where(sublane == k, held[SUBLANES * half + k], rows)
            out_ref[SUBLANES * half : SUBLANES * (half + 1), lanes] = rows
        return 0

    lax.fori_loop(0, dist_ref.shape[1] // LANES, block, 0)


def reverse_kernel(gathered, new_lists_ref, old_lists_ref, new_back_ref, old_back_ref, place_ref, out_ref):
    slots_new, peers_new = new_lists_ref.shape
    groups, slots_old = old_lists_ref.shape
    rows = SUBLANES * LANES
    best = jnp.full((1, rows), cap_value, jnp.float32)
    chunk = 256

    def fold(best, index, back):
        matches = index == iota((chunk, rows), 1)
        return jnp.minimum(best, jnp.min(jnp.where(matches, back, cap_value), axis=0, keepdims=True))

    for start in range(0, groups * slots_old, chunk):
        index = index_column(old_lists_ref[...], flat_parts(start, chunk, groups, slots_old, straight))
        if gathered:
            mine = lambda block: block * groups + place_ref[0]
            parts = flat_parts(start, chunk, groups * groups, slots_old, mine)
        else:
            parts = flat_parts(start, chunk, groups, slots_old, straight)
        best = fold(best, index, column(*parts, old_back_ref[...]))
    for start in range(0, peers_new * slots_new, chunk):
        index = index_column(new_lists_ref[...], flat_parts(start, chunk, peers_new, slots_new, straight, True))
        parts = flat_parts(start, chunk, peers_new, slots_new, straight)
        best = fold(best, index, column(*parts, new_back_ref[...]))
    for k in range(SUBLANES):
        out_ref[k : k + 1, :] = best[:, LANES * k : LANES * (k + 1)]


GATHERED = False


def apart(groups, away):
    return [(g, g ^ away) for g in range(groups)]


def body(points, serve_new, serve_old, count_new, count_old):
    rows, features = points.shape
    peers, slots = serve_new.shape
    groups, group_slots = serve_old.shape
    lists_new = serve_new.T
    counts_new, counts_old = count_new.T, count_old.T
    params = pltpu.CompilerParams(vmem_limit_bytes=VMEM_LIMIT)
    vmem = pl.BlockSpec(memory_space=pltpu.VMEM)
    smem = pl.BlockSpec(memory_space=pltpu.SMEM)
    place = lax.axis_index("grp").astype(jnp.int32).reshape(1)

    (offered_new,) = gather(points, lists_new, place, peers, slots, True, 1)
    pulled_new = lax.all_to_all(
        offered_new.reshape(peers, slots, features), "shard", split_axis=0, concat_axis=0, tiled=True
    ).reshape(peers * slots, features)

    pieces = gather(points, serve_old, place, groups, group_slots, False, groups // 2)
    evens = [pieces[0]] + [
        lax.ppermute(pieces[k], "grp", apart(groups, 2 * k)) for k in range(1, groups // 2)
    ]
    odds = lax.ppermute(
        jnp.concatenate([piece[group_slots:] for piece in evens], axis=0), "grp", apart(groups, 1)
    )

    own_sq = jnp.sum(jnp.square(points.astype(jnp.float32)), axis=1)[None, :]

    total_old = groups * group_slots
    held, minima_old = pl.pallas_call(
        functools.partial(near_kernel, groups, group_slots),
        in_specs=[vmem] * (groups // 2 + 4) + [smem],
        out_shape=(
            jax.ShapeDtypeStruct((16 * SUBLANES, rows), jnp.float32),
            jax.ShapeDtypeStruct((groups, group_slots), jnp.bfloat16),
        ),
        scratch_shapes=[pltpu.VMEM((total_old, rows), jnp.float32)],
        compiler_params=params,
        cost_estimate=pl.CostEstimate(
            flops=2 * total_old * rows * features, bytes_accessed=2 * (total_old + rows) * features, transcendentals=0
        ),
    )(*evens, odds, points, own_sq, counts_old, place)
    pulled_new, minima_old = lax.optimization_barrier((pulled_new, minima_old))
    if GATHERED:
        back_old = lax.all_gather(minima_old, "grp", axis=0, tiled=True)
    else:
        back_old = lax.all_to_all(minima_old, "grp", split_axis=0, concat_axis=0, tiled=True)

    total_new = peers * slots
    minima_new = pl.pallas_call(
        functools.partial(minima_kernel, peers, slots, 256),
        out_shape=jax.ShapeDtypeStruct((peers, slots), jnp.bfloat16),
        compiler_params=params,
        cost_estimate=pl.CostEstimate(
            flops=2 * total_new * rows * features, bytes_accessed=4 * total_new * features, transcendentals=0
        ),
    )(pulled_new, points, own_sq, counts_new)
    back_new = lax.all_to_all(minima_new, "shard", split_axis=0, concat_axis=0, tiled=True)

    pulled_new, _ = lax.optimization_barrier((pulled_new, minima_new))
    nearest = pl.pallas_call(
        functools.partial(select_kernel, peers, slots, 256),
        out_shape=jax.ShapeDtypeStruct((NEAR, rows), jnp.float32),
        scratch_shapes=[pltpu.VMEM((total_new, rows), jnp.float32)],
        compiler_params=params,
        cost_estimate=pl.CostEstimate(
            flops=4 * total_new * rows * features, bytes_accessed=4 * total_new * features, transcendentals=0
        ),
    )(pulled_new, points, own_sq, counts_new, held)

    reverse = pl.pallas_call(
        functools.partial(reverse_kernel, GATHERED),
        in_specs=[vmem] * 4 + [smem],
        out_shape=jax.ShapeDtypeStruct((SUBLANES, LANES), jnp.float32),
        compiler_params=params,
    )(lists_new, serve_old, back_new, back_old, place)
    return nearest.T, reverse.reshape(rows)


def solution(mesh):
    placed = (P(("grp", "shard"), None),) * 5
    return jax.shard_map(
        body,
        mesh=mesh,
        in_specs=placed,
        out_specs=(P(("grp", "shard"), None), P(("grp", "shard"))),
        check_vma=False,
    )
```

time: 139 us -> 107 us (0.77)
  waiting for transfers between devices: 72.6 us -> 20.1 us
  starting transfers between devices: 41.1 us -> 65.1 us
  local copies, waits for them, and re-layouts: 7.92 us -> 4.45 us
    all_to_all x1, waiting for transfers between devices: 41.5 us -> 0.01 us  [body(): lax.all_to_all(offered_new.reshape(peers, slots, features), 'shard', spli...]
    ppermute x0 -> x8, starting transfers between devices: none -> 29.1 us  [the longest x7 25.5 us: body(): lax.ppermute(pieces[k], 'grp', apart(groups, 2 * k))]
    all_to_all x1 -> x0, waiting for transfers between devices: 22.3 us -> none  [body(): lax.all_to_all(offered_old.reshape(groups, group_slots, features), 'grp',...]
    all_to_all x1 -> x0, starting transfers between devices: 14 us -> none  [body(): lax.all_to_all(offered_old.reshape(groups, group_slots, features), 'grp',...]
    ppermute x0 -> x8, waiting for transfers between devices: none -> 9.88 us  [the longest x7 8.94 us: body(): lax.ppermute(pieces[k], 'grp', apart(groups, 2 * k))]
    all_to_all x1, starting transfers between devices: 12.7 us -> 19 us  [body(): lax.all_to_all(offered_new.reshape(peers, slots, features), 'shard', spli...]
    all_to_all x1, starting transfers between devices: 3.37 us -> 9.26 us  [body(): lax.all_to_all(minima_old, 'grp', split_axis=0, concat_axis=0, tiled=True)]
    unnamed x21 -> x24, local copies, waits for them, and re-layouts: 6.7 us -> 3.2 us
  transfers between devices with their start and end apart: 4 -> 11, of which waited for: 4 -> 5; matrix products, arithmetic and copies ran while one was open for 0% -> 1% of each run, Pallas kernels for 4% -> 11%
where the time goes in v2:
time: 107 us
  starting transfers between devices  65.1 us (61%)
  waiting for transfers between devices  20.1 us (19%)
  Pallas kernels  15.6 us (15%)
  local copies, waits for them, and re-layouts  4.45 us (4%)
    ppermute x7, starting transfers between devices, body(): lax.ppermute(pieces[k], 'grp', apart(groups, 2 * k))  25.5 us
    all_to_all x1, starting transfers between devices, body(): lax.all_to_all(offered_new.reshape(peers, slots, features), 'shard', spli...  19 us
    all_to_all x1, starting transfers between devices, body(): lax.all_to_all(minima_old, 'grp', split_axis=0, concat_axis=0, tiled=True)  9.26 us
    ppermute x7, waiting for transfers between devices, body(): lax.ppermute(pieces[k], 'grp', apart(groups, 2 * k))  8.94 us
    all_to_all x1, starting transfers between devices, body(): lax.all_to_all(minima_new, 'shard', split_axis=0, concat_axis=0, tiled=True)  7.77 us
    all_to_all x1, waiting for transfers between devices, body(): lax.all_to_all(minima_new, 'shard', split_axis=0, concat_axis=0, tiled=True)  5.88 us
    pallas_call x1, Pallas kernels, body(): pl.pallas_call(functools.partial(select_kernel, peers, slots, 256), out_s...  5.22 us
    all_to_all x1, waiting for transfers between devices, body(): lax.all_to_all(minima_old, 'grp', split_axis=0, concat_axis=0, tiled=True)  4.33 us
  transfers between devices with their start and end apart: 11, of which 5 were waited for; matrix products, arithmetic and copies ran while one was open for 1% of the time, Pallas kernels for 11%

profile of v2, /device:TPU:1, one launch (start us, length us, event | category | flops | bytes accessed | tf_op | source)
XLA Modules:
  0.0 106.5 jit_solution(3482243711943472104)
XLA Ops:
  0.6 0.0 copy-start
  0.6 1.4 %copy-done = bf16[1024,768]{1,0:T(8,128)(2,1)S(1)} copy-done((bf16[1024,768]{1,0:T(8,128)(2,1)S(1)}, bf16[1024,768]{1,0:T(8,128)(2,1)}, u32[]{:S(2)}) %copy-start) | copy-done | bytes 1572888
  2.0 0.0 copy-start.3
  2.0 0.7 copy-done.3
  2.7 2.2 %shard_map.68 = bf16[768,768]{1,0:T(8,128)(2,1)S(1)} custom-call(bf16[1024,768]{1,0:T(8,128)(2,1)S(1)} %copy-done, s32[16,48]{1,0:T(8,128)S(1)} %bitcast.24, s32[1]{0:T(128)} %bitcast.1.refs_2_.refs_12_.place_ref), custom_call_target="tpu_custom_call" | custom-call | flops 1207959552 | bytes 2752512 | tf_op jit(solution)/shard_map/pallas_call | solution.py:88
  4.9 0.0 copy-start.2
  4.9 1.0 copy-done.2
  6.0 0.0 copy-start.1
  6.0 0.0 copy-start.5
  6.0 19.0 %all-to-all-start = ((bf16[48,16,768]{2,1,0:T(8,128)(2,1)}), bf16[48,16,768]{2,1,0:T(8,128)(2,1)S(1)}, u32[]{:S(2)}, u32[]{:S(2)}) async-start(bf16[48,16,768]{2,1,0:T(8,128)(2,1)} %bitcast.20), calls=%async_computation | async-start | bytes 2359296 | tf_op jit(solution)/shard_map/all_to_all | solution.py:258
  25.0 0.0 copy-done.1
  25.0 0.0 copy-done.5
  25.0 1.5 %shard_map.69 = (bf16[64,768]{1,0:T(8,128)(2,1)S(1)}, bf16[64,768]{1,0:T(8,128)(2,1)S(1)}, bf16[64,768]{1,0:T(8,128)(2,1)S(1)}, bf16[64,768]{1,0:T(8,128)(2,1)S(...) custom-call(bf16[1024,768]{1,0:T(8,128)(2,1)S(1)} %copy-done.1, ...), custom_call_target="tpu_custom_call" | custom-call | flops 805306368 | bytes 2359296 | tf_op jit(solution)/shard_map/pallas_call | solution.py:88
  26.4 0.0 copy-start.6
  26.4 3.2 %collective-permute-start = (bf16[64,768]{1,0:T(8,128)(2,1)S(1)}, bf16[64,768]{1,0:T(8,128)(2,1)S(1)}, u32[]{:S(2)}, u32[]{:S(2)}) collective-permute-start(bf16[64,768]{1,0:T(8,128)(2,1)S(1)} %get-tuple-element.16), channel_id=1, source_target_pairs={{0,96},{48,144},{96,0},{144,48},{192,288},{240,336},{288,192},{336... | collective-permute-start | bytes 294920 | tf_op jit(solution)/shard_map/ppermute | solution.py:264
  29.7 4.2 %collective-permute-start.1 = (bf16[64,768]{1,0:T(8,128)(2,1)S(1)}, bf16[64,768]{1,0:T(8,128)(2,1)S(1)}, u32[]{:S(2)}, u32[]{:S(2)}) collective-permute-start(bf16[64,768]{1,0:T(8,128)(2,1)S(1)} %get-tuple-element.17), channel_id=1, source_target_pairs={{0,192},{48,240},{96,288},{144,336},{192,0},{240,48},{288,96},{336... | collective-permute-start | bytes 294920 | tf_op jit(solution)/shard_map/ppermute | solution.py:264
  33.9 1.9 %collective-permute-start.2 = (bf16[64,768]{1,0:T(8,128)(2,1)S(1)}, bf16[64,768]{1,0:T(8,128)(2,1)S(1)}, u32[]{:S(2)}, u32[]{:S(2)}) collective-permute-start(bf16[64,768]{1,0:T(8,128)(2,1)S(1)} %get-tuple-element.18), channel_id=1, source_target_pairs={{0,288},{48,336},{96,192},{144,240},{192,96},{240,144},{288,0},{33... | collective-permute-start | bytes 294920 | tf_op jit(solution)/shard_map/ppermute | solution.py:264
  35.8 7.4 %collective-permute-start.3 = (bf16[64,768]{1,0:T(8,128)(2,1)S(1)}, bf16[64,768]{1,0:T(8,128)(2,1)S(1)}, u32[]{:S(2)}, u32[]{:S(2)}) collective-permute-start(bf16[64,768]{1,0:T(8,128)(2,1)S(1)} %get-tuple-element.19), channel_id=1, source_target_pairs={{0,384},{48,432},{96,480},{144,528},{192,576},{240,624},{288,672},... | collective-permute-start | bytes 294920 | tf_op jit(solution)/shard_map/ppermute | solution.py:264
  43.2 1.9 %collective-permute-start.4 = (bf16[64,768]{1,0:T(8,128)(2,1)S(1)}, bf16[64,768]{1,0:T(8,128)(2,1)S(1)}, u32[]{:S(2)}, u32[]{:S(2)}) collective-permute-start(bf16[64,768]{1,0:T(8,128)(2,1)S(1)} %get-tuple-element.20), channel_id=1, source_target_pairs={{0,480},{48,528},{96,384},{144,432},{192,672},{240,720},{288,576},... | collective-permute-start | bytes 294920 | tf_op jit(solution)/shard_map/ppermute | solution.py:264
  45.1 0.0 collective-permute-done.refs_1_
  45.2 4.9 %collective-permute-start.5 = (bf16[64,768]{1,0:T(8,128)(2,1)S(1)}, bf16[64,768]{1,0:T(8,128)(2,1)S(1)}, u32[]{:S(2)}, u32[]{:S(2)}) collective-permute-start(bf16[64,768]{1,0:T(8,128)(2,1)S(1)} %get-tuple-element.21), channel_id=1, source_target_pairs={{0,576},{48,624},{96,672},{144,720},{192,384},{240,432},{288,480},... | collective-permute-start | bytes 294920 | tf_op jit(solution)/shard_map/ppermute | solution.py:264
  50.1 0.0 collective-permute-done.1.refs_2_
  50.1 1.9 %collective-permute-start.6 = (bf16[64,768]{1,0:T(8,128)(2,1)S(1)}, bf16[64,768]{1,0:T(8,128)(2,1)S(1)}, u32[]{:S(2)}, u32[]{:S(2)}) collective-permute-start(bf16[64,768]{1,0:T(8,128)(2,1)S(1)} %get-tuple-element.22), channel_id=1, source_target_pairs={{0,672},{48,720},{96,576},{144,624},{192,480},{240,528},{288,384},... | collective-permute-start | bytes 294920 | tf_op jit(solution)/shard_map/ppermute | solution.py:264
  52.0 0.0 collective-permute-done.2.refs_3_
  52.1 0.0 collective-permute-done.3.refs_4_
  52.1 0.0 collective-permute-done.4.refs_5_
  52.1 3.7 %collective-permute-done.5.refs_6_ = bf16[64,768]{1,0:T(8,128)(2,1)S(1)} collective-permute-done((bf16[64,768]{1,0:T(8,128)(2,1)S(1)}, bf16[64,768]{1,0:T(8,128)(2,1)S(1)}, u32[]{:S(2)}, u32[]{:S(2)}) %collective-permute-start.5) | collective-permute-done | bytes 98336 | tf_op jit(solution)/shard_map/ppermute | solution.py:264
  55.8 5.2 %collective-permute-done.6.refs_7_ = bf16[64,768]{1,0:T(8,128)(2,1)S(1)} collective-permute-done((bf16[64,768]{1,0:T(8,128)(2,1)S(1)}, bf16[64,768]{1,0:T(8,128)(2,1)S(1)}, u32[]{:S(2)}, u32[]{:S(2)}) %collective-permute-start.6) | collective-permute-done | bytes 98336 | tf_op jit(solution)/shard_map/ppermute | solution.py:264
  61.1 3.6 %collective-permute-start.7 = (bf16[256,768]{1,0:T(8,128)(2,1)S(1)}, bf16[256,768]{1,0:T(8,128)(2,1)S(1)}, u32[]{:S(2)}, u32[]{:S(2)}) collective-permute-start(bf16[256,768]{1,0:T(8,128)(2,1)S(1)} %slice_dynamic-update-slice_fusion), channel_id=1, source_target_pairs={{0,48},{48,0},{96,144},{144,96},{192,240},{240,192},{288,336},{336... | collective-permute-start | bytes 1179656 | tf_op jit(solution)/shard_map/ppermute | solution.py:266
  64.7 0.4 multiply_reduce_fusion
  65.1 0.0 copy-start.7
  65.1 0.9 collective-permute-done.7.refs_8_
  66.0 0.0 copy-done.6
  66.0 2.8 %shard_map.70 = (f32[128,1024]{1,0:T(8,128)S(1)}, bf16[16,32]{1,0:T(8,128)(2,1)S(1)}) custom-call(bf16[64,768]{1,0:T(8,128)(2,1)S(1)} %get-tuple-element.15.refs_0_, bf16[64,768]{1,0:T(8,128)(2,1)S(1)} %collective-permute-done.refs_1_, bf16[64,768]{1,0:T(8,128)(2,1)S(1)} %collective-permute-done.1.refs_2_, ...), custom_call_target="tpu_custom_call" | custom-call | flops 805306368 | bytes 2359296 | tf_op jit(solution)/shard_map/pallas_call | solution.py:273
  68.9 0.0 all-to-all-done
  68.9 0.6 copy.11
  69.5 9.3 %all-to-all-start.2 = ((bf16[16,1,32]{2,1,0:T(2,128)(2,1)}), bf16[16,1,32]{2,1,0:T(2,128)(2,1)S(1)}, u32[]{:S(2)}, u32[]{:S(2)}) async-start(bf16[16,1,32]{2,1,0:T(2,128)(2,1)} %copy.11), calls=%async_computation.2 | async-start | bytes 16384 | tf_op jit(solution)/shard_map/all_to_all | solution.py:290
  78.8 0.0 copy-done.7
  78.8 2.0 %shard_map.71 = bf16[48,16]{1,0:T(8,128)(2,1)S(1)} custom-call(bf16[768,768]{1,0:T(8,128)(2,1)S(1)} %bitcast.18, bf16[1024,768]{1,0:T(8,128)(2,1)S(1)} %copy-done.1, f32[1,1024]{1,0:T(1,128)S(1)} %bitcast.27, s32[1,48]{1,0:T(1,128)S(1)} %bitcast.31), custom_call_target="tpu_custom_call" | custom-call | flops 1207959552 | bytes 2359296 | tf_op jit(solution)/shard_map/pallas_call | solution.py:293
  80.7 0.6 copy.9
  81.4 4.3 %all-to-all-done.2 = bf16[16,1,32]{2,1,0:T(2,128)(2,1)S(1)} async-done(((bf16[16,1,32]{2,1,0:T(2,128)(2,1)}), bf16[16,1,32]{2,1,0:T(2,128)(2,1)S(1)}, u32[]{:S(2)}, u32[]{:S(2)}) %all-to-all-start.2) | async-done | bytes 1056 | tf_op jit(solution)/shard_map/all_to_all | solution.py:290
  85.7 7.8 %all-to-all-start.1 = ((bf16[48,1,16]{2,1,0:T(2,128)(2,1)}), bf16[48,1,16]{2,1,0:T(2,128)(2,1)S(1)}, u32[]{:S(2)}, u32[]{:S(2)}) async-start(bf16[48,1,16]{2,1,0:T(2,128)(2,1)} %copy.9), calls=%async_computation.1 | async-start | bytes 49152 | tf_op jit(solution)/shard_map/all_to_all | solution.py:301
  93.5 0.0 copy-start.4
  93.5 5.2 %shard_map.72 = f32[16,1024]{1,0:T(8,128)} custom-call(bf16[768,768]{1,0:T(8,128)(2,1)S(1)} %bitcast.19, bf16[1024,768]{1,0:T(8,128)(2,1)S(1)} %copy-done.1, f32[1,1024]{1,0:T(1,128)S(1)} %bitcast.28, s32[1,48]{1,0:T(1,128)S(1)} %bitcast.32, f32[128,1024]{1,0:T(8,128)S(1)} %get-tuple-element.26.held_ref), custom_call_target="tpu_custom_call" | custom-call | flops 2415919104 | bytes 2359296 | tf_op jit(solution)/shard_map/pallas_call | solution.py:304
  98.7 5.9 %all-to-all-done.1 = bf16[48,1,16]{2,1,0:T(2,128)(2,1)S(1)} async-done(((bf16[48,1,16]{2,1,0:T(2,128)(2,1)}), bf16[48,1,16]{2,1,0:T(2,128)(2,1)S(1)}, u32[]{:S(2)}, u32[]{:S(2)}) %all-to-all-start.1) | async-done | bytes 1568 | tf_op jit(solution)/shard_map/all_to_all | solution.py:301
  104.6 0.0 copy-done.4
  104.6 1.9 %shard_map.73 = f32[8,128]{1,0:T(8,128)} custom-call(s32[16,48]{1,0:T(8,128)S(1)} %bitcast.25, s32[16,32]{1,0:T(8,128)S(1)} %copy-done.5, bf16[48,16]{1,0:T(8,128)(2,1)S(1)} %bitcast.21, bf16[16,32]{1,0:T(8,128)(2,1)S(1)} %bitcast.22, s32[1]{0:T(128)} %bitcast.1.refs_2_.refs_12_.place_ref), custom_call_target="tpu_custom_call" | custom-call | tf_op jit(solution)/shard_map/pallas_call | solution.py:314
  (10 shorter events, 0.0 us)
Async XLA Ops:
  0.6 1.4 %copy-start = (bf16[1024,768]{1,0:T(8,128)(2,1)S(1)}, bf16[1024,768]{1,0:T(8,128)(2,1)}, u32[]{:S(2)}) copy-start(bf16[1024,768]{1,0:T(8,128)(2,1)} %points_ref.3) | copy-start | bytes 4718596
  2.0 0.7 copy-start.3
  4.9 1.0 copy-start.2
  6.0 19.0 %copy-start.1 = (bf16[1024,768]{1,0:T(8,128)(2,1)S(1)}, bf16[1024,768]{1,0:T(8,128)(2,1)}, u32[]{:S(2)}) copy-start(bf16[1024,768]{1,0:T(8,128)(2,1)} %points_ref.3) | copy-start | bytes 4718596
  6.0 19.0 %copy-start.5 = (s32[16,32]{1,0:T(8,128)S(1)}, s32[16,32]{1,0:T(8,128)}, u32[]{:S(2)}) copy-start(s32[16,32]{1,0:T(8,128)} %old_lists_ref.1) | copy-start | bytes 6148
  6.0 62.9 %all-to-all-start = ((bf16[48,16,768]{2,1,0:T(8,128)(2,1)}), bf16[48,16,768]{2,1,0:T(8,128)(2,1)S(1)}, u32[]{:S(2)}, u32[]{:S(2)}) async-start(bf16[48,16,768]{2,1,0:T(8,128)(2,1)} %bitcast.20), calls=%async_computation | async-start | bytes 2359296 | tf_op jit(solution)/shard_map/all_to_all | solution.py:258
  26.4 39.6 %copy-start.6 = (s32[16,1]{0,1:T(1,128)S(1)}, s32[16,1]{0,1:T(1,128)}, u32[]{:S(2)}) copy-start(s32[16,1]{0,1:T(1,128)} %param.9) | copy-start | bytes 196
  26.4 18.7 %collective-permute-start = (bf16[64,768]{1,0:T(8,128)(2,1)S(1)}, bf16[64,768]{1,0:T(8,128)(2,1)S(1)}, u32[]{:S(2)}, u32[]{:S(2)}) collective-permute-start(bf16[64,768]{1,0:T(8,128)(2,1)S(1)} %get-tuple-element.16), channel_id=1, source_target_pairs={{0,96},{48,144},{96,0},{144,48},{192,288},{240,336},{288,192},{336... | collective-permute-start | bytes 294920 | tf_op jit(solution)/shard_map/ppermute | solution.py:264
  29.7 20.4 %collective-permute-start.1 = (bf16[64,768]{1,0:T(8,128)(2,1)S(1)}, bf16[64,768]{1,0:T(8,128)(2,1)S(1)}, u32[]{:S(2)}, u32[]{:S(2)}) collective-permute-start(bf16[64,768]{1,0:T(8,128)(2,1)S(1)} %get-tuple-element.17), channel_id=1, source_target_pairs={{0,192},{48,240},{96,288},{144,336},{192,0},{240,48},{288,96},{336... | collective-permute-start | bytes 294920 | tf_op jit(solution)/shard_map/ppermute | solution.py:264
  33.9 18.2 %collective-permute-start.2 = (bf16[64,768]{1,0:T(8,128)(2,1)S(1)}, bf16[64,768]{1,0:T(8,128)(2,1)S(1)}, u32[]{:S(2)}, u32[]{:S(2)}) collective-permute-start(bf16[64,768]{1,0:T(8,128)(2,1)S(1)} %get-tuple-element.18), channel_id=1, source_target_pairs={{0,288},{48,336},{96,192},{144,240},{192,96},{240,144},{288,0},{33... | collective-permute-start | bytes 294920 | tf_op jit(solution)/shard_map/ppermute | solution.py:264
  35.8 16.3 %collective-permute-start.3 = (bf16[64,768]{1,0:T(8,128)(2,1)S(1)}, bf16[64,768]{1,0:T(8,128)(2,1)S(1)}, u32[]{:S(2)}, u32[]{:S(2)}) collective-permute-start(bf16[64,768]{1,0:T(8,128)(2,1)S(1)} %get-tuple-element.19), channel_id=1, source_target_pairs={{0,384},{48,432},{96,480},{144,528},{192,576},{240,624},{288,672},... | collective-permute-start | bytes 294920 | tf_op jit(solution)/shard_map/ppermute | solution.py:264
  43.2 8.9 %collective-permute-start.4 = (bf16[64,768]{1,0:T(8,128)(2,1)S(1)}, bf16[64,768]{1,0:T(8,128)(2,1)S(1)}, u32[]{:S(2)}, u32[]{:S(2)}) collective-permute-start(bf16[64,768]{1,0:T(8,128)(2,1)S(1)} %get-tuple-element.20), channel_id=1, source_target_pairs={{0,480},{48,528},{96,384},{144,432},{192,672},{240,720},{288,576},... | collective-permute-start | bytes 294920 | tf_op jit(solution)/shard_map/ppermute | solution.py:264
  45.2 10.6 %collective-permute-start.5 = (bf16[64,768]{1,0:T(8,128)(2,1)S(1)}, bf16[64,768]{1,0:T(8,128)(2,1)S(1)}, u32[]{:S(2)}, u32[]{:S(2)}) collective-permute-start(bf16[64,768]{1,0:T(8,128)(2,1)S(1)} %get-tuple-element.21), channel_id=1, source_target_pairs={{0,576},{48,624},{96,672},{144,720},{192,384},{240,432},{288,480},... | collective-permute-start | bytes 294920 | tf_op jit(solution)/shard_map/ppermute | solution.py:264
  50.1 11.0 %collective-permute-start.6 = (bf16[64,768]{1,0:T(8,128)(2,1)S(1)}, bf16[64,768]{1,0:T(8,128)(2,1)S(1)}, u32[]{:S(2)}, u32[]{:S(2)}) collective-permute-start(bf16[64,768]{1,0:T(8,128)(2,1)S(1)} %get-tuple-element.22), channel_id=1, source_target_pairs={{0,672},{48,720},{96,576},{144,624},{192,480},{240,528},{288,384},... | collective-permute-start | bytes 294920 | tf_op jit(solution)/shard_map/ppermute | solution.py:264
  61.1 5.0 %collective-permute-start.7 = (bf16[256,768]{1,0:T(8,128)(2,1)S(1)}, bf16[256,768]{1,0:T(8,128)(2,1)S(1)}, u32[]{:S(2)}, u32[]{:S(2)}) collective-permute-start(bf16[256,768]{1,0:T(8,128)(2,1)S(1)} %slice_dynamic-update-slice_fusion), channel_id=1, source_target_pairs={{0,48},{48,0},{96,144},{144,96},{192,240},{240,192},{288,336},{336... | collective-permute-start | bytes 1179656 | tf_op jit(solution)/shard_map/ppermute | solution.py:266
  65.1 13.7 %copy-start.7 = (s32[48,1]{0,1:T(1,128)S(1)}, s32[48,1]{0,1:T(1,128)}, u32[]{:S(2)}) copy-start(s32[48,1]{0,1:T(1,128)} %param.8) | copy-start | bytes 580
  69.5 16.2 %all-to-all-start.2 = ((bf16[16,1,32]{2,1,0:T(2,128)(2,1)}), bf16[16,1,32]{2,1,0:T(2,128)(2,1)S(1)}, u32[]{:S(2)}, u32[]{:S(2)}) async-start(bf16[16,1,32]{2,1,0:T(2,128)(2,1)} %copy.11), calls=%async_computation.2 | async-start | bytes 16384 | tf_op jit(solution)/shard_map/all_to_all | solution.py:290
  85.7 18.9 %all-to-all-start.1 = ((bf16[48,1,16]{2,1,0:T(2,128)(2,1)}), bf16[48,1,16]{2,1,0:T(2,128)(2,1)S(1)}, u32[]{:S(2)}, u32[]{:S(2)}) async-start(bf16[48,1,16]{2,1,0:T(2,128)(2,1)} %copy.9), calls=%async_computation.1 | async-start | bytes 49152 | tf_op jit(solution)/shard_map/all_to_all | solution.py:301
  93.5 11.1 %copy-start.4 = (s32[48,16]{0,1:T(8,128)S(1)}, s32[48,16]{0,1:T(8,128)}, u32[]{:S(2)}) copy-start(s32[48,16]{0,1:T(8,128)} %param.6) | copy-start | bytes 9220

commit v3 on v2

--- a/solution.py
+++ b/solution.py
@@ -67,26 +67,73 @@
     return high.astype(jnp.int32) * 32 + low.astype(jnp.int32)
 
 
-def gather_kernel(peers, slots, flipped, chunk, *refs):
-    points_ref, lists_ref, place_ref = refs[:3]
-    outs = refs[3:]
+def gather_new_kernel(peers, slots, chunk, points_ref, lists_ref, out_ref, points, lists, picked, in_sems, out_sems):
+    total, rows = peers * slots, points.shape[0]
+    loads = [pltpu.make_async_copy(lists_ref, lists, in_sems.at[0])]
+    for k, start in enumerate(range(0, rows, chunk)):
+        part = pl.ds(start, chunk)
+        loads.append(pltpu.make_async_copy(points_ref.at[part, :], points.at[part, :], in_sems.at[k + 1]))
+    for load in loads:
+        load.start()
+    loads[0].wait()
+    index = index_column(lists[...], flat_parts(0, total, peers, slots, straight, True))
+    stores = []
+    for c, at in enumerate(range(0, total, chunk)):
+        acc = None
+        for k, start in enumerate(range(0, rows, chunk)):
+            if c == 0:
+                loads[k + 1].wait()
+            picks = onehot(index[at : at + chunk, :] == iota((chunk, chunk), 1) + start)
+            term = dot(picks, points[start : start + chunk, :])
+            acc = term if acc is None else acc + term
+        picked[at : at + chunk, :] = acc.astype(jnp.bfloat16)
+        part = pl.ds(at, chunk)
+        stores.append(pltpu.make_async_copy(picked.at[part, :], out_ref.at[part, :], out_sems.at[c]))
+        stores[-1].start()
+    for store in stores:
+        store.wait()
+
+
+def gather_new(points, lists, peers, slots):
+    total, chunk = peers * slots, 256
+    rows, features = points.shape
+    hbm = pl.BlockSpec(memory_space=pltpu.HBM)
+    return pl.pallas_call(
+        functools.partial(gather_new_kernel, peers, slots, chunk),
+        in_specs=[hbm, hbm],
+        out_specs=hbm,
+        out_shape=pltpu.HBM((total, features), jnp.bfloat16),
+        scratch_shapes=[
+            pltpu.VMEM((rows, features), jnp.bfloat16),
+            pltpu.VMEM(lists.shape, jnp.int32),
+            pltpu.VMEM((total, features), jnp.bfloat16),
+            pltpu.SemaphoreType.DMA((rows // chunk + 1,)),
+            pltpu.SemaphoreType.DMA((total // chunk,)),
+        ],
+        compiler_params=pltpu.CompilerParams(vmem_limit_bytes=VMEM_LIMIT),
+        cost_estimate=pl.CostEstimate(
+            flops=2 * total * rows * features, bytes_accessed=2 * (total + rows) * features, transcendentals=0
+        ),
+    )(pltpu.with_memory_space_constraint(points, pltpu.HBM), pltpu.with_memory_space_constraint(lists, pltpu.HBM))
+
+
+def gather_old_kernel(groups, slots, chunk, points_ref, lists_ref, place_ref, *outs):
     rows = points_ref.shape[0]
-    order = straight if flipped else lambda block: block ^ place_ref[0]
     size = outs[0].shape[0]
-    for start in range(0, peers * slots, chunk):
-        index = index_column(lists_ref[...], flat_parts(start, chunk, peers, slots, order, flipped))
+    for start in range(0, groups * slots, chunk):
+        parts = flat_parts(start, chunk, groups, slots, lambda block: block ^ place_ref[0])
+        index = index_column(lists_ref[...], parts)
         picked = dot(onehot(index == iota((chunk, rows), 1)), points_ref[...]).astype(jnp.bfloat16)
-        for at in range(start, start + chunk, min(size, chunk)):
-            piece = min(size, chunk)
-            outs[at // size][at % size : at % size + piece, :] = picked[at - start : at - start + piece, :]
-
-
-def gather(points, lists, place, peers, slots, flipped, pieces):
-    total = peers * slots
+        for at in range(0, chunk, size):
+            outs[(start + at) // size][...] = picked[at : at + size, :]
+
+
+def gather_old(points, lists, place, groups, slots, pieces):
+    total = groups * slots
     rows, features = points.shape
     vmem = pl.BlockSpec(memory_space=pltpu.VMEM)
     return pl.pallas_call(
-        functools.partial(gather_kernel, peers, slots, flipped, 256),
+        functools.partial(gather_old_kernel, groups, slots, 256),
         in_specs=[vmem, vmem, pl.BlockSpec(memory_space=pltpu.SMEM)],
         out_shape=(jax.ShapeDtypeStruct((total // pieces, features), jnp.bfloat16),) * pieces,
         compiler_params=pltpu.CompilerParams(vmem_limit_bytes=VMEM_LIMIT),
@@ -143,15 +190,16 @@
     return cand_sq + own_sq_ref[...] - 2.0 * inner
 
 
-def judge(dist, counts_ref, start, peers, slots, order):
-    chunk = dist.shape[0]
-    peer_of, slot_of = flat_parts(start, chunk, peers, slots, order)
+def usable_slots(counts_ref, start, chunk, peers, slots, order):
+    peer_of, _ = flat_parts(start, chunk, peers, slots, order)
     count = jnp.sum(jnp.where(peer_of, counts_ref[...], 0), axis=1, keepdims=True)
-    usable = (iota((chunk, 1), 0) + start) % slots < count
-    minima = jnp.where(usable, jnp.min(dist, axis=1, keepdims=True), cap_value)
-    spread = jnp.where(slot_of, minima, 0.0).astype(jnp.bfloat16)
-    owner = iota((peers, chunk), 0) == order((iota((peers, chunk), 1) + start) // slots)
-    return jnp.where(usable, dist, far_value), dot(onehot(owner), spread)
+    return (iota((chunk, 1), 0) + start) % slots < count
+
+
+def slot_rows(minima, slots):
+    chunk = minima.shape[0]
+    spread = jnp.where(iota((chunk, slots), 1) == iota((chunk, slots), 0) % slots, minima, 0.0)
+    return [jnp.sum(spread[at : at + slots, :], axis=0, keepdims=True) for at in range(0, chunk, slots)]
 
 
 def near_kernel(groups, slots, *refs):
@@ -164,12 +212,15 @@
 
     half = count * slots
     even = jnp.concatenate([ref[:slots, :] for ref in evens], axis=0)
-    back = jnp.zeros((groups, slots), jnp.float32)
+    minima_ref[...] = jnp.zeros_like(minima_ref)
     for start, cand in ((0, even), (half, odd_ref[...])):
-        dist, term = judge(distances(cand, points_ref, own_sq_ref), counts_ref, start, groups, slots, order)
-        dist_ref[start : start + half, :] = dist
-        back = back + term
-    minima_ref[...] = back.astype(jnp.bfloat16)
+        usable = usable_slots(counts_ref, start, half, groups, slots, order)
+        dist = distances(cand, points_ref, own_sq_ref)
+        dist_ref[start : start + half, :] = jnp.where(usable, dist, far_value)
+        minima = jnp.where(usable, jnp.min(dist, axis=1, keepdims=True), cap_value)
+        for k, row in enumerate(slot_rows(minima.astype(jnp.bfloat16).astype(jnp.float32), slots)):
+            source = order(start // slots + k)
+            minima_ref[pl.ds(source * groups + place_ref[0], 1), :] = row
 
     def block(t, _):
         lanes = pl.ds(pl.multiple_of(t * LANES, LANES), LANES)
@@ -180,18 +231,26 @@
     lax.fori_loop(0, dist_ref.shape[1] // LANES, block, 0)
 
 
-def minima_kernel(peers, slots, chunk, cand_ref, points_ref, own_sq_ref, counts_ref, minima_ref):
-    back = jnp.zeros((peers, slots), jnp.float32)
-    for start in range(0, peers * slots, chunk):
-        dist = distances(cand_ref[start : start + chunk, :], points_ref, own_sq_ref)
-        back = back + judge(dist, counts_ref, start, peers, slots, straight)[1]
-    minima_ref[...] = back.astype(jnp.bfloat16)
+def minima_kernel(peers, slots, cand_ref, points_ref, own_sq_ref, counts_ref, minima_ref):
+    total, rows = peers * slots, points_ref.shape[0]
+    cand = cand_ref[...]
+    least = None
+    for start in range(0, rows, 256):
+        part = slice(start, start + 256)
+        dist = distances(cand, points_ref.at[part, :], own_sq_ref.at[:, part])
+        dist = jnp.minimum(dist[:, :LANES], dist[:, LANES:])
+        least = dist if least is None else jnp.minimum(least, dist)
+    usable = usable_slots(counts_ref, 0, total, peers, slots, straight)
+    minima = jnp.where(usable, jnp.min(least, axis=1, keepdims=True), cap_value)
+    for k, row in enumerate(slot_rows(minima, slots)):
+        minima_ref[k] = row.astype(jnp.bfloat16)
 
 
 def select_kernel(peers, slots, chunk, cand_ref, points_ref, own_sq_ref, counts_ref, held_ref, out_ref, dist_ref):
     for start in range(0, peers * slots, chunk):
+        usable = usable_slots(counts_ref, start, chunk, peers, slots, straight)
         dist = distances(cand_ref[start : start + chunk, :], points_ref, own_sq_ref)
-        dist_ref[start : start + chunk, :] = judge(dist, counts_ref, start, peers, slots, straight)[0]
+        dist_ref[start : start + chunk, :] = jnp.where(usable, dist, far_value)
     sublane = iota((SUBLANES, LANES), 0)
 
     def block(t, _):
@@ -209,34 +268,25 @@
     lax.fori_loop(0, dist_ref.shape[1] // LANES, block, 0)
 
 
-def reverse_kernel(gathered, new_lists_ref, old_lists_ref, new_back_ref, old_back_ref, place_ref, out_ref):
-    slots_new, peers_new = new_lists_ref.shape
-    groups, slots_old = old_lists_ref.shape
-    rows = SUBLANES * LANES
-    best = jnp.full((1, rows), cap_value, jnp.float32)
-    chunk = 256
-
-    def fold(best, index, back):
-        matches = index == iota((chunk, rows), 1)
-        return jnp.minimum(best, jnp.min(jnp.where(matches, back, cap_value), axis=0, keepdims=True))
-
-    for start in range(0, groups * slots_old, chunk):
-        index = index_column(old_lists_ref[...], flat_parts(start, chunk, groups, slots_old, straight))
-        if gathered:
-            mine = lambda block: block * groups + place_ref[0]
-            parts = flat_parts(start, chunk, groups * groups, slots_old, mine)
-        else:
-            parts = flat_parts(start, chunk, groups, slots_old, straight)
-        best = fold(best, index, column(*parts, old_back_ref[...]))
-    for start in range(0, peers_new * slots_new, chunk):
-        index = index_column(new_lists_ref[...], flat_parts(start, chunk, peers_new, slots_new, straight, True))
-        parts = flat_parts(start, chunk, peers_new, slots_new, straight)
-        best = fold(best, index, column(*parts, new_back_ref[...]))
+def fold(best, lists, back):
+    peers, slots = lists.shape
+    for c in range(slots):
+        for at in range(0, peers, SUBLANES):
+            index = lists[at : at + SUBLANES, c : c + 1]
+            value = back[at : at + SUBLANES, c : c + 1]
+            best = jnp.where(index == iota(best.shape, 1), jnp.minimum(best, value), best)
+    return best
+
+
+def reverse_old_kernel(lists_ref, back_ref, best_ref):
+    best_ref[...] = fold(jnp.full(best_ref.shape, cap_value, jnp.float32), lists_ref[...], back_ref[...])
+
+
+def reverse_new_kernel(lists_ref, back_ref, best_ref, out_ref):
+    back = back_ref[...].reshape(lists_ref.shape).astype(jnp.float32)
+    best = jnp.min(fold(best_ref[...], lists_ref[...], back), axis=0, keepdims=True)
     for k in range(SUBLANES):
         out_ref[k : k + 1, :] = best[:, LANES * k : LANES * (k + 1)]
-
-
-GATHERED = False
 
 
 def apart(groups, away):
@@ -254,12 +304,12 @@
     smem = pl.BlockSpec(memory_space=pltpu.SMEM)
     place = lax.axis_index("grp").astype(jnp.int32).reshape(1)
 
-    (offered_new,) = gather(points, lists_new, place, peers, slots, True, 1)
+    offered_new = gather_new(points, lists_new, peers, slots)
     pulled_new = lax.all_to_all(
         offered_new.reshape(peers, slots, features), "shard", split_axis=0, concat_axis=0, tiled=True
     ).reshape(peers * slots, features)
 
-    pieces = gather(points, serve_old, place, groups, group_slots, False, groups // 2)
+    pieces = gather_old(points, serve_old, place, groups, group_slots, groups // 2)
     evens = [pieces[0]] + [
         lax.ppermute(pieces[k], "grp", apart(groups, 2 * k)) for k in range(1, groups // 2)
     ]
@@ -274,8 +324,8 @@
         functools.partial(near_kernel, groups, group_slots),
         in_specs=[vmem] * (groups // 2 + 4) + [smem],
         out_shape=(
-            jax.ShapeDtypeStruct((16 * SUBLANES, rows), jnp.float32),
-            jax.ShapeDtypeStruct((groups, group_slots), jnp.bfloat16),
+            pltpu.HBM((16 * SUBLANES, rows), jnp.float32),
+            jax.ShapeDtypeStruct((groups * groups, group_slots), jnp.float32),
         ),
         scratch_shapes=[pltpu.VMEM((total_old, rows), jnp.float32)],
         compiler_params=params,
@@ -283,16 +333,12 @@
             flops=2 * total_old * rows * features, bytes_accessed=2 * (total_old + rows) * features, transcendentals=0
         ),
     )(*evens, odds, points, own_sq, counts_old, place)
-    pulled_new, minima_old = lax.optimization_barrier((pulled_new, minima_old))
-    if GATHERED:
-        back_old = lax.all_gather(minima_old, "grp", axis=0, tiled=True)
-    else:
-        back_old = lax.all_to_all(minima_old, "grp", split_axis=0, concat_axis=0, tiled=True)
+    back_old = lax.psum_scatter(minima_old, "grp", scatter_dimension=0, tiled=True)
 
     total_new = peers * slots
     minima_new = pl.pallas_call(
-        functools.partial(minima_kernel, peers, slots, 256),
-        out_shape=jax.ShapeDtypeStruct((peers, slots), jnp.bfloat16),
+        functools.partial(minima_kernel, peers, slots),
+        out_shape=jax.ShapeDtypeStruct((peers, 1, slots), jnp.bfloat16),
         compiler_params=params,
         cost_estimate=pl.CostEstimate(
             flops=2 * total_new * rows * features, bytes_accessed=4 * total_new * features, transcendentals=0
@@ -311,12 +357,17 @@
         ),
     )(pulled_new, points, own_sq, counts_new, held)
 
+    nearest, back_old = lax.optimization_barrier((nearest, back_old))
+    best = pl.pallas_call(
+        reverse_old_kernel,
+        out_shape=jax.ShapeDtypeStruct((SUBLANES, rows), jnp.float32),
+        compiler_params=params,
+    )(serve_old, back_old)
     reverse = pl.pallas_call(
-        functools.partial(reverse_kernel, GATHERED),
-        in_specs=[vmem] * 4 + [smem],
+        reverse_new_kernel,
         out_shape=jax.ShapeDtypeStruct((SUBLANES, LANES), jnp.float32),
         compiler_params=params,
-    )(lists_new, serve_old, back_new, back_old, place)
+    )(serve_new, back_new, best)
     return nearest.T, reverse.reshape(rows)
 
 

time: 107 us -> 145 us (1.36)
  waiting for transfers between devices: 20.1 us -> 43.8 us
  between operations: 0.91 us -> 14.3 us
  starting transfers between devices: 65.1 us -> 60.9 us
  Pallas kernels: 15.6 us -> 19.1 us
    reduce_scatter x0 -> x1, waiting for transfers between devices: none -> 38.6 us  [body(): lax.psum_scatter(minima_old, 'grp', scatter_dimension=0, tiled=True)]
    all_to_all x1 -> x0, starting transfers between devices: 9.26 us -> none  [body(): lax.all_to_all(minima_old, 'grp', split_axis=0, concat_axis=0, tiled=True)]
    all_to_all x1, waiting for transfers between devices: 5.88 us -> 0.01 us  [body(): lax.all_to_all(minima_new, 'shard', split_axis=0, concat_axis=0, tiled=True)]
    ppermute x7, waiting for transfers between devices: 8.94 us -> 4.06 us  [body(): lax.ppermute(pieces[k], 'grp', apart(groups, 2 * k))]
    all_to_all x1 -> x0, waiting for transfers between devices: 4.33 us -> none  [body(): lax.all_to_all(minima_old, 'grp', split_axis=0, concat_axis=0, tiled=True)]
    all_to_all x1, starting transfers between devices: 7.77 us -> 12.1 us  [body(): lax.all_to_all(minima_new, 'shard', split_axis=0, concat_axis=0, tiled=True)]
    unnamed x24 -> x26, local copies, waits for them, and re-layouts: 3.2 us -> 5.14 us
    pallas_call x4 -> x5, Pallas kernels: 7.53 us -> 9.39 us  [the longest x1 3.66 us: gather_new(): pl.pallas_call(functools.partial(gather_new_kernel, peers, slots, chunk),...]
  transfers between devices with their start and end apart: 11 -> 11, of which waited for: 5 -> 3; matrix products, arithmetic and copies ran while one was open for 1% -> 4% of each run, Pallas kernels for 11% -> 9%
where the time goes in v3:
time: 145 us; the launch traced here: 144 us
  starting transfers between devices  60.9 us (42%)
  waiting for transfers between devices  43.8 us (30%)
  Pallas kernels  19.1 us (13%)
  between operations  14.3 us (10%)
  local copies, waits for them, and re-layouts  5.8 us (4%)
    reduce_scatter x1, waiting for transfers between devices, body(): lax.psum_scatter(minima_old, 'grp', scatter_dimension=0, tiled=True)  38.6 us
    ppermute x7, starting transfers between devices, body(): lax.ppermute(pieces[k], 'grp', apart(groups, 2 * k))  25.5 us
    all_to_all x1, starting transfers between devices, body(): lax.all_to_all(offered_new.reshape(peers, slots, features), 'shard', spli...  19 us
    all_to_all x1, starting transfers between devices, body(): lax.all_to_all(minima_new, 'shard', split_axis=0, concat_axis=0, tiled=True)  12.1 us
    unnamed x26, local copies, waits for them, and re-layouts  5.14 us
    pallas_call x1, Pallas kernels, body(): pl.pallas_call(functools.partial(select_kernel, peers, slots, 256), out_s...  5.13 us
    pallas_call x1, Pallas kernels, body(): pl.pallas_call(functools.partial(near_kernel, groups, group_slots), in_sp...  4.56 us
    ppermute x1, starting transfers between devices, body(): lax.ppermute(jnp.concatenate([piece[group_slots:] for piece in evens], ax...  4.34 us
  transfers between devices with their start and end apart: 11, of which 3 were waited for; matrix products, arithmetic and copies ran while one was open for 4% of the time, Pallas kernels for 9%

profile of v3, /device:TPU:1, one launch (start us, length us, event | category | flops | bytes accessed | tf_op | source)
XLA Modules:
  0.0 144.2 jit_solution(3376933591455127734)
XLA Ops:
  7.2 3.7 %shard_map.68 = bf16[768,768]{1,0:T(8,128)(2,1)} custom-call(bf16[1024,768]{1,0:T(8,128)(2,1)} %points_ref.7, s32[16,48]{1,0:T(8,128)} %bitcast.18), custom_call_target="tpu_custom_call" | custom-call | flops 1207959552 | bytes 2752512 | tf_op jit(solution)/shard_map/pallas_call | solution.py:101
  10.8 0.0 copy-start
  10.8 0.0 copy-start.3
  10.9 19.0 %all-to-all-start = ((bf16[48,16,768]{2,1,0:T(8,128)(2,1)}), bf16[48,16,768]{2,1,0:T(8,128)(2,1)S(1)}, u32[]{:S(2)}, u32[]{:S(2)}) async-start(bf16[48,16,768]{2,1,0:T(8,128)(2,1)} %bitcast.17), calls=%async_computation | async-start | bytes 2359296 | tf_op jit(solution)/shard_map/all_to_all | solution.py:308
  29.8 0.0 reduce-scatter.2.cloned.1.call-start
  29.9 0.0 copy-done
  29.9 0.0 copy-done.3
  29.9 0.0 copy-start.8
  29.9 1.5 %shard_map.70 = (bf16[64,768]{1,0:T(8,128)(2,1)S(1)}, bf16[64,768]{1,0:T(8,128)(2,1)S(1)}, bf16[64,768]{1,0:T(8,128)(2,1)S(1)}, bf16[64,768]{1,0:T(8,128)(2,1)S(...) custom-call(bf16[1024,768]{1,0:T(8,128)(2,1)S(1)} %copy-done, ...), custom_call_target="tpu_custom_call" | custom-call | flops 805306368 | bytes 2359296 | tf_op jit(solution)/shard_map/pallas_call | solution.py:135
  31.4 0.0 copy-start.5
  31.4 3.2 %collective-permute-start = (bf16[64,768]{1,0:T(8,128)(2,1)S(1)}, bf16[64,768]{1,0:T(8,128)(2,1)S(1)}, u32[]{:S(2)}, u32[]{:S(2)}) collective-permute-start(bf16[64,768]{1,0:T(8,128)(2,1)S(1)} %get-tuple-element.17), channel_id=1, source_target_pairs={{0,96},{48,144},{96,0},{144,48},{192,288},{240,336},{288,192},{336... | collective-permute-start | bytes 294920 | tf_op jit(solution)/shard_map/ppermute | solution.py:314
  34.6 4.2 %collective-permute-start.1 = (bf16[64,768]{1,0:T(8,128)(2,1)S(1)}, bf16[64,768]{1,0:T(8,128)(2,1)S(1)}, u32[]{:S(2)}, u32[]{:S(2)}) collective-permute-start(bf16[64,768]{1,0:T(8,128)(2,1)S(1)} %get-tuple-element.18), channel_id=1, source_target_pairs={{0,192},{48,240},{96,288},{144,336},{192,0},{240,48},{288,96},{336... | collective-permute-start | bytes 294920 | tf_op jit(solution)/shard_map/ppermute | solution.py:314
  38.8 1.9 %collective-permute-start.2 = (bf16[64,768]{1,0:T(8,128)(2,1)S(1)}, bf16[64,768]{1,0:T(8,128)(2,1)S(1)}, u32[]{:S(2)}, u32[]{:S(2)}) collective-permute-start(bf16[64,768]{1,0:T(8,128)(2,1)S(1)} %get-tuple-element.19), channel_id=1, source_target_pairs={{0,288},{48,336},{96,192},{144,240},{192,96},{240,144},{288,0},{33... | collective-permute-start | bytes 294920 | tf_op jit(solution)/shard_map/ppermute | solution.py:314
  40.8 7.4 %collective-permute-start.3 = (bf16[64,768]{1,0:T(8,128)(2,1)S(1)}, bf16[64,768]{1,0:T(8,128)(2,1)S(1)}, u32[]{:S(2)}, u32[]{:S(2)}) collective-permute-start(bf16[64,768]{1,0:T(8,128)(2,1)S(1)} %get-tuple-element.20), channel_id=1, source_target_pairs={{0,384},{48,432},{96,480},{144,528},{192,576},{240,624},{288,672},... | collective-permute-start | bytes 294920 | tf_op jit(solution)/shard_map/ppermute | solution.py:314
  48.2 1.9 %collective-permute-start.4 = (bf16[64,768]{1,0:T(8,128)(2,1)S(1)}, bf16[64,768]{1,0:T(8,128)(2,1)S(1)}, u32[]{:S(2)}, u32[]{:S(2)}) collective-permute-start(bf16[64,768]{1,0:T(8,128)(2,1)S(1)} %get-tuple-element.21), channel_id=1, source_target_pairs={{0,480},{48,528},{96,384},{144,432},{192,672},{240,720},{288,576},... | collective-permute-start | bytes 294920 | tf_op jit(solution)/shard_map/ppermute | solution.py:314
  50.1 0.6 slice_dynamic-update-slice_fusion.7
  50.7 0.0 collective-permute-done.refs_1_
  50.7 4.9 %collective-permute-start.5 = (bf16[64,768]{1,0:T(8,128)(2,1)S(1)}, bf16[64,768]{1,0:T(8,128)(2,1)S(1)}, u32[]{:S(2)}, u32[]{:S(2)}) collective-permute-start(bf16[64,768]{1,0:T(8,128)(2,1)S(1)} %get-tuple-element.22), channel_id=1, source_target_pairs={{0,576},{48,624},{96,672},{144,720},{192,384},{240,432},{288,480},... | collective-permute-start | bytes 294920 | tf_op jit(solution)/shard_map/ppermute | solution.py:314
  55.6 0.6 slice_dynamic-update-slice_fusion.6
  56.3 0.0 collective-permute-done.1.refs_2_
  56.3 1.9 %collective-permute-start.6 = (bf16[64,768]{1,0:T(8,128)(2,1)S(1)}, bf16[64,768]{1,0:T(8,128)(2,1)S(1)}, u32[]{:S(2)}, u32[]{:S(2)}) collective-permute-start(bf16[64,768]{1,0:T(8,128)(2,1)S(1)} %get-tuple-element.23), channel_id=1, source_target_pairs={{0,672},{48,720},{96,576},{144,624},{192,480},{240,528},{288,384},... | collective-permute-start | bytes 294920 | tf_op jit(solution)/shard_map/ppermute | solution.py:314
  58.2 0.6 slice_dynamic-update-slice_fusion.5
  58.8 0.0 collective-permute-done.2.refs_3_
  58.8 0.6 slice_dynamic-update-slice_fusion.4
  59.4 0.0 collective-permute-done.3.refs_4_
  59.4 0.6 slice_dynamic-update-slice_fusion.3
  60.0 0.0 collective-permute-done.4.refs_5_
  60.0 0.6 slice_dynamic-update-slice_fusion.2
  60.6 0.0 collective-permute-done.5.refs_6_
  60.7 0.6 slice_dynamic-update-slice_fusion.1
  61.3 4.0 %collective-permute-done.6.refs_7_ = bf16[64,768]{1,0:T(8,128)(2,1)S(1)} collective-permute-done((bf16[64,768]{1,0:T(8,128)(2,1)S(1)}, bf16[64,768]{1,0:T(8,128)(2,1)S(1)}, u32[]{:S(2)}, u32[]{:S(2)}) %collective-permute-start.6) | collective-permute-done | bytes 98336 | tf_op jit(solution)/shard_map/ppermute | solution.py:314
  65.3 0.0 copy-start.1
  65.3 0.7 slice_dynamic-update-slice_fusion
  66.0 0.0 copy-done.1
  66.0 4.3 %collective-permute-start.7 = (bf16[256,768]{1,0:T(8,128)(2,1)}, bf16[256,768]{1,0:T(8,128)(2,1)}, u32[]{:S(2)}, u32[]{:S(2)}) collective-permute-start(bf16[256,768]{1,0:T(8,128)(2,1)} %slice_dynamic-update-slice_fusion), channel_id=1, source_target_pairs={{0,48},{48,0},{96,144},{144,96},{192,240},{240,192},{288,336},{336... | collective-permute-start | bytes 1179656 | tf_op jit(solution)/shard_map/ppermute | solution.py:316
  70.3 0.0 copy-done.8
  70.3 0.1 copy.7.lists_ref
  70.4 0.0 copy-start.2
  70.4 0.4 multiply_reduce_fusion
  70.8 0.0 copy-start.6
  70.8 1.2 collective-permute-done.7.refs_8_
  72.0 0.0 copy-done.5
  72.0 0.0 copy-done.2
  72.0 4.6 %shard_map.71 = (f32[128,1024]{1,0:T(8,128)}, f32[256,32]{1,0:T(8,128)}) custom-call(bf16[64,768]{1,0:T(8,128)(2,1)S(1)} %get-tuple-element.16.refs_0_, bf16[64,768]{1,0:T(8,128)(2,1)S(1)} %collective-permute-done.refs_1_, bf16[64,768]{1,0:T(8,128)(2,1)S(1)} %collective-permute-done.1.refs_2_, bf16[64,768]{1,0:T(8,128)(2,1)S(1)} %collective-permute-done.2.refs_3_, ...), custom_call_target="tpu_custom_call" | custom-call | flops 805306368 | bytes 2359296 | tf_op jit(solution)/shard_map/pallas_call | solution.py:323
  76.6 0.0 reduce-scatter.2.cloned.1.call-update
  76.6 0.0 all-to-all-done
  76.6 0.0 copy-done.6
  76.6 0.0 copy-start.7
  76.6 2.3 %shard_map.69 = bf16[48,1,16]{2,1,0:T(2,128)(2,1)} custom-call(bf16[768,768]{1,0:T(8,128)(2,1)S(1)} %bitcast.9, bf16[1024,768]{1,0:T(8,128)(2,1)S(1)} %copy-done, f32[1,1024]{1,0:T(1,128)S(1)} %bitcast.12, s32[1,48]{1,0:T(1,128)S(1)} %bitcast.15), custom_call_target="tpu_custom_call" | custom-call | flops 1207959552 | bytes 2359296 | tf_op jit(solution)/shard_map/pallas_call | solution.py:339
  78.9 12.1 %all-to-all-start.1 = ((bf16[48,1,16]{2,1,0:T(2,128)(2,1)}), bf16[48,1,16]{2,1,0:T(2,128)(2,1)S(1)}, u32[]{:S(2)}, u32[]{:S(2)}) async-start(bf16[48,1,16]{2,1,0:T(2,128)(2,1)} %shard_map.69), calls=%async_computation.2 | async-start | bytes 49152 | tf_op jit(solution)/shard_map/all_to_all | solution.py:347
  91.0 0.0 copy-done.7
  91.0 5.1 %shard_map.72 = f32[16,1024]{1,0:T(8,128)} custom-call(bf16[768,768]{1,0:T(8,128)(2,1)S(1)} %bitcast.10, bf16[1024,768]{1,0:T(8,128)(2,1)S(1)} %copy-done, f32[1,1024]{1,0:T(1,128)S(1)} %bitcast.13, s32[1,48]{1,0:T(1,128)S(1)} %bitcast.16, f32[128,1024]{1,0:T(8,128)S(1)} %copy-done.7), custom_call_target="tpu_custom_call" | custom-call | flops 2415919104 | bytes 2359296 | tf_op jit(solution)/shard_map/pallas_call | solution.py:350
  96.1 38.6 %reduce-scatter.2.cloned.1.call-done.back_ref = f32[16,32]{1,0:T(8,128)} async-done(((f32[256,32]{1,0:T(8,128)}), f32[16,32]{1,0:T(8,128)}) %reduce-scatter.2.cloned.1.call-update) | async-done | bytes 2064 | tf_op jit(solution)/shard_map/reduce_scatter | solution.py:336
  134.7 0.0 copy-start.4
  134.7 0.7 copy-done.4
  135.4 0.3 shard_map.73.best_ref
  135.7 0.0 all-to-all-done.1.back_ref
  135.7 1.7 %shard_map.74 = f32[8,128]{1,0:T(8,128)} custom-call(s32[48,16]{1,0:T(8,128)S(1)} %copy.7.lists_ref, bf16[48,1,16]{2,1,0:T(2,128)(2,1)S(1)} %all-to-all-done.1.back_ref, f32[8,1024]{1,0:T(8,128)S(1)} %shard_map.73.best_ref), custom_call_target="tpu_custom_call" | custom-call | tf_op jit(solution)/shard_map/pallas_call | solution.py:366
Async XLA Ops:
  10.8 19.1 %copy-start = (bf16[1024,768]{1,0:T(8,128)(2,1)S(1)}, bf16[1024,768]{1,0:T(8,128)(2,1)}, u32[]{:S(2)}) copy-start(bf16[1024,768]{1,0:T(8,128)(2,1)} %points_ref.7) | copy-start | bytes 4718596
  10.8 19.1 %copy-start.3 = (s32[16,32]{1,0:T(8,128)S(1)}, s32[16,32]{1,0:T(8,128)}, u32[]{:S(2)}) copy-start(s32[16,32]{1,0:T(8,128)} %lists_ref.4) | copy-start | bytes 6148
  10.9 65.7 %all-to-all-start = ((bf16[48,16,768]{2,1,0:T(8,128)(2,1)}), bf16[48,16,768]{2,1,0:T(8,128)(2,1)S(1)}, u32[]{:S(2)}, u32[]{:S(2)}) async-start(bf16[48,16,768]{2,1,0:T(8,128)(2,1)} %bitcast.17), calls=%async_computation | async-start | bytes 2359296 | tf_op jit(solution)/shard_map/all_to_all | solution.py:308
  29.8 104.8 %reduce-scatter.2.cloned.1.call-start = ((), (), s32[]{:S(2)}) async-start(), calls=%async_computation.3 | async-start | bytes 139264 | tf_op jit(solution)/shard_map/reduce_scatter | solution.py:336
  29.9 40.4 %copy-start.8 = (s32[48,16]{0,1:T(8,128)S(1)}, s32[48,16]{0,1:T(8,128)}, u32[]{:S(2)}) copy-start(s32[48,16]{0,1:T(8,128)} %param.6) | copy-start | bytes 9220
  31.4 40.6 %copy-start.5 = (s32[16,1]{0,1:T(1,128)S(1)}, s32[16,1]{0,1:T(1,128)}, u32[]{:S(2)}) copy-start(s32[16,1]{0,1:T(1,128)} %param.9) | copy-start | bytes 196
  31.4 19.3 %collective-permute-start = (bf16[64,768]{1,0:T(8,128)(2,1)S(1)}, bf16[64,768]{1,0:T(8,128)(2,1)S(1)}, u32[]{:S(2)}, u32[]{:S(2)}) collective-permute-start(bf16[64,768]{1,0:T(8,128)(2,1)S(1)} %get-tuple-element.17), channel_id=1, source_target_pairs={{0,96},{48,144},{96,0},{144,48},{192,288},{240,336},{288,192},{336... | collective-permute-start | bytes 294920 | tf_op jit(solution)/shard_map/ppermute | solution.py:314
  34.6 21.6 %collective-permute-start.1 = (bf16[64,768]{1,0:T(8,128)(2,1)S(1)}, bf16[64,768]{1,0:T(8,128)(2,1)S(1)}, u32[]{:S(2)}, u32[]{:S(2)}) collective-permute-start(bf16[64,768]{1,0:T(8,128)(2,1)S(1)} %get-tuple-element.18), channel_id=1, source_target_pairs={{0,192},{48,240},{96,288},{144,336},{192,0},{240,48},{288,96},{336... | collective-permute-start | bytes 294920 | tf_op jit(solution)/shard_map/ppermute | solution.py:314
  38.8 19.9 %collective-permute-start.2 = (bf16[64,768]{1,0:T(8,128)(2,1)S(1)}, bf16[64,768]{1,0:T(8,128)(2,1)S(1)}, u32[]{:S(2)}, u32[]{:S(2)}) collective-permute-start(bf16[64,768]{1,0:T(8,128)(2,1)S(1)} %get-tuple-element.19), channel_id=1, source_target_pairs={{0,288},{48,336},{96,192},{144,240},{192,96},{240,144},{288,0},{33... | collective-permute-start | bytes 294920 | tf_op jit(solution)/shard_map/ppermute | solution.py:314
  40.8 18.6 %collective-permute-start.3 = (bf16[64,768]{1,0:T(8,128)(2,1)S(1)}, bf16[64,768]{1,0:T(8,128)(2,1)S(1)}, u32[]{:S(2)}, u32[]{:S(2)}) collective-permute-start(bf16[64,768]{1,0:T(8,128)(2,1)S(1)} %get-tuple-element.20), channel_id=1, source_target_pairs={{0,384},{48,432},{96,480},{144,528},{192,576},{240,624},{288,672},... | collective-permute-start | bytes 294920 | tf_op jit(solution)/shard_map/ppermute | solution.py:314
  48.2 11.9 %collective-permute-start.4 = (bf16[64,768]{1,0:T(8,128)(2,1)S(1)}, bf16[64,768]{1,0:T(8,128)(2,1)S(1)}, u32[]{:S(2)}, u32[]{:S(2)}) collective-permute-start(bf16[64,768]{1,0:T(8,128)(2,1)S(1)} %get-tuple-element.21), channel_id=1, source_target_pairs={{0,480},{48,528},{96,384},{144,432},{192,672},{240,720},{288,576},... | collective-permute-start | bytes 294920 | tf_op jit(solution)/shard_map/ppermute | solution.py:314
  50.7 9.9 %collective-permute-start.5 = (bf16[64,768]{1,0:T(8,128)(2,1)S(1)}, bf16[64,768]{1,0:T(8,128)(2,1)S(1)}, u32[]{:S(2)}, u32[]{:S(2)}) collective-permute-start(bf16[64,768]{1,0:T(8,128)(2,1)S(1)} %get-tuple-element.22), channel_id=1, source_target_pairs={{0,576},{48,624},{96,672},{144,720},{192,384},{240,432},{288,480},... | collective-permute-start | bytes 294920 | tf_op jit(solution)/shard_map/ppermute | solution.py:314
  56.3 9.1 %collective-permute-start.6 = (bf16[64,768]{1,0:T(8,128)(2,1)S(1)}, bf16[64,768]{1,0:T(8,128)(2,1)S(1)}, u32[]{:S(2)}, u32[]{:S(2)}) collective-permute-start(bf16[64,768]{1,0:T(8,128)(2,1)S(1)} %get-tuple-element.23), channel_id=1, source_target_pairs={{0,672},{48,720},{96,576},{144,624},{192,480},{240,528},{288,384},... | collective-permute-start | bytes 294920 | tf_op jit(solution)/shard_map/ppermute | solution.py:314
  65.3 0.7 copy-start.1
  66.0 6.0 %collective-permute-start.7 = (bf16[256,768]{1,0:T(8,128)(2,1)}, bf16[256,768]{1,0:T(8,128)(2,1)}, u32[]{:S(2)}, u32[]{:S(2)}) collective-permute-start(bf16[256,768]{1,0:T(8,128)(2,1)} %slice_dynamic-update-slice_fusion), channel_id=1, source_target_pairs={{0,48},{48,0},{96,144},{144,96},{192,240},{240,192},{288,336},{336... | collective-permute-start | bytes 1179656 | tf_op jit(solution)/shard_map/ppermute | solution.py:316
  70.4 1.6 %copy-start.2 = (bf16[64,768]{1,0:T(8,128)(2,1)S(1)}, bf16[64,768]{1,0:T(8,128)(2,1)}, u32[]{:S(2)}) copy-start(bf16[64,768]{1,0:T(8,128)(2,1)} %copy-done.1) | copy-start | bytes 294916
  70.8 5.8 %copy-start.6 = (s32[48,1]{0,1:T(1,128)S(1)}, s32[48,1]{0,1:T(1,128)}, u32[]{:S(2)}) copy-start(s32[48,1]{0,1:T(1,128)} %param.8) | copy-start | bytes 580
  76.6 14.4 %copy-start.7 = (f32[128,1024]{1,0:T(8,128)S(1)}, f32[128,1024]{1,0:T(8,128)}, u32[]{:S(2)}) copy-start(f32[128,1024]{1,0:T(8,128)} %get-tuple-element.24.held_ref) | copy-start | bytes 1572868
  78.9 56.8 %all-to-all-start.1 = ((bf16[48,1,16]{2,1,0:T(2,128)(2,1)}), bf16[48,1,16]{2,1,0:T(2,128)(2,1)S(1)}, u32[]{:S(2)}, u32[]{:S(2)}) async-start(bf16[48,1,16]{2,1,0:T(2,128)(2,1)} %shard_map.69), calls=%async_computation.2 | async-start | bytes 49152 | tf_op jit(solution)/shard_map/all_to_all | solution.py:347
  134.7 0.7 copy-start.4
Sparse Core Ops, SparseCore 0:
  76.7 57.9 reduce-scatter.1

commit v4 on v3

--- a/solution.py
+++ b/solution.py
@@ -2,6 +2,7 @@
 
 import jax
 import jax.numpy as jnp
+import numpy as np
 from jax import lax
 from jax.experimental import pallas as pl
 from jax.experimental.pallas import tpu as pltpu
@@ -205,22 +206,22 @@
 def near_kernel(groups, slots, *refs):
     count = groups // 2
     evens, (odd_ref, points_ref, own_sq_ref, counts_ref, place_ref) = refs[:count], refs[count : count + 5]
-    held_ref, minima_ref, dist_ref = refs[count + 5 :]
+    held_ref, minima_ref, dist_ref, rows_ref = refs[count + 5 :]
 
     def order(block):
         return jnp.where(block < count, 2 * block, 2 * (block - count) + 1) ^ place_ref[0]
 
     half = count * slots
     even = jnp.concatenate([ref[:slots, :] for ref in evens], axis=0)
-    minima_ref[...] = jnp.zeros_like(minima_ref)
     for start, cand in ((0, even), (half, odd_ref[...])):
         usable = usable_slots(counts_ref, start, half, groups, slots, order)
         dist = distances(cand, points_ref, own_sq_ref)
         dist_ref[start : start + half, :] = jnp.where(usable, dist, far_value)
         minima = jnp.where(usable, jnp.min(dist, axis=1, keepdims=True), cap_value)
-        for k, row in enumerate(slot_rows(minima.astype(jnp.bfloat16).astype(jnp.float32), slots)):
-            source = order(start // slots + k)
-            minima_ref[pl.ds(source * groups + place_ref[0], 1), :] = row
+        for k, row in enumerate(slot_rows(minima, slots)):
+            at = 2 * k + (start > 0)
+            rows_ref[at : at + 1, :] = row
+    minima_ref[...] = rows_ref[...].astype(jnp.bfloat16)
 
     def block(t, _):
         lanes = pl.ds(pl.multiple_of(t * LANES, LANES), LANES)
@@ -234,38 +235,53 @@
 def minima_kernel(peers, slots, cand_ref, points_ref, own_sq_ref, counts_ref, minima_ref):
     total, rows = peers * slots, points_ref.shape[0]
     cand = cand_ref[...]
+    wide = cand.astype(jnp.float32)
+    cand_sq = jnp.sum(wide * wide, axis=1, keepdims=True)
     least = None
     for start in range(0, rows, 256):
-        part = slice(start, start + 256)
-        dist = distances(cand, points_ref.at[part, :], own_sq_ref.at[:, part])
-        dist = jnp.minimum(dist[:, :LANES], dist[:, LANES:])
-        least = dist if least is None else jnp.minimum(least, dist)
+        inner = lax.dot_general(
+            cand, points_ref[start : start + 256, :], (((1,), (1,)), ((), ())), preferred_element_type=jnp.float32
+        )
+        for at in range(0, 256, LANES):
+            own = own_sq_ref[:, start + at : start + at + LANES]
+            dist = cand_sq + own - 2.0 * inner[:, at : at + LANES]
+            least = dist if least is None else jnp.minimum(least, dist)
     usable = usable_slots(counts_ref, 0, total, peers, slots, straight)
     minima = jnp.where(usable, jnp.min(least, axis=1, keepdims=True), cap_value)
     for k, row in enumerate(slot_rows(minima, slots)):
         minima_ref[k] = row.astype(jnp.bfloat16)
 
 
-def select_kernel(peers, slots, chunk, cand_ref, points_ref, own_sq_ref, counts_ref, held_ref, out_ref, dist_ref):
-    for start in range(0, peers * slots, chunk):
+def select_kernel(peers, slots, first, done, *refs):
+    cand_ref, points_ref, own_sq_ref, counts_ref, held_ref = refs[:5]
+    parts, (out_ref, dist_ref) = refs[5 : 5 + done], refs[5 + done :]
+    total, rows = dist_ref.shape
+    chunk = 256
+    for start in range(0, total, chunk):
         usable = usable_slots(counts_ref, start, chunk, peers, slots, straight)
-        dist = distances(cand_ref[start : start + chunk, :], points_ref, own_sq_ref)
+        points, own = points_ref.at[first : first + rows, :], own_sq_ref.at[:, first : first + rows]
+        dist = distances(cand_ref[start : start + chunk, :], points, own)
         dist_ref[start : start + chunk, :] = jnp.where(usable, dist, far_value)
     sublane = iota((SUBLANES, LANES), 0)
+    for k, part in enumerate(parts):
+        out_ref[:, k * rows : (k + 1) * rows] = part[...]
+    shift_out = done * rows
 
     def block(t, _):
         lanes = pl.ds(pl.multiple_of(t * LANES, LANES), LANES)
-        held = smallest16(dist_ref, lanes, block16(held_ref, 0, lanes))
+        there = pl.ds(pl.multiple_of(t * LANES + first, LANES), LANES)
+        held = smallest16(dist_ref, lanes, block16(held_ref, 0, there))
         for shift in (4, 2, 1):
             held = merge16(held, [pltpu.roll(value, shift, 0) for value in held])
         for half in range(2):
-            rows = held[SUBLANES * half]
+            near = held[SUBLANES * half]
             for k in range(1, SUBLANES):
-                rows = jnp.where(sublane == k, held[SUBLANES * half + k], rows)
-            out_ref[SUBLANES * half : SUBLANES * (half + 1), lanes] = rows
+                near = jnp.where(sublane == k, held[SUBLANES * half + k], near)
+            out_lanes = pl.ds(pl.multiple_of(t * LANES + shift_out, LANES), LANES)
+            out_ref[SUBLANES * half : SUBLANES * (half + 1), out_lanes] = near
         return 0
 
-    lax.fori_loop(0, dist_ref.shape[1] // LANES, block, 0)
+    lax.fori_loop(0, rows // LANES, block, 0)
 
 
 def fold(best, lists, back):
@@ -278,8 +294,12 @@
     return best
 
 
-def reverse_old_kernel(lists_ref, back_ref, best_ref):
-    best_ref[...] = fold(jnp.full(best_ref.shape, cap_value, jnp.float32), lists_ref[...], back_ref[...])
+def reverse_old_kernel(bit, lists_ref, kept_ref, came_ref, place_ref, best_ref):
+    groups = lists_ref.shape[0]
+    back = jnp.where(iota(kept_ref.shape, 0) & bit != 0, came_ref[...].astype(jnp.float32), kept_ref[...].astype(jnp.float32))
+    rows_of = iota((groups, groups), 1) == iota((groups, groups), 0) ^ place_ref[0]
+    back = dot(onehot(rows_of), back.astype(jnp.bfloat16))
+    best_ref[...] = fold(jnp.full(best_ref.shape, cap_value, jnp.float32), lists_ref[...], back)
 
 
 def reverse_new_kernel(lists_ref, back_ref, best_ref, out_ref):
@@ -324,17 +344,18 @@
         functools.partial(near_kernel, groups, group_slots),
         in_specs=[vmem] * (groups // 2 + 4) + [smem],
         out_shape=(
-            pltpu.HBM((16 * SUBLANES, rows), jnp.float32),
-            jax.ShapeDtypeStruct((groups * groups, group_slots), jnp.float32),
+            jax.ShapeDtypeStruct((16 * SUBLANES, rows), jnp.float32),
+            jax.ShapeDtypeStruct((groups, group_slots), jnp.bfloat16),
         ),
-        scratch_shapes=[pltpu.VMEM((total_old, rows), jnp.float32)],
+        scratch_shapes=[
+            pltpu.VMEM((total_old, rows), jnp.float32),
+            pltpu.VMEM((groups, group_slots), jnp.float32),
+        ],
         compiler_params=params,
         cost_estimate=pl.CostEstimate(
             flops=2 * total_old * rows * features, bytes_accessed=2 * (total_old + rows) * features, transcendentals=0
         ),
     )(*evens, odds, points, own_sq, counts_old, place)
-    back_old = lax.psum_scatter(minima_old, "grp", scatter_dimension=0, tiled=True)
-
     total_new = peers * slots
     minima_new = pl.pallas_call(
         functools.partial(minima_kernel, peers, slots),
@@ -346,23 +367,36 @@
     )(pulled_new, points, own_sq, counts_new)
     back_new = lax.all_to_all(minima_new, "shard", split_axis=0, concat_axis=0, tiled=True)
 
-    pulled_new, _ = lax.optimization_barrier((pulled_new, minima_new))
-    nearest = pl.pallas_call(
-        functools.partial(select_kernel, peers, slots, 256),
-        out_shape=jax.ShapeDtypeStruct((NEAR, rows), jnp.float32),
-        scratch_shapes=[pltpu.VMEM((total_new, rows), jnp.float32)],
-        compiler_params=params,
-        cost_estimate=pl.CostEstimate(
-            flops=4 * total_new * rows * features, bytes_accessed=4 * total_new * features, transcendentals=0
-        ),
-    )(pulled_new, points, own_sq, counts_new, held)
-
-    nearest, back_old = lax.optimization_barrier((nearest, back_old))
+    pulled_new, kept, _ = lax.optimization_barrier((pulled_new, minima_old, minima_new))
+    steps = groups.bit_length() - 1
+    part = rows // steps
+    nearest = []
+    for step in range(steps):
+        bit = 1 << step
+        came = lax.ppermute(kept, "grp", apart(groups, bit))
+        last = step == steps - 1
+        nearest.append(
+            pl.pallas_call(
+                functools.partial(select_kernel, peers, slots, step * part, step if last else 0),
+                out_shape=jax.ShapeDtypeStruct((NEAR, rows if last else part), jnp.float32),
+                scratch_shapes=[pltpu.VMEM((total_new, part), jnp.float32)],
+                compiler_params=params,
+                cost_estimate=pl.CostEstimate(
+                    flops=2 * total_new * rows * features, bytes_accessed=4 * total_new * features, transcendentals=0
+                ),
+            )(pulled_new, points, own_sq, counts_new, held, *(nearest if last else []))
+        )
+        if not last:
+            kept = jnp.where(np.arange(groups)[:, None] & np.full(group_slots, bit) != 0, came, kept)
+            kept, pulled_new = lax.optimization_barrier((kept, pulled_new))
+    nearest = nearest[-1]
+
     best = pl.pallas_call(
-        reverse_old_kernel,
+        functools.partial(reverse_old_kernel, bit),
+        in_specs=[vmem] * 3 + [smem],
         out_shape=jax.ShapeDtypeStruct((SUBLANES, rows), jnp.float32),
         compiler_params=params,
-    )(serve_old, back_old)
+    )(serve_old, kept, came, place)
     reverse = pl.pallas_call(
         reverse_new_kernel,
         out_shape=jax.ShapeDtypeStruct((SUBLANES, LANES), jnp.float32),

time: 145 us -> 111 us (0.77)
  the two profiles are of different devices: /device:TPU:1 before, /device:TPU:6 now
where the time goes in v4:
time: 111 us
  starting transfers between devices  74.6 us (67%)
  Pallas kernels  19.6 us (18%)
  waiting for transfers between devices  9.21 us (8%)
  local copies, waits for them, and re-layouts  5.92 us (5%)
    ppermute x7, starting transfers between devices, body(): lax.ppermute(pieces[k], 'grp', apart(groups, 2 * k))  27.1 us
    all_to_all x1, starting transfers between devices, body(): lax.all_to_all(offered_new.reshape(peers, slots, features), 'shard', spli...  18.7 us
    ppermute x4, starting transfers between devices, body(): came = lax.ppermute(kept, 'grp', apart(groups, bit))  14.3 us
    all_to_all x1, starting transfers between devices, body(): lax.all_to_all(minima_new, 'shard', split_axis=0, concat_axis=0, tiled=True)  12.5 us
    pallas_call x4, Pallas kernels, body(): pl.pallas_call(functools.partial(select_kernel, peers, slots, step * part...  6.36 us
    unnamed x32, local copies, waits for them, and re-layouts  5.28 us
    ppermute x4, waiting for transfers between devices, body(): came = lax.ppermute(kept, 'grp', apart(groups, bit))  3.92 us
    ppermute x7, waiting for transfers between devices, body(): lax.ppermute(pieces[k], 'grp', apart(groups, 2 * k))  3.73 us
  transfers between devices with their start and end apart: 14, of which 6 were waited for; matrix products, arithmetic and copies ran while one was open for 5% of the time, Pallas kernels for 11%

profile of v4, /device:TPU:6, one launch (start us, length us, event | category | flops | bytes accessed | tf_op | source)
XLA Modules:
  0.0 110.7 jit_solution(11287458716548039500)
XLA Ops:
  0.6 3.6 %shard_map.95 = bf16[768,768]{1,0:T(8,128)(2,1)} custom-call(bf16[1024,768]{1,0:T(8,128)(2,1)} %refs_1_.7, s32[16,48]{1,0:T(8,128)} %bitcast.27), custom_call_target="tpu_custom_call" | custom-call | flops 1207959552 | bytes 2752512 | tf_op jit(solution)/shard_map/pallas_call | solution.py:102
  4.3 0.0 copy-start
  4.3 0.0 copy-start.3
  4.3 18.7 %all-to-all-start = ((bf16[48,16,768]{2,1,0:T(8,128)(2,1)}), bf16[48,16,768]{2,1,0:T(8,128)(2,1)S(1)}, u32[]{:S(2)}, u32[]{:S(2)}) async-start(bf16[48,16,768]{2,1,0:T(8,128)(2,1)} %bitcast.26), calls=%async_computation | async-start | bytes 2359296 | tf_op jit(solution)/shard_map/all_to_all | solution.py:328
  23.0 0.0 copy-done
  23.0 0.0 copy-done.3
  23.0 0.0 copy-start.8
  23.0 1.5 %shard_map.96 = (bf16[64,768]{1,0:T(8,128)(2,1)S(1)}, bf16[64,768]{1,0:T(8,128)(2,1)S(1)}, bf16[64,768]{1,0:T(8,128)(2,1)S(1)}, bf16[64,768]{1,0:T(8,128)(2,1)S(...) custom-call(bf16[1024,768]{1,0:T(8,128)(2,1)S(1)} %copy-done, ...), custom_call_target="tpu_custom_call" | custom-call | flops 805306368 | bytes 2359296 | tf_op jit(solution)/shard_map/pallas_call | solution.py:136
  24.5 0.0 copy-start.4
  24.5 3.5 %collective-permute-start = (bf16[64,768]{1,0:T(8,128)(2,1)S(1)}, bf16[64,768]{1,0:T(8,128)(2,1)S(1)}, u32[]{:S(2)}, u32[]{:S(2)}) collective-permute-start(bf16[64,768]{1,0:T(8,128)(2,1)S(1)} %get-tuple-element.21), channel_id=1, source_target_pairs={{0,96},{48,144},{96,0},{144,48},{192,288},{240,336},{288,192},{336... | collective-permute-start | bytes 294920 | tf_op jit(solution)/shard_map/ppermute | solution.py:334
  28.0 4.5 %collective-permute-start.1 = (bf16[64,768]{1,0:T(8,128)(2,1)S(1)}, bf16[64,768]{1,0:T(8,128)(2,1)S(1)}, u32[]{:S(2)}, u32[]{:S(2)}) collective-permute-start(bf16[64,768]{1,0:T(8,128)(2,1)S(1)} %get-tuple-element.22), channel_id=1, source_target_pairs={{0,192},{48,240},{96,288},{144,336},{192,0},{240,48},{288,96},{336... | collective-permute-start | bytes 294920 | tf_op jit(solution)/shard_map/ppermute | solution.py:334
  32.5 2.1 %collective-permute-start.2 = (bf16[64,768]{1,0:T(8,128)(2,1)S(1)}, bf16[64,768]{1,0:T(8,128)(2,1)S(1)}, u32[]{:S(2)}, u32[]{:S(2)}) collective-permute-start(bf16[64,768]{1,0:T(8,128)(2,1)S(1)} %get-tuple-element.23), channel_id=1, source_target_pairs={{0,288},{48,336},{96,192},{144,240},{192,96},{240,144},{288,0},{33... | collective-permute-start | bytes 294920 | tf_op jit(solution)/shard_map/ppermute | solution.py:334
  34.7 7.7 %collective-permute-start.3 = (bf16[64,768]{1,0:T(8,128)(2,1)S(1)}, bf16[64,768]{1,0:T(8,128)(2,1)S(1)}, u32[]{:S(2)}, u32[]{:S(2)}) collective-permute-start(bf16[64,768]{1,0:T(8,128)(2,1)S(1)} %get-tuple-element.24), channel_id=1, source_target_pairs={{0,384},{48,432},{96,480},{144,528},{192,576},{240,624},{288,672},... | collective-permute-start | bytes 294920 | tf_op jit(solution)/shard_map/ppermute | solution.py:334
  42.4 1.9 %collective-permute-start.4 = (bf16[64,768]{1,0:T(8,128)(2,1)S(1)}, bf16[64,768]{1,0:T(8,128)(2,1)S(1)}, u32[]{:S(2)}, u32[]{:S(2)}) collective-permute-start(bf16[64,768]{1,0:T(8,128)(2,1)S(1)} %get-tuple-element.25), channel_id=1, source_target_pairs={{0,480},{48,528},{96,384},{144,432},{192,672},{240,720},{288,576},... | collective-permute-start | bytes 294920 | tf_op jit(solution)/shard_map/ppermute | solution.py:334
  44.3 0.6 slice_dynamic-update-slice_fusion.7
  45.0 0.0 collective-permute-done.refs_1_
  45.0 5.5 %collective-permute-start.5 = (bf16[64,768]{1,0:T(8,128)(2,1)S(1)}, bf16[64,768]{1,0:T(8,128)(2,1)S(1)}, u32[]{:S(2)}, u32[]{:S(2)}) collective-permute-start(bf16[64,768]{1,0:T(8,128)(2,1)S(1)} %get-tuple-element.26), channel_id=1, source_target_pairs={{0,576},{48,624},{96,672},{144,720},{192,384},{240,432},{288,480},... | collective-permute-start | bytes 294920 | tf_op jit(solution)/shard_map/ppermute | solution.py:334
  50.4 0.6 slice_dynamic-update-slice_fusion.6
  51.0 0.0 collective-permute-done.1.refs_2_
  51.0 1.9 %collective-permute-start.6 = (bf16[64,768]{1,0:T(8,128)(2,1)S(1)}, bf16[64,768]{1,0:T(8,128)(2,1)S(1)}, u32[]{:S(2)}, u32[]{:S(2)}) collective-permute-start(bf16[64,768]{1,0:T(8,128)(2,1)S(1)} %get-tuple-element.27), channel_id=1, source_target_pairs={{0,672},{48,720},{96,576},{144,624},{192,480},{240,528},{288,384},... | collective-permute-start | bytes 294920 | tf_op jit(solution)/shard_map/ppermute | solution.py:334
  53.0 0.6 slice_dynamic-update-slice_fusion.5
  53.6 0.0 collective-permute-done.2.refs_3_
  53.6 0.6 slice_dynamic-update-slice_fusion.4
  54.2 0.0 collective-permute-done.3.refs_4_
  54.2 0.6 slice_dynamic-update-slice_fusion.3
  54.8 0.0 collective-permute-done.4.refs_5_
  54.8 0.6 slice_dynamic-update-slice_fusion.2
  55.5 0.2 collective-permute-done.5.refs_6_
  55.7 0.6 slice_dynamic-update-slice_fusion.1
  56.3 3.5 %collective-permute-done.6.refs_7_ = bf16[64,768]{1,0:T(8,128)(2,1)S(1)} collective-permute-done((bf16[64,768]{1,0:T(8,128)(2,1)S(1)}, bf16[64,768]{1,0:T(8,128)(2,1)S(1)}, u32[]{:S(2)}, u32[]{:S(2)}) %collective-permute-start.6) | collective-permute-done | bytes 98336 | tf_op jit(solution)/shard_map/ppermute | solution.py:334
  59.8 0.6 slice_dynamic-update-slice_fusion
  60.5 0.0 copy-done.1
  60.5 1.9 %collective-permute-start.7 = (bf16[256,768]{1,0:T(8,128)(2,1)}, bf16[256,768]{1,0:T(8,128)(2,1)}, u32[]{:S(2)}, u32[]{:S(2)}) collective-permute-start(bf16[256,768]{1,0:T(8,128)(2,1)} %slice_dynamic-update-slice_fusion), channel_id=1, source_target_pairs={{0,48},{48,0},{96,144},{144,96},{192,240},{240,192},{288,336},{336... | collective-permute-start | bytes 1179656 | tf_op jit(solution)/shard_map/ppermute | solution.py:336
  62.4 0.0 copy-done.8
  62.4 0.1 copy.10.lists_ref
  62.5 0.4 multiply_reduce_fusion
  62.9 0.0 copy-start.5
  62.9 1.5 %collective-permute-done.7.refs_8_ = bf16[256,768]{1,0:T(8,128)(2,1)} collective-permute-done((bf16[256,768]{1,0:T(8,128)(2,1)}, bf16[256,768]{1,0:T(8,128)(2,1)}, u32[]{:S(2)}, u32[]{:S(2)}) %collective-permute-start.7) | collective-permute-done | bytes 393248 | tf_op jit(solution)/shard_map/ppermute | solution.py:336
  64.4 0.0 copy-done.4
  64.4 0.0 copy-done.2
  64.4 3.7 %shard_map.97 = (f32[128,1024]{1,0:T(8,128)S(1)}, bf16[16,32]{1,0:T(8,128)(2,1)S(1)}) custom-call(bf16[64,768]{1,0:T(8,128)(2,1)S(1)} %get-tuple-element.20.refs_0_, bf16[64,768]{1,0:T(8,128)(2,1)S(1)} %collective-permute-done.refs_1_, bf16[64,768]{1,0:T(8,128)(2,1)S(1)} %collective-permute-done.1.refs_2_, ...), custom_call_target="tpu_custom_call" | custom-call | flops 805306368 | bytes 2359296 | tf_op jit(solution)/shard_map/pallas_call | solution.py:343
  68.1 0.0 copy-start.6
  68.2 0.8 copy-done.6
  68.9 0.0 all-to-all-done
  68.9 2.2 %shard_map.98 = bf16[48,1,16]{2,1,0:T(2,128)(2,1)} custom-call(bf16[768,768]{1,0:T(8,128)(2,1)S(1)} %bitcast.9, bf16[1024,768]{1,0:T(8,128)(2,1)S(1)} %copy-done, f32[1,1024]{1,0:T(1,128)S(1)} %bitcast.15, s32[1,48]{1,0:T(1,128)S(1)} %bitcast.21), custom_call_target="tpu_custom_call" | custom-call | flops 1207959552 | bytes 2359296 | tf_op jit(solution)/shard_map/pallas_call | solution.py:360
  71.2 12.5 %all-to-all-start.1 = ((bf16[48,1,16]{2,1,0:T(2,128)(2,1)}), bf16[48,1,16]{2,1,0:T(2,128)(2,1)S(1)}, u32[]{:S(2)}, u32[]{:S(2)}) async-start(bf16[48,1,16]{2,1,0:T(2,128)(2,1)} %shard_map.98), calls=%async_computation.1 | async-start | bytes 49152 | tf_op jit(solution)/shard_map/all_to_all | solution.py:368
  83.7 1.9 %collective-permute-start.8 = (bf16[16,32]{1,0:T(8,128)(2,1)S(1)}, bf16[16,32]{1,0:T(8,128)(2,1)S(1)}, u32[]{:S(2)}, u32[]{:S(2)}) collective-permute-start(bf16[16,32]{1,0:T(8,128)(2,1)S(1)} %get-tuple-element.29), channel_id=1, source_target_pairs={{0,48},{48,0},{96,144},{144,96},{192,240},{240,192},{288,336},{336... | collective-permute-start | bytes 3080 | tf_op jit(solution)/shard_map/ppermute | solution.py:376
  85.6 0.0 copy-start.11
  85.6 1.4 %shard_map.99.refs_5_ = f32[16,256]{1,0:T(8,128)S(1)} custom-call(bf16[768,768]{1,0:T(8,128)(2,1)S(1)} %bitcast.10, bf16[1024,768]{1,0:T(8,128)(2,1)S(1)} %copy-done, f32[1,1024]{1,0:T(1,128)S(1)} %bitcast.16, s32[1,48]{1,0:T(1,128)S(1)} %bitcast.22, f32[128,1024]{1,0:T(8,128)S(1)} %copy-done.7), custom_call_target="tpu_custom_call" | custom-call | flops 1207959552 | bytes 2359296 | tf_op jit(solution)/shard_map/pallas_call | solution.py:379
  87.0 0.0 collective-permute-done.8
  87.1 0.0 copy-start.10
  87.1 3.2 %collective-permute-start.9 = (bf16[16,32]{1,0:T(8,128)(2,1)S(1)}, bf16[16,32]{1,0:T(8,128)(2,1)S(1)}, u32[]{:S(2)}, u32[]{:S(2)}) collective-permute-start(bf16[16,32]{1,0:T(8,128)(2,1)S(1)} %select_n.10), channel_id=1, source_target_pairs={{0,96},{48,144},{96,0},{144,48},{192,288},{240,336},{288,192},{336... | collective-permute-start | bytes 3080 | tf_op jit(solution)/shard_map/ppermute | solution.py:376
  90.3 1.4 %shard_map.100.refs_6_ = f32[16,256]{1,0:T(8,128)S(1)} custom-call(bf16[768,768]{1,0:T(8,128)(2,1)S(1)} %bitcast.11, bf16[1024,768]{1,0:T(8,128)(2,1)S(1)} %copy-done, f32[1,1024]{1,0:T(1,128)S(1)} %bitcast.17, s32[1,48]{1,0:T(1,128)S(1)} %bitcast.23, f32[128,1024]{1,0:T(8,128)S(1)} %copy-done.7), custom_call_target="tpu_custom_call" | custom-call | flops 1207959552 | bytes 2359296 | tf_op jit(solution)/shard_map/pallas_call | solution.py:379
  91.8 0.8 collective-permute-done.9
  92.6 0.0 copy-start.9
  92.6 4.0 %collective-permute-start.10 = (bf16[16,32]{1,0:T(8,128)(2,1)S(1)}, bf16[16,32]{1,0:T(8,128)(2,1)S(1)}, u32[]{:S(2)}, u32[]{:S(2)}) collective-permute-start(bf16[16,32]{1,0:T(8,128)(2,1)S(1)} %select_n.11), channel_id=1, source_target_pairs={{0,192},{48,240},{96,288},{144,336},{192,0},{240,48},{288,96},{336... | collective-permute-start | bytes 3080 | tf_op jit(solution)/shard_map/ppermute | solution.py:376
  96.6 1.4 %shard_map.101.refs_7_ = f32[16,256]{1,0:T(8,128)S(1)} custom-call(bf16[768,768]{1,0:T(8,128)(2,1)S(1)} %bitcast.12, bf16[1024,768]{1,0:T(8,128)(2,1)S(1)} %copy-done, f32[1,1024]{1,0:T(1,128)S(1)} %bitcast.18, s32[1,48]{1,0:T(1,128)S(1)} %bitcast.24, f32[128,1024]{1,0:T(8,128)S(1)} %copy-done.7), custom_call_target="tpu_custom_call" | custom-call | flops 1207959552 | bytes 2359296 | tf_op jit(solution)/shard_map/pallas_call | solution.py:379
  98.1 0.9 collective-permute-done.10
  99.0 5.2 %collective-permute-start.11 = (bf16[16,32]{1,0:T(8,128)(2,1)S(1)}, bf16[16,32]{1,0:T(8,128)(2,1)S(1)}, u32[]{:S(2)}, u32[]{:S(2)}) collective-permute-start(bf16[16,32]{1,0:T(8,128)(2,1)S(1)} %select_n.12.kept_ref), channel_id=1, source_target_pairs={{0,384},{48,432},{96,480},{144,528},{192,576},{240,624},{288,672},... | collective-permute-start | bytes 3080 | tf_op jit(solution)/shard_map/ppermute | solution.py:376
  104.2 2.1 %shard_map.102 = f32[16,1024]{1,0:T(8,128)} custom-call(bf16[768,768]{1,0:T(8,128)(2,1)S(1)} %bitcast.13, bf16[1024,768]{1,0:T(8,128)(2,1)S(1)} %copy-done, f32[1,1024]{1,0:T(1,128)S(1)} %bitcast.19, s32[1,48]{1,0:T(1,128)S(1)} %bitcast.25, f32[128,1024]{1,0:T(8,128)S(1)} %copy-done.7, f32[16,256]{1,0:T(8,128)S(1)} %shard_map.99.refs_5_, ...), custom_call_target="tpu_custom_call" | custom-call | flops 1207959552 | bytes 2359296 | tf_op jit(solution)/shard_map/pallas_call | solution.py:379
  106.3 2.1 %collective-permute-done.11.came_ref = bf16[16,32]{1,0:T(8,128)(2,1)S(1)} collective-permute-done((bf16[16,32]{1,0:T(8,128)(2,1)S(1)}, bf16[16,32]{1,0:T(8,128)(2,1)S(1)}, u32[]{:S(2)}, u32[]{:S(2)}) %collective-permute-start.11) | collective-permute-done | bytes 1056 | tf_op jit(solution)/shard_map/ppermute | solution.py:376
  108.4 0.5 shard_map.103.best_ref
  108.9 0.0 all-to-all-done.1.back_ref
  109.0 1.7 %shard_map.104 = f32[8,128]{1,0:T(8,128)} custom-call(s32[48,16]{1,0:T(8,128)S(1)} %copy.10.lists_ref, bf16[48,1,16]{2,1,0:T(2,128)(2,1)S(1)} %all-to-all-done.1.back_ref, f32[8,1024]{1,0:T(8,128)S(1)} %shard_map.103.best_ref), custom_call_target="tpu_custom_call" | custom-call | tf_op jit(solution)/shard_map/pallas_call | solution.py:400
  (11 shorter events, 0.0 us)
Async XLA Ops:
  4.3 18.7 %copy-start = (bf16[1024,768]{1,0:T(8,128)(2,1)S(1)}, bf16[1024,768]{1,0:T(8,128)(2,1)}, u32[]{:S(2)}) copy-start(bf16[1024,768]{1,0:T(8,128)(2,1)} %refs_1_.7) | copy-start | bytes 4718596
  4.3 18.7 %copy-start.3 = (s32[16,32]{1,0:T(8,128)S(1)}, s32[16,32]{1,0:T(8,128)}, u32[]{:S(2)}) copy-start(s32[16,32]{1,0:T(8,128)} %lists_ref.4) | copy-start | bytes 6148
  4.3 64.6 %all-to-all-start = ((bf16[48,16,768]{2,1,0:T(8,128)(2,1)}), bf16[48,16,768]{2,1,0:T(8,128)(2,1)S(1)}, u32[]{:S(2)}, u32[]{:S(2)}) async-start(bf16[48,16,768]{2,1,0:T(8,128)(2,1)} %bitcast.26), calls=%async_computation | async-start | bytes 2359296 | tf_op jit(solution)/shard_map/all_to_all | solution.py:328
  23.0 39.4 %copy-start.8 = (s32[48,16]{0,1:T(8,128)S(1)}, s32[48,16]{0,1:T(8,128)}, u32[]{:S(2)}) copy-start(s32[48,16]{0,1:T(8,128)} %param.9) | copy-start | bytes 9220
  24.5 39.9 %copy-start.4 = (s32[16,1]{0,1:T(1,128)S(1)}, s32[16,1]{0,1:T(1,128)}, u32[]{:S(2)}) copy-start(s32[16,1]{0,1:T(1,128)} %param.12) | copy-start | bytes 196
  24.5 20.4 %collective-permute-start = (bf16[64,768]{1,0:T(8,128)(2,1)S(1)}, bf16[64,768]{1,0:T(8,128)(2,1)S(1)}, u32[]{:S(2)}, u32[]{:S(2)}) collective-permute-start(bf16[64,768]{1,0:T(8,128)(2,1)S(1)} %get-tuple-element.21), channel_id=1, source_target_pairs={{0,96},{48,144},{96,0},{144,48},{192,288},{240,336},{288,192},{336... | collective-permute-start | bytes 294920 | tf_op jit(solution)/shard_map/ppermute | solution.py:334
  28.0 23.0 %collective-permute-start.1 = (bf16[64,768]{1,0:T(8,128)(2,1)S(1)}, bf16[64,768]{1,0:T(8,128)(2,1)S(1)}, u32[]{:S(2)}, u32[]{:S(2)}) collective-permute-start(bf16[64,768]{1,0:T(8,128)(2,1)S(1)} %get-tuple-element.22), channel_id=1, source_target_pairs={{0,192},{48,240},{96,288},{144,336},{192,0},{240,48},{288,96},{336... | collective-permute-start | bytes 294920 | tf_op jit(solution)/shard_map/ppermute | solution.py:334
  32.5 21.1 %collective-permute-start.2 = (bf16[64,768]{1,0:T(8,128)(2,1)S(1)}, bf16[64,768]{1,0:T(8,128)(2,1)S(1)}, u32[]{:S(2)}, u32[]{:S(2)}) collective-permute-start(bf16[64,768]{1,0:T(8,128)(2,1)S(1)} %get-tuple-element.23), channel_id=1, source_target_pairs={{0,288},{48,336},{96,192},{144,240},{192,96},{240,144},{288,0},{33... | collective-permute-start | bytes 294920 | tf_op jit(solution)/shard_map/ppermute | solution.py:334
  34.7 19.6 %collective-permute-start.3 = (bf16[64,768]{1,0:T(8,128)(2,1)S(1)}, bf16[64,768]{1,0:T(8,128)(2,1)S(1)}, u32[]{:S(2)}, u32[]{:S(2)}) collective-permute-start(bf16[64,768]{1,0:T(8,128)(2,1)S(1)} %get-tuple-element.24), channel_id=1, source_target_pairs={{0,384},{48,432},{96,480},{144,528},{192,576},{240,624},{288,672},... | collective-permute-start | bytes 294920 | tf_op jit(solution)/shard_map/ppermute | solution.py:334
  42.4 12.4 %collective-permute-start.4 = (bf16[64,768]{1,0:T(8,128)(2,1)S(1)}, bf16[64,768]{1,0:T(8,128)(2,1)S(1)}, u32[]{:S(2)}, u32[]{:S(2)}) collective-permute-start(bf16[64,768]{1,0:T(8,128)(2,1)S(1)} %get-tuple-element.25), channel_id=1, source_target_pairs={{0,480},{48,528},{96,384},{144,432},{192,672},{240,720},{288,576},... | collective-permute-start | bytes 294920 | tf_op jit(solution)/shard_map/ppermute | solution.py:334
  45.0 10.7 %collective-permute-start.5 = (bf16[64,768]{1,0:T(8,128)(2,1)S(1)}, bf16[64,768]{1,0:T(8,128)(2,1)S(1)}, u32[]{:S(2)}, u32[]{:S(2)}) collective-permute-start(bf16[64,768]{1,0:T(8,128)(2,1)S(1)} %get-tuple-element.26), channel_id=1, source_target_pairs={{0,576},{48,624},{96,672},{144,720},{192,384},{240,432},{288,480},... | collective-permute-start | bytes 294920 | tf_op jit(solution)/shard_map/ppermute | solution.py:334
  51.0 8.8 %collective-permute-start.6 = (bf16[64,768]{1,0:T(8,128)(2,1)S(1)}, bf16[64,768]{1,0:T(8,128)(2,1)S(1)}, u32[]{:S(2)}, u32[]{:S(2)}) collective-permute-start(bf16[64,768]{1,0:T(8,128)(2,1)S(1)} %get-tuple-element.27), channel_id=1, source_target_pairs={{0,672},{48,720},{96,576},{144,624},{192,480},{240,528},{288,384},... | collective-permute-start | bytes 294920 | tf_op jit(solution)/shard_map/ppermute | solution.py:334
  59.8 0.7 copy-start.1
  60.5 3.9 %collective-permute-start.7 = (bf16[256,768]{1,0:T(8,128)(2,1)}, bf16[256,768]{1,0:T(8,128)(2,1)}, u32[]{:S(2)}, u32[]{:S(2)}) collective-permute-start(bf16[256,768]{1,0:T(8,128)(2,1)} %slice_dynamic-update-slice_fusion), channel_id=1, source_target_pairs={{0,48},{48,0},{96,144},{144,96},{192,240},{240,192},{288,336},{336... | collective-permute-start | bytes 1179656 | tf_op jit(solution)/shard_map/ppermute | solution.py:336
  62.5 1.9 %copy-start.2 = (bf16[64,768]{1,0:T(8,128)(2,1)S(1)}, bf16[64,768]{1,0:T(8,128)(2,1)}, u32[]{:S(2)}) copy-start(bf16[64,768]{1,0:T(8,128)(2,1)} %copy-done.1) | copy-start | bytes 294916
  62.9 6.1 %copy-start.5 = (s32[48,1]{0,1:T(1,128)S(1)}, s32[48,1]{0,1:T(1,128)}, u32[]{:S(2)}) copy-start(s32[48,1]{0,1:T(1,128)} %param.11) | copy-start | bytes 580
  68.1 0.8 copy-start.6
  68.9 16.7 %copy-start.7 = (f32[128,1024]{1,0:T(8,128)S(1)}, f32[128,1024]{1,0:T(8,128)}, u32[]{:S(2)}) copy-start(f32[128,1024]{1,0:T(8,128)} %copy-done.6) | copy-start | bytes 1572868
  71.2 37.8 %all-to-all-start.1 = ((bf16[48,1,16]{2,1,0:T(2,128)(2,1)}), bf16[48,1,16]{2,1,0:T(2,128)(2,1)S(1)}, u32[]{:S(2)}, u32[]{:S(2)}) async-start(bf16[48,1,16]{2,1,0:T(2,128)(2,1)} %shard_map.98), calls=%async_computation.1 | async-start | bytes 49152 | tf_op jit(solution)/shard_map/all_to_all | solution.py:368
  83.7 3.4 %collective-permute-start.8 = (bf16[16,32]{1,0:T(8,128)(2,1)S(1)}, bf16[16,32]{1,0:T(8,128)(2,1)S(1)}, u32[]{:S(2)}, u32[]{:S(2)}) collective-permute-start(bf16[16,32]{1,0:T(8,128)(2,1)S(1)} %get-tuple-element.29), channel_id=1, source_target_pairs={{0,48},{48,0},{96,144},{144,96},{192,240},{240,192},{288,336},{336... | collective-permute-start | bytes 3080 | tf_op jit(solution)/shard_map/ppermute | solution.py:376
  85.6 1.5 %copy-start.11 = (pred[16,32]{1,0:T(8,128)(4,1)S(1)}, pred[16,32]{1,0:T(8,128)(4,1)}, u32[]{:S(2)}) copy-start(pred[16,32]{1,0:T(8,128)(4,1)} %constant.13.clone) | copy-start | bytes 1540
  87.1 5.5 %copy-start.10 = (pred[16,32]{1,0:T(8,128)(4,1)S(1)}, pred[16,32]{1,0:T(8,128)(4,1)}, u32[]{:S(2)}) copy-start(pred[16,32]{1,0:T(8,128)(4,1)} %constant.14.clone) | copy-start | bytes 1540
  87.1 5.5 %collective-permute-start.9 = (bf16[16,32]{1,0:T(8,128)(2,1)S(1)}, bf16[16,32]{1,0:T(8,128)(2,1)S(1)}, u32[]{:S(2)}, u32[]{:S(2)}) collective-permute-start(bf16[16,32]{1,0:T(8,128)(2,1)S(1)} %select_n.10), channel_id=1, source_target_pairs={{0,96},{48,144},{96,0},{144,48},{192,288},{240,336},{288,192},{336... | collective-permute-start | bytes 3080 | tf_op jit(solution)/shard_map/ppermute | solution.py:376
  92.6 6.4 %copy-start.9 = (pred[16,32]{1,0:T(8,128)(4,1)S(1)}, pred[16,32]{1,0:T(8,128)(4,1)}, u32[]{:S(2)}) copy-start(pred[16,32]{1,0:T(8,128)(4,1)} %constant.15.clone) | copy-start | bytes 1540
  92.6 6.4 %collective-permute-start.10 = (bf16[16,32]{1,0:T(8,128)(2,1)S(1)}, bf16[16,32]{1,0:T(8,128)(2,1)S(1)}, u32[]{:S(2)}, u32[]{:S(2)}) collective-permute-start(bf16[16,32]{1,0:T(8,128)(2,1)S(1)} %select_n.11), channel_id=1, source_target_pairs={{0,192},{48,240},{96,288},{144,336},{192,0},{240,48},{288,96},{336... | collective-permute-start | bytes 3080 | tf_op jit(solution)/shard_map/ppermute | solution.py:376
  99.0 9.4 %collective-permute-start.11 = (bf16[16,32]{1,0:T(8,128)(2,1)S(1)}, bf16[16,32]{1,0:T(8,128)(2,1)S(1)}, u32[]{:S(2)}, u32[]{:S(2)}) collective-permute-start(bf16[16,32]{1,0:T(8,128)(2,1)S(1)} %select_n.12.kept_ref), channel_id=1, source_target_pairs={{0,384},{48,432},{96,480},{144,528},{192,576},{240,624},{288,672},... | collective-permute-start | bytes 3080 | tf_op jit(solution)/shard_map/ppermute | solution.py:376

commit v5 on v3

--- a/solution.py
+++ b/solution.py
@@ -202,55 +202,79 @@
     return [jnp.sum(spread[at : at + slots, :], axis=0, keepdims=True) for at in range(0, chunk, slots)]
 
 
-def near_kernel(groups, slots, *refs):
+def halves_kernel(slots, *refs):
+    pieces, (mine_ref, handed_ref) = refs[:-2], refs[-2:]
+    for k, piece in enumerate(pieces):
+        mine_ref[k * slots : (k + 1) * slots, :] = piece[:slots, :]
+        handed_ref[k * slots : (k + 1) * slots, :] = piece[slots:, :]
+
+
+def near_kernel(
+    groups, slots, even_ref, odd_ref, points_ref, own_sq_ref, counts_ref, place_ref,
+    held_ref, minima_ref, dist_ref, held, sems,
+):
     count = groups // 2
-    evens, (odd_ref, points_ref, own_sq_ref, counts_ref, place_ref) = refs[:count], refs[count : count + 5]
-    held_ref, minima_ref, dist_ref = refs[count + 5 :]
+    half = count * slots
 
     def order(block):
         return jnp.where(block < count, 2 * block, 2 * (block - count) + 1) ^ place_ref[0]
 
-    half = count * slots
-    even = jnp.concatenate([ref[:slots, :] for ref in evens], axis=0)
-    minima_ref[...] = jnp.zeros_like(minima_ref)
-    for start, cand in ((0, even), (half, odd_ref[...])):
+    for start, cand_ref in ((0, even_ref), (half, odd_ref)):
         usable = usable_slots(counts_ref, start, half, groups, slots, order)
-        dist = distances(cand, points_ref, own_sq_ref)
+        dist = distances(cand_ref[...], points_ref, own_sq_ref)
         dist_ref[start : start + half, :] = jnp.where(usable, dist, far_value)
         minima = jnp.where(usable, jnp.min(dist, axis=1, keepdims=True), cap_value)
-        for k, row in enumerate(slot_rows(minima.astype(jnp.bfloat16).astype(jnp.float32), slots)):
-            source = order(start // slots + k)
-            minima_ref[pl.ds(source * groups + place_ref[0], 1), :] = row
+        for k, row in enumerate(slot_rows(minima, slots)):
+            minima_ref[order(start // slots + k)] = row.astype(jnp.bfloat16)
 
     def block(t, _):
         lanes = pl.ds(pl.multiple_of(t * LANES, LANES), LANES)
         for k, value in enumerate(smallest16(dist_ref, lanes, None)):
-            held_ref[SUBLANES * k : SUBLANES * (k + 1), lanes] = value
+            held[SUBLANES * k : SUBLANES * (k + 1), lanes] = value
         return 0
 
-    lax.fori_loop(0, dist_ref.shape[1] // LANES, block, 0)
+    blocks = dist_ref.shape[1] // LANES
+    copies = []
+    for part in range(2):
+        first, last = part * blocks // 2, (part + 1) * blocks // 2
+        lax.fori_loop(first, last, block, 0)
+        lanes = pl.ds(first * LANES, (last - first) * LANES)
+        copies.append(pltpu.make_async_copy(held.at[:, lanes], held_ref.at[:, lanes], sems.at[part]))
+        copies[-1].start()
+    for copy in copies:
+        copy.wait()
 
 
 def minima_kernel(peers, slots, cand_ref, points_ref, own_sq_ref, counts_ref, minima_ref):
     total, rows = peers * slots, points_ref.shape[0]
     cand = cand_ref[...]
+    wide = cand.astype(jnp.float32)
+    cand_sq = jnp.sum(wide * wide, axis=1, keepdims=True)
     least = None
     for start in range(0, rows, 256):
-        part = slice(start, start + 256)
-        dist = distances(cand, points_ref.at[part, :], own_sq_ref.at[:, part])
-        dist = jnp.minimum(dist[:, :LANES], dist[:, LANES:])
-        least = dist if least is None else jnp.minimum(least, dist)
+        inner = lax.dot_general(
+            cand, points_ref[start : start + 256, :], (((1,), (1,)), ((), ())), preferred_element_type=jnp.float32
+        )
+        for at in range(0, 256, LANES):
+            own = own_sq_ref[:, start + at : start + at + LANES]
+            dist = cand_sq + own - 2.0 * inner[:, at : at + LANES]
+            least = dist if least is None else jnp.minimum(least, dist)
     usable = usable_slots(counts_ref, 0, total, peers, slots, straight)
     minima = jnp.where(usable, jnp.min(least, axis=1, keepdims=True), cap_value)
     for k, row in enumerate(slot_rows(minima, slots)):
         minima_ref[k] = row.astype(jnp.bfloat16)
 
 
-def select_kernel(peers, slots, chunk, cand_ref, points_ref, own_sq_ref, counts_ref, held_ref, out_ref, dist_ref):
+def select_kernel(
+    peers, slots, chunk, cand_ref, points_ref, own_sq_ref, counts_ref, held_hbm_ref, out_ref, dist_ref, held_ref, sem
+):
+    fetch = pltpu.make_async_copy(held_hbm_ref, held_ref, sem)
+    fetch.start()
     for start in range(0, peers * slots, chunk):
         usable = usable_slots(counts_ref, start, chunk, peers, slots, straight)
         dist = distances(cand_ref[start : start + chunk, :], points_ref, own_sq_ref)
         dist_ref[start : start + chunk, :] = jnp.where(usable, dist, far_value)
+    fetch.wait()
     sublane = iota((SUBLANES, LANES), 0)
 
     def block(t, _):
@@ -278,13 +302,11 @@
     return best
 
 
-def reverse_old_kernel(lists_ref, back_ref, best_ref):
-    best_ref[...] = fold(jnp.full(best_ref.shape, cap_value, jnp.float32), lists_ref[...], back_ref[...])
-
-
-def reverse_new_kernel(lists_ref, back_ref, best_ref, out_ref):
-    back = back_ref[...].reshape(lists_ref.shape).astype(jnp.float32)
-    best = jnp.min(fold(best_ref[...], lists_ref[...], back), axis=0, keepdims=True)
+def reverse_kernel(new_lists_ref, old_lists_ref, new_back_ref, old_back_ref, out_ref):
+    best = jnp.full((SUBLANES, SUBLANES * LANES), cap_value, jnp.float32)
+    for lists_ref, back_ref in ((old_lists_ref, old_back_ref), (new_lists_ref, new_back_ref)):
+        best = fold(best, lists_ref[...], back_ref[...].reshape(lists_ref.shape).astype(jnp.float32))
+    best = jnp.min(best, axis=0, keepdims=True)
     for k in range(SUBLANES):
         out_ref[k : k + 1, :] = best[:, LANES * k : LANES * (k + 1)]
 
@@ -310,30 +332,42 @@
     ).reshape(peers * slots, features)
 
     pieces = gather_old(points, serve_old, place, groups, group_slots, groups // 2)
-    evens = [pieces[0]] + [
-        lax.ppermute(pieces[k], "grp", apart(groups, 2 * k)) for k in range(1, groups // 2)
-    ]
-    odds = lax.ppermute(
-        jnp.concatenate([piece[group_slots:] for piece in evens], axis=0), "grp", apart(groups, 1)
-    )
+    came = {0: pieces[0]}
+    for k in sorted(range(1, groups // 2), key=lambda k: min(k, groups // 2 - k), reverse=True):
+        came[k] = lax.ppermute(pieces[k], "grp", apart(groups, 2 * k))
+    evens = [came[k] for k in range(groups // 2)]
+    half = groups // 2 * group_slots
+    evens, handed = pl.pallas_call(
+        functools.partial(halves_kernel, group_slots),
+        out_shape=(jax.ShapeDtypeStruct((half, features), jnp.bfloat16),) * 2,
+        compiler_params=params,
+        cost_estimate=pl.CostEstimate(flops=0, bytes_accessed=8 * half * features, transcendentals=0),
+    )(*evens)
+    odds = lax.ppermute(handed, "grp", apart(groups, 1))
 
     own_sq = jnp.sum(jnp.square(points.astype(jnp.float32)), axis=1)[None, :]
 
     total_old = groups * group_slots
     held, minima_old = pl.pallas_call(
         functools.partial(near_kernel, groups, group_slots),
-        in_specs=[vmem] * (groups // 2 + 4) + [smem],
+        in_specs=[vmem] * 5 + [smem],
+        out_specs=(pl.BlockSpec(memory_space=pltpu.HBM), vmem),
         out_shape=(
             pltpu.HBM((16 * SUBLANES, rows), jnp.float32),
-            jax.ShapeDtypeStruct((groups * groups, group_slots), jnp.float32),
-        ),
-        scratch_shapes=[pltpu.VMEM((total_old, rows), jnp.float32)],
+            jax.ShapeDtypeStruct((groups, 1, group_slots), jnp.bfloat16),
+        ),
+        scratch_shapes=[
+            pltpu.VMEM((total_old, rows), jnp.float32),
+            pltpu.VMEM((16 * SUBLANES, rows), jnp.float32),
+            pltpu.SemaphoreType.DMA((2,)),
+        ],
         compiler_params=params,
         cost_estimate=pl.CostEstimate(
             flops=2 * total_old * rows * features, bytes_accessed=2 * (total_old + rows) * features, transcendentals=0
         ),
-    )(*evens, odds, points, own_sq, counts_old, place)
-    back_old = lax.psum_scatter(minima_old, "grp", scatter_dimension=0, tiled=True)
+    )(evens, odds, points, own_sq, counts_old, place)
+    pulled_new, minima_old = lax.optimization_barrier((pulled_new, minima_old))
+    back_old = lax.all_to_all(minima_old, "grp", split_axis=0, concat_axis=0, tiled=True)
 
     total_new = peers * slots
     minima_new = pl.pallas_call(
@@ -349,25 +383,24 @@
     pulled_new, _ = lax.optimization_barrier((pulled_new, minima_new))
     nearest = pl.pallas_call(
         functools.partial(select_kernel, peers, slots, 256),
+        in_specs=[vmem] * 4 + [pl.BlockSpec(memory_space=pltpu.HBM)],
         out_shape=jax.ShapeDtypeStruct((NEAR, rows), jnp.float32),
-        scratch_shapes=[pltpu.VMEM((total_new, rows), jnp.float32)],
+        scratch_shapes=[
+            pltpu.VMEM((total_new, rows), jnp.float32),
+            pltpu.VMEM((16 * SUBLANES, rows), jnp.float32),
+            pltpu.SemaphoreType.DMA,
+        ],
         compiler_params=params,
         cost_estimate=pl.CostEstimate(
             flops=4 * total_new * rows * features, bytes_accessed=4 * total_new * features, transcendentals=0
         ),
-    )(pulled_new, points, own_sq, counts_new, held)
-
-    nearest, back_old = lax.optimization_barrier((nearest, back_old))
-    best = pl.pallas_call(
-        reverse_old_kernel,
-        out_shape=jax.ShapeDtypeStruct((SUBLANES, rows), jnp.float32),
-        compiler_params=params,
-    )(serve_old, back_old)
+    )(pulled_new, points, own_sq, counts_new, pltpu.with_memory_space_constraint(held, pltpu.HBM))
+
     reverse = pl.pallas_call(
-        reverse_new_kernel,
+        reverse_kernel,
         out_shape=jax.ShapeDtypeStruct((SUBLANES, LANES), jnp.float32),
         compiler_params=params,
-    )(serve_new, back_new, best)
+    )(serve_new, serve_old, back_new, back_old)
     return nearest.T, reverse.reshape(rows)
 
 

time: 145 us -> 109 us (0.75)
  waiting for transfers between devices: 43.8 us -> 20.9 us
  between operations: 14.3 us -> 0.87 us
  local copies, waits for them, and re-layouts: 5.8 us -> 0.11 us
  starting transfers between devices: 60.9 us -> 65.1 us
  Pallas kernels: 19.1 us -> 21.1 us
    reduce_scatter x1 -> x0, waiting for transfers between devices: 38.6 us -> none  [body(): lax.psum_scatter(minima_old, 'grp', scatter_dimension=0, tiled=True)]
    all_to_all x0 -> x1, starting transfers between devices: none -> 5.81 us  [body(): lax.all_to_all(minima_old, 'grp', split_axis=0, concat_axis=0, tiled=True)]
    all_to_all x1, waiting for transfers between devices: 0.01 us -> 5.71 us  [body(): lax.all_to_all(minima_new, 'shard', split_axis=0, concat_axis=0, tiled=True)]
    ppermute x8, waiting for transfers between devices: 5.25 us -> 10.5 us  [the longest x7 9.33 us: body(): came[k] = lax.ppermute(pieces[k], 'grp', apart(groups, 2 * k))]
    unnamed x26 -> x11, local copies, waits for them, and re-layouts: 5.14 us -> 0.11 us
    all_to_all x0 -> x1, waiting for transfers between devices: none -> 4.66 us  [body(): lax.all_to_all(minima_old, 'grp', split_axis=0, concat_axis=0, tiled=True)]
    pallas_call x3, Pallas kernels: 7.12 us -> 8.58 us  [the longest x1 5.21 us: body(): pl.pallas_call(functools.partial(select_kernel, peers, slots, 256), in_sp...]
  transfers between devices with their start and end apart: 11 -> 11, of which waited for: 3 -> 5; matrix products, arithmetic and copies ran while one was open for 4% -> 0% of each run, Pallas kernels for 9% -> 14%
where the time goes in v5:
time: 109 us; the launch traced here: 108 us
  starting transfers between devices  65.1 us (60%)
  Pallas kernels  21.1 us (19%)
  waiting for transfers between devices  20.9 us (19%)
    ppermute x7, starting transfers between devices, body(): came[k] = lax.ppermute(pieces[k], 'grp', apart(groups, 2 * k))  25.5 us
    all_to_all x1, starting transfers between devices, body(): lax.all_to_all(offered_new.reshape(peers, slots, features), 'shard', spli...  19 us
    all_to_all x1, starting transfers between devices, body(): lax.all_to_all(minima_new, 'shard', split_axis=0, concat_axis=0, tiled=True)  11.4 us
    ppermute x7, waiting for transfers between devices, body(): came[k] = lax.ppermute(pieces[k], 'grp', apart(groups, 2 * k))  9.33 us
    all_to_all x1, starting transfers between devices, body(): lax.all_to_all(minima_old, 'grp', split_axis=0, concat_axis=0, tiled=True)  5.81 us
    all_to_all x1, waiting for transfers between devices, body(): lax.all_to_all(minima_new, 'shard', split_axis=0, concat_axis=0, tiled=True)  5.71 us
    pallas_call x1, Pallas kernels, body(): pl.pallas_call(functools.partial(select_kernel, peers, slots, 256), in_sp...  5.21 us
    pallas_call x1, Pallas kernels, body(): pl.pallas_call(functools.partial(near_kernel, groups, group_slots), in_sp...  5.12 us
  transfers between devices with their start and end apart: 11, of which 5 were waited for; matrix products, arithmetic and copies ran while one was open for 0% of the time, Pallas kernels for 14%

profile of v5, /device:TPU:1, one launch (start us, length us, event | category | flops | bytes accessed | tf_op | source)
XLA Modules:
  0.0 108.4 jit_solution(3098580436280366936)
XLA Ops:
  0.6 3.7 %shard_map.68 = bf16[768,768]{1,0:T(8,128)(2,1)} custom-call(bf16[1024,768]{1,0:T(8,128)(2,1)} %points_ref.9, s32[16,48]{1,0:T(8,128)} %bitcast.18), custom_call_target="tpu_custom_call" | custom-call | flops 1207959552 | bytes 2752512 | tf_op jit(solution)/shard_map/pallas_call | solution.py:101
  4.3 0.0 copy-start
  4.3 0.0 copy-start.1
  4.3 19.0 %all-to-all-start = ((bf16[48,16,768]{2,1,0:T(8,128)(2,1)}), bf16[48,16,768]{2,1,0:T(8,128)(2,1)S(1)}, u32[]{:S(2)}, u32[]{:S(2)}) async-start(bf16[48,16,768]{2,1,0:T(8,128)(2,1)} %bitcast.17), calls=%async_computation | async-start | bytes 2359296 | tf_op jit(solution)/shard_map/all_to_all | solution.py:330
  23.3 0.0 copy-done
  23.3 0.0 copy-done.1
  23.3 0.0 copy-start.4
  23.3 1.5 %shard_map.69 = (bf16[64,768]{1,0:T(8,128)(2,1)S(1)}, bf16[64,768]{1,0:T(8,128)(2,1)S(1)}, bf16[64,768]{1,0:T(8,128)(2,1)S(1)}, bf16[64,768]{1,0:T(8,128)(2,1)S(...) custom-call(bf16[1024,768]{1,0:T(8,128)(2,1)S(1)} %copy-done, ...), custom_call_target="tpu_custom_call" | custom-call | flops 805306368 | bytes 2359296 | tf_op jit(solution)/shard_map/pallas_call | solution.py:135
  24.8 0.0 copy-start.2
  24.9 3.2 %collective-permute-start = (bf16[64,768]{1,0:T(8,128)(2,1)S(1)}, bf16[64,768]{1,0:T(8,128)(2,1)S(1)}, u32[]{:S(2)}, u32[]{:S(2)}) collective-permute-start(bf16[64,768]{1,0:T(8,128)(2,1)S(1)} %get-tuple-element.18), channel_id=1, source_target_pairs={{0,96},{48,144},{96,0},{144,48},{192,288},{240,336},{288,192},{336... | collective-permute-start | bytes 294920 | tf_op jit(solution)/shard_map/ppermute | solution.py:337
  28.1 4.2 %collective-permute-start.1 = (bf16[64,768]{1,0:T(8,128)(2,1)S(1)}, bf16[64,768]{1,0:T(8,128)(2,1)S(1)}, u32[]{:S(2)}, u32[]{:S(2)}) collective-permute-start(bf16[64,768]{1,0:T(8,128)(2,1)S(1)} %get-tuple-element.19), channel_id=1, source_target_pairs={{0,192},{48,240},{96,288},{144,336},{192,0},{240,48},{288,96},{336... | collective-permute-start | bytes 294920 | tf_op jit(solution)/shard_map/ppermute | solution.py:337
  32.3 1.9 %collective-permute-start.2 = (bf16[64,768]{1,0:T(8,128)(2,1)S(1)}, bf16[64,768]{1,0:T(8,128)(2,1)S(1)}, u32[]{:S(2)}, u32[]{:S(2)}) collective-permute-start(bf16[64,768]{1,0:T(8,128)(2,1)S(1)} %get-tuple-element.20), channel_id=1, source_target_pairs={{0,288},{48,336},{96,192},{144,240},{192,96},{240,144},{288,0},{33... | collective-permute-start | bytes 294920 | tf_op jit(solution)/shard_map/ppermute | solution.py:337
  34.2 7.4 %collective-permute-start.3 = (bf16[64,768]{1,0:T(8,128)(2,1)S(1)}, bf16[64,768]{1,0:T(8,128)(2,1)S(1)}, u32[]{:S(2)}, u32[]{:S(2)}) collective-permute-start(bf16[64,768]{1,0:T(8,128)(2,1)S(1)} %get-tuple-element.21), channel_id=1, source_target_pairs={{0,384},{48,432},{96,480},{144,528},{192,576},{240,624},{288,672},... | collective-permute-start | bytes 294920 | tf_op jit(solution)/shard_map/ppermute | solution.py:337
  41.6 1.9 %collective-permute-start.4 = (bf16[64,768]{1,0:T(8,128)(2,1)S(1)}, bf16[64,768]{1,0:T(8,128)(2,1)S(1)}, u32[]{:S(2)}, u32[]{:S(2)}) collective-permute-start(bf16[64,768]{1,0:T(8,128)(2,1)S(1)} %get-tuple-element.22), channel_id=1, source_target_pairs={{0,480},{48,528},{96,384},{144,432},{192,672},{240,720},{288,576},... | collective-permute-start | bytes 294920 | tf_op jit(solution)/shard_map/ppermute | solution.py:337
  43.5 0.0 collective-permute-done.refs_1_
  43.6 4.9 %collective-permute-start.5 = (bf16[64,768]{1,0:T(8,128)(2,1)S(1)}, bf16[64,768]{1,0:T(8,128)(2,1)S(1)}, u32[]{:S(2)}, u32[]{:S(2)}) collective-permute-start(bf16[64,768]{1,0:T(8,128)(2,1)S(1)} %get-tuple-element.23), channel_id=1, source_target_pairs={{0,576},{48,624},{96,672},{144,720},{192,384},{240,432},{288,480},... | collective-permute-start | bytes 294920 | tf_op jit(solution)/shard_map/ppermute | solution.py:337
  48.5 0.0 collective-permute-done.1.refs_2_
  48.5 1.9 %collective-permute-start.6 = (bf16[64,768]{1,0:T(8,128)(2,1)S(1)}, bf16[64,768]{1,0:T(8,128)(2,1)S(1)}, u32[]{:S(2)}, u32[]{:S(2)}) collective-permute-start(bf16[64,768]{1,0:T(8,128)(2,1)S(1)} %get-tuple-element.24), channel_id=1, source_target_pairs={{0,672},{48,720},{96,576},{144,624},{192,480},{240,528},{288,384},... | collective-permute-start | bytes 294920 | tf_op jit(solution)/shard_map/ppermute | solution.py:337
  50.4 0.0 collective-permute-done.2.refs_3_
  50.4 0.0 collective-permute-done.3.refs_4_
  50.4 0.0 collective-permute-done.4.refs_5_
  50.4 3.8 %collective-permute-done.5.refs_6_ = bf16[64,768]{1,0:T(8,128)(2,1)S(1)} collective-permute-done((bf16[64,768]{1,0:T(8,128)(2,1)S(1)}, bf16[64,768]{1,0:T(8,128)(2,1)S(1)}, u32[]{:S(2)}, u32[]{:S(2)}) %collective-permute-start.5) | collective-permute-done | bytes 98336 | tf_op jit(solution)/shard_map/ppermute | solution.py:337
  54.2 5.5 %collective-permute-done.6.refs_7_ = bf16[64,768]{1,0:T(8,128)(2,1)S(1)} collective-permute-done((bf16[64,768]{1,0:T(8,128)(2,1)S(1)}, bf16[64,768]{1,0:T(8,128)(2,1)S(1)}, u32[]{:S(2)}, u32[]{:S(2)}) %collective-permute-start.6) | collective-permute-done | bytes 98336 | tf_op jit(solution)/shard_map/ppermute | solution.py:337
  59.8 0.8 shard_map.70
  60.6 3.3 %collective-permute-start.7 = (bf16[256,768]{1,0:T(8,128)(2,1)}, bf16[256,768]{1,0:T(8,128)(2,1)}, u32[]{:S(2)}, u32[]{:S(2)}) collective-permute-start(bf16[256,768]{1,0:T(8,128)(2,1)} %get-tuple-element.26), channel_id=1, source_target_pairs={{0,48},{48,0},{96,144},{144,96},{192,240},{240,192},{288,336},{336... | collective-permute-start | bytes 1179656 | tf_op jit(solution)/shard_map/ppermute | solution.py:346
  63.9 0.0 copy-done.4
  63.9 0.1 copy.7.new_lists_ref
  64.0 0.4 multiply_reduce_fusion
  64.4 0.0 copy-start.3
  64.4 1.2 %collective-permute-done.7.odd_ref = bf16[256,768]{1,0:T(8,128)(2,1)} collective-permute-done((bf16[256,768]{1,0:T(8,128)(2,1)}, bf16[256,768]{1,0:T(8,128)(2,1)}, u32[]{:S(2)}, u32[]{:S(2)}) %collective-permute-start.7) | collective-permute-done | bytes 393248 | tf_op jit(solution)/shard_map/ppermute | solution.py:346
  65.6 0.0 copy-done.2
  65.6 5.1 %shard_map.71 = (f32[128,1024]{1,0:T(8,128)}, bf16[16,1,32]{2,1,0:T(2,128)(2,1)}) custom-call(bf16[256,768]{1,0:T(8,128)(2,1)S(1)} %get-tuple-element.25.even_ref, bf16[256,768]{1,0:T(8,128)(2,1)} %collective-permute-done.7.odd_ref, bf16[1024,768]{1,0:T(8,128)(2,1)S(1)} %copy-done, f32[1,1024]{1,0:T(1,128)S(1)} %bitcast.11, s32[1,16]{1,0:T(1,128)S(1)} %bitcast.14, ...), custom_call_target="tpu_custom_call" | custom-call | flops 805306368 | bytes 2359296 | tf_op jit(solution)/shard_map/pallas_call | solution.py:351
  70.7 0.0 all-to-all-done
  70.7 5.8 %all-to-all-start.2 = ((bf16[16,1,32]{2,1,0:T(2,128)(2,1)}), bf16[16,1,32]{2,1,0:T(2,128)(2,1)S(1)}, u32[]{:S(2)}, u32[]{:S(2)}) async-start(bf16[16,1,32]{2,1,0:T(2,128)(2,1)} %get-tuple-element.31), calls=%async_computation.2 | async-start | bytes 16384 | tf_op jit(solution)/shard_map/all_to_all | solution.py:370
  76.5 0.0 copy-done.3
  76.5 2.3 %shard_map.72 = bf16[48,1,16]{2,1,0:T(2,128)(2,1)} custom-call(bf16[768,768]{1,0:T(8,128)(2,1)S(1)} %bitcast.9, bf16[1024,768]{1,0:T(8,128)(2,1)S(1)} %copy-done, f32[1,1024]{1,0:T(1,128)S(1)} %bitcast.12, s32[1,48]{1,0:T(1,128)S(1)} %bitcast.15), custom_call_target="tpu_custom_call" | custom-call | flops 1207959552 | bytes 2359296 | tf_op jit(solution)/shard_map/pallas_call | solution.py:373
  78.8 4.7 %all-to-all-done.2.old_back_ref = bf16[16,1,32]{2,1,0:T(2,128)(2,1)S(1)} async-done(((bf16[16,1,32]{2,1,0:T(2,128)(2,1)}), bf16[16,1,32]{2,1,0:T(2,128)(2,1)S(1)}, u32[]{:S(2)}, u32[]{:S(2)}) %all-to-all-start.2) | async-done | bytes 1056 | tf_op jit(solution)/shard_map/all_to_all | solution.py:370
  83.5 11.4 %all-to-all-start.1 = ((bf16[48,1,16]{2,1,0:T(2,128)(2,1)}), bf16[48,1,16]{2,1,0:T(2,128)(2,1)S(1)}, u32[]{:S(2)}, u32[]{:S(2)}) async-start(bf16[48,1,16]{2,1,0:T(2,128)(2,1)} %shard_map.72), calls=%async_computation.1 | async-start | bytes 49152 | tf_op jit(solution)/shard_map/all_to_all | solution.py:381
  94.9 5.2 %shard_map.73 = f32[16,1024]{1,0:T(8,128)} custom-call(bf16[768,768]{1,0:T(8,128)(2,1)S(1)} %bitcast.10, bf16[1024,768]{1,0:T(8,128)(2,1)S(1)} %copy-done, f32[1,1024]{1,0:T(1,128)S(1)} %bitcast.13, s32[1,48]{1,0:T(1,128)S(1)} %bitcast.16, f32[128,1024]{1,0:T(8,128)} %get-tuple-element.30.held_hbm_ref), custom_call_target="tpu_custom_call" | custom-call | flops 2415919104 | bytes 2359296 | tf_op jit(solution)/shard_map/pallas_call | solution.py:384
  100.1 5.7 %all-to-all-done.1.new_back_ref = bf16[48,1,16]{2,1,0:T(2,128)(2,1)S(1)} async-done(((bf16[48,1,16]{2,1,0:T(2,128)(2,1)}), bf16[48,1,16]{2,1,0:T(2,128)(2,1)S(1)}, u32[]{:S(2)}, u32[]{:S(2)}) %all-to-all-start.1) | async-done | bytes 1568 | tf_op jit(solution)/shard_map/all_to_all | solution.py:381
  105.8 2.6 %shard_map.74 = f32[8,128]{1,0:T(8,128)} custom-call(s32[48,16]{1,0:T(8,128)S(1)} %copy.7.new_lists_ref, s32[16,32]{1,0:T(8,128)S(1)} %copy-done.1, bf16[48,1,16]{2,1,0:T(2,128)(2,1)S(1)} %all-to-all-done.1.new_back_ref, bf16[16,1,32]{2,1,0:T(2,128)(2,1)S(1)} %all-to-all-done.2.old_back_ref), custom_call_target="tpu_custom_call" | custom-call | tf_op jit(solution)/shard_map/pallas_call | solution.py:399
Async XLA Ops:
  4.3 19.0 %copy-start = (bf16[1024,768]{1,0:T(8,128)(2,1)S(1)}, bf16[1024,768]{1,0:T(8,128)(2,1)}, u32[]{:S(2)}) copy-start(bf16[1024,768]{1,0:T(8,128)(2,1)} %points_ref.9) | copy-start | bytes 4718596
  4.3 19.0 %copy-start.1 = (s32[16,32]{1,0:T(8,128)S(1)}, s32[16,32]{1,0:T(8,128)}, u32[]{:S(2)}) copy-start(s32[16,32]{1,0:T(8,128)} %old_lists_ref.1) | copy-start | bytes 6148
  4.3 66.4 %all-to-all-start = ((bf16[48,16,768]{2,1,0:T(8,128)(2,1)}), bf16[48,16,768]{2,1,0:T(8,128)(2,1)S(1)}, u32[]{:S(2)}, u32[]{:S(2)}) async-start(bf16[48,16,768]{2,1,0:T(8,128)(2,1)} %bitcast.17), calls=%async_computation | async-start | bytes 2359296 | tf_op jit(solution)/shard_map/all_to_all | solution.py:330
  23.3 40.6 %copy-start.4 = (s32[48,16]{0,1:T(8,128)S(1)}, s32[48,16]{0,1:T(8,128)}, u32[]{:S(2)}) copy-start(s32[48,16]{0,1:T(8,128)} %param.6) | copy-start | bytes 9220
  24.8 40.7 %copy-start.2 = (s32[16,1]{0,1:T(1,128)S(1)}, s32[16,1]{0,1:T(1,128)}, u32[]{:S(2)}) copy-start(s32[16,1]{0,1:T(1,128)} %param.9) | copy-start | bytes 196
  24.9 18.7 %collective-permute-start = (bf16[64,768]{1,0:T(8,128)(2,1)S(1)}, bf16[64,768]{1,0:T(8,128)(2,1)S(1)}, u32[]{:S(2)}, u32[]{:S(2)}) collective-permute-start(bf16[64,768]{1,0:T(8,128)(2,1)S(1)} %get-tuple-element.18), channel_id=1, source_target_pairs={{0,96},{48,144},{96,0},{144,48},{192,288},{240,336},{288,192},{336... | collective-permute-start | bytes 294920 | tf_op jit(solution)/shard_map/ppermute | solution.py:337
  28.1 20.4 %collective-permute-start.1 = (bf16[64,768]{1,0:T(8,128)(2,1)S(1)}, bf16[64,768]{1,0:T(8,128)(2,1)S(1)}, u32[]{:S(2)}, u32[]{:S(2)}) collective-permute-start(bf16[64,768]{1,0:T(8,128)(2,1)S(1)} %get-tuple-element.19), channel_id=1, source_target_pairs={{0,192},{48,240},{96,288},{144,336},{192,0},{240,48},{288,96},{336... | collective-permute-start | bytes 294920 | tf_op jit(solution)/shard_map/ppermute | solution.py:337
  32.3 18.1 %collective-permute-start.2 = (bf16[64,768]{1,0:T(8,128)(2,1)S(1)}, bf16[64,768]{1,0:T(8,128)(2,1)S(1)}, u32[]{:S(2)}, u32[]{:S(2)}) collective-permute-start(bf16[64,768]{1,0:T(8,128)(2,1)S(1)} %get-tuple-element.20), channel_id=1, source_target_pairs={{0,288},{48,336},{96,192},{144,240},{192,96},{240,144},{288,0},{33... | collective-permute-start | bytes 294920 | tf_op jit(solution)/shard_map/ppermute | solution.py:337
  34.2 16.2 %collective-permute-start.3 = (bf16[64,768]{1,0:T(8,128)(2,1)S(1)}, bf16[64,768]{1,0:T(8,128)(2,1)S(1)}, u32[]{:S(2)}, u32[]{:S(2)}) collective-permute-start(bf16[64,768]{1,0:T(8,128)(2,1)S(1)} %get-tuple-element.21), channel_id=1, source_target_pairs={{0,384},{48,432},{96,480},{144,528},{192,576},{240,624},{288,672},... | collective-permute-start | bytes 294920 | tf_op jit(solution)/shard_map/ppermute | solution.py:337
  41.6 8.8 %collective-permute-start.4 = (bf16[64,768]{1,0:T(8,128)(2,1)S(1)}, bf16[64,768]{1,0:T(8,128)(2,1)S(1)}, u32[]{:S(2)}, u32[]{:S(2)}) collective-permute-start(bf16[64,768]{1,0:T(8,128)(2,1)S(1)} %get-tuple-element.22), channel_id=1, source_target_pairs={{0,480},{48,528},{96,384},{144,432},{192,672},{240,720},{288,576},... | collective-permute-start | bytes 294920 | tf_op jit(solution)/shard_map/ppermute | solution.py:337
  43.6 10.7 %collective-permute-start.5 = (bf16[64,768]{1,0:T(8,128)(2,1)S(1)}, bf16[64,768]{1,0:T(8,128)(2,1)S(1)}, u32[]{:S(2)}, u32[]{:S(2)}) collective-permute-start(bf16[64,768]{1,0:T(8,128)(2,1)S(1)} %get-tuple-element.23), channel_id=1, source_target_pairs={{0,576},{48,624},{96,672},{144,720},{192,384},{240,432},{288,480},... | collective-permute-start | bytes 294920 | tf_op jit(solution)/shard_map/ppermute | solution.py:337
  48.5 11.3 %collective-permute-start.6 = (bf16[64,768]{1,0:T(8,128)(2,1)S(1)}, bf16[64,768]{1,0:T(8,128)(2,1)S(1)}, u32[]{:S(2)}, u32[]{:S(2)}) collective-permute-start(bf16[64,768]{1,0:T(8,128)(2,1)S(1)} %get-tuple-element.24), channel_id=1, source_target_pairs={{0,672},{48,720},{96,576},{144,624},{192,480},{240,528},{288,384},... | collective-permute-start | bytes 294920 | tf_op jit(solution)/shard_map/ppermute | solution.py:337
  60.6 5.0 %collective-permute-start.7 = (bf16[256,768]{1,0:T(8,128)(2,1)}, bf16[256,768]{1,0:T(8,128)(2,1)}, u32[]{:S(2)}, u32[]{:S(2)}) collective-permute-start(bf16[256,768]{1,0:T(8,128)(2,1)} %get-tuple-element.26), channel_id=1, source_target_pairs={{0,48},{48,0},{96,144},{144,96},{192,240},{240,192},{288,336},{336... | collective-permute-start | bytes 1179656 | tf_op jit(solution)/shard_map/ppermute | solution.py:346
  64.4 12.2 %copy-start.3 = (s32[48,1]{0,1:T(1,128)S(1)}, s32[48,1]{0,1:T(1,128)}, u32[]{:S(2)}) copy-start(s32[48,1]{0,1:T(1,128)} %param.8) | copy-start | bytes 580
  70.7 12.7 %all-to-all-start.2 = ((bf16[16,1,32]{2,1,0:T(2,128)(2,1)}), bf16[16,1,32]{2,1,0:T(2,128)(2,1)S(1)}, u32[]{:S(2)}, u32[]{:S(2)}) async-start(bf16[16,1,32]{2,1,0:T(2,128)(2,1)} %get-tuple-element.31), calls=%async_computation.2 | async-start | bytes 16384 | tf_op jit(solution)/shard_map/all_to_all | solution.py:370
  83.5 22.4 %all-to-all-start.1 = ((bf16[48,1,16]{2,1,0:T(2,128)(2,1)}), bf16[48,1,16]{2,1,0:T(2,128)(2,1)S(1)}, u32[]{:S(2)}, u32[]{:S(2)}) async-start(bf16[48,1,16]{2,1,0:T(2,128)(2,1)} %shard_map.72), calls=%async_computation.1 | async-start | bytes 49152 | tf_op jit(solution)/shard_map/all_to_all | solution.py:381

commit v6 on v5

--- a/solution.py
+++ b/solution.py
@@ -202,56 +202,22 @@
     return [jnp.sum(spread[at : at + slots, :], axis=0, keepdims=True) for at in range(0, chunk, slots)]
 
 
-def halves_kernel(slots, *refs):
+def halves_kernel(slots, order, *refs):
     pieces, (mine_ref, handed_ref) = refs[:-2], refs[-2:]
-    for k, piece in enumerate(pieces):
+    for k, piece in zip(order, pieces):
         mine_ref[k * slots : (k + 1) * slots, :] = piece[:slots, :]
         handed_ref[k * slots : (k + 1) * slots, :] = piece[slots:, :]
 
 
-def near_kernel(
-    groups, slots, even_ref, odd_ref, points_ref, own_sq_ref, counts_ref, place_ref,
-    held_ref, minima_ref, dist_ref, held, sems,
-):
-    count = groups // 2
-    half = count * slots
-
-    def order(block):
-        return jnp.where(block < count, 2 * block, 2 * (block - count) + 1) ^ place_ref[0]
-
-    for start, cand_ref in ((0, even_ref), (half, odd_ref)):
-        usable = usable_slots(counts_ref, start, half, groups, slots, order)
-        dist = distances(cand_ref[...], points_ref, own_sq_ref)
-        dist_ref[start : start + half, :] = jnp.where(usable, dist, far_value)
-        minima = jnp.where(usable, jnp.min(dist, axis=1, keepdims=True), cap_value)
-        for k, row in enumerate(slot_rows(minima, slots)):
-            minima_ref[order(start // slots + k)] = row.astype(jnp.bfloat16)
-
-    def block(t, _):
-        lanes = pl.ds(pl.multiple_of(t * LANES, LANES), LANES)
-        for k, value in enumerate(smallest16(dist_ref, lanes, None)):
-            held[SUBLANES * k : SUBLANES * (k + 1), lanes] = value
-        return 0
-
-    blocks = dist_ref.shape[1] // LANES
-    copies = []
-    for part in range(2):
-        first, last = part * blocks // 2, (part + 1) * blocks // 2
-        lax.fori_loop(first, last, block, 0)
-        lanes = pl.ds(first * LANES, (last - first) * LANES)
-        copies.append(pltpu.make_async_copy(held.at[:, lanes], held_ref.at[:, lanes], sems.at[part]))
-        copies[-1].start()
-    for copy in copies:
-        copy.wait()
-
-
-def minima_kernel(peers, slots, cand_ref, points_ref, own_sq_ref, counts_ref, minima_ref):
-    total, rows = peers * slots, points_ref.shape[0]
-    cand = cand_ref[...]
+def source_of(count, place_ref):
+    return lambda block: jnp.where(block < count, 2 * block, 2 * (block - count) + 1) ^ place_ref[0]
+
+
+def least_distances(cand, points_ref, own_sq_ref):
     wide = cand.astype(jnp.float32)
     cand_sq = jnp.sum(wide * wide, axis=1, keepdims=True)
     least = None
-    for start in range(0, rows, 256):
+    for start in range(0, points_ref.shape[0], 256):
         inner = lax.dot_general(
             cand, points_ref[start : start + 256, :], (((1,), (1,)), ((), ())), preferred_element_type=jnp.float32
         )
@@ -259,8 +225,39 @@
             own = own_sq_ref[:, start + at : start + at + LANES]
             dist = cand_sq + own - 2.0 * inner[:, at : at + LANES]
             least = dist if least is None else jnp.minimum(least, dist)
-    usable = usable_slots(counts_ref, 0, total, peers, slots, straight)
-    minima = jnp.where(usable, jnp.min(least, axis=1, keepdims=True), cap_value)
+    return jnp.min(least, axis=1, keepdims=True)
+
+
+def minima_old_kernel(groups, slots, even_ref, odd_ref, points_ref, own_sq_ref, counts_ref, place_ref, minima_ref):
+    half = groups // 2 * slots
+    order = source_of(groups // 2, place_ref)
+    for start, cand_ref in ((0, even_ref), (half, odd_ref)):
+        usable = usable_slots(counts_ref, start, half, groups, slots, order)
+        minima = jnp.where(usable, least_distances(cand_ref[...], points_ref, own_sq_ref), cap_value)
+        for k, row in enumerate(slot_rows(minima, slots)):
+            minima_ref[order(start // slots + k)] = row.astype(jnp.bfloat16)
+
+
+def held_kernel(groups, slots, even_ref, odd_ref, points_ref, own_sq_ref, counts_ref, place_ref, held_ref, dist_ref):
+    half = groups // 2 * slots
+    order = source_of(groups // 2, place_ref)
+    for start, cand_ref in ((0, even_ref), (half, odd_ref)):
+        usable = usable_slots(counts_ref, start, half, groups, slots, order)
+        dist = distances(cand_ref[...], points_ref, own_sq_ref)
+        dist_ref[start : start + half, :] = jnp.where(usable, dist, far_value)
+
+    def block(t, _):
+        lanes = pl.ds(pl.multiple_of(t * LANES, LANES), LANES)
+        for k, value in enumerate(smallest16(dist_ref, lanes, None)):
+            held_ref[SUBLANES * k : SUBLANES * (k + 1), lanes] = value
+        return 0
+
+    lax.fori_loop(0, dist_ref.shape[1] // LANES, block, 0)
+
+
+def minima_kernel(peers, slots, cand_ref, points_ref, own_sq_ref, counts_ref, minima_ref):
+    usable = usable_slots(counts_ref, 0, peers * slots, peers, slots, straight)
+    minima = jnp.where(usable, least_distances(cand_ref[...], points_ref, own_sq_ref), cap_value)
     for k, row in enumerate(slot_rows(minima, slots)):
         minima_ref[k] = row.astype(jnp.bfloat16)
 
@@ -292,23 +289,34 @@
     lax.fori_loop(0, dist_ref.shape[1] // LANES, block, 0)
 
 
-def fold(best, lists, back):
-    peers, slots = lists.shape
+def ready_kernel(old_lists_ref, old_back_ref, new_lists_ref, best_ref, wide_ref):
+    best = jnp.full(best_ref.shape, cap_value, jnp.float32)
+    old_back = old_back_ref[...].reshape(old_lists_ref.shape).astype(jnp.float32)
+    peers, slots = old_lists_ref.shape
     for c in range(slots):
         for at in range(0, peers, SUBLANES):
-            index = lists[at : at + SUBLANES, c : c + 1]
+            index = old_lists_ref[at : at + SUBLANES, c : c + 1]
+            value = old_back[at : at + SUBLANES, c : c + 1]
+            best = jnp.where(index == iota(best.shape, 1), jnp.minimum(best, value), best)
+    best_ref[...] = best
+    peers, slots = new_lists_ref.shape
+    for c in range(slots):
+        wide_ref[c * peers : (c + 1) * peers, :] = jnp.broadcast_to(new_lists_ref[:, c : c + 1], (peers, LANES))
+
+
+def reverse_kernel(back_ref, best_ref, wide_ref, out_ref):
+    peers, _, slots = back_ref.shape
+    back = back_ref[...].reshape(peers, slots).astype(jnp.float32)
+    lane = iota((SUBLANES, LANES), 1)
+    best = [best_ref[:, LANES * k : LANES * (k + 1)] for k in range(SUBLANES)]
+    for c in range(slots):
+        for at in range(0, peers, SUBLANES):
+            index = wide_ref[c * peers + at : c * peers + at + SUBLANES, :]
             value = back[at : at + SUBLANES, c : c + 1]
-            best = jnp.where(index == iota(best.shape, 1), jnp.minimum(best, value), best)
-    return best
-
-
-def reverse_kernel(new_lists_ref, old_lists_ref, new_back_ref, old_back_ref, out_ref):
-    best = jnp.full((SUBLANES, SUBLANES * LANES), cap_value, jnp.float32)
-    for lists_ref, back_ref in ((old_lists_ref, old_back_ref), (new_lists_ref, new_back_ref)):
-        best = fold(best, lists_ref[...], back_ref[...].reshape(lists_ref.shape).astype(jnp.float32))
-    best = jnp.min(best, axis=0, keepdims=True)
+            for k in range(SUBLANES):
+                best[k] = jnp.minimum(best[k], jnp.where(index == lane + k * LANES, value, cap_value))
     for k in range(SUBLANES):
-        out_ref[k : k + 1, :] = best[:, LANES * k : LANES * (k + 1)]
+        out_ref[k : k + 1, :] = jnp.min(best[k], axis=0, keepdims=True)
 
 
 def apart(groups, away):
@@ -332,39 +340,30 @@
     ).reshape(peers * slots, features)
 
     pieces = gather_old(points, serve_old, place, groups, group_slots, groups // 2)
-    came = {0: pieces[0]}
-    for k in sorted(range(1, groups // 2), key=lambda k: min(k, groups // 2 - k), reverse=True):
-        came[k] = lax.ppermute(pieces[k], "grp", apart(groups, 2 * k))
-    evens = [came[k] for k in range(groups // 2)]
+    spread = (4, 2, 6, 3, 7, 5, 1)
+    order = tuple(k for k in spread if k < groups // 2) + tuple(range(len(spread) + 1, groups // 2))
+    came = [lax.ppermute(pieces[k], "grp", apart(groups, 2 * k)) for k in order]
     half = groups // 2 * group_slots
     evens, handed = pl.pallas_call(
-        functools.partial(halves_kernel, group_slots),
+        functools.partial(halves_kernel, group_slots, order + (0,)),
         out_shape=(jax.ShapeDtypeStruct((half, features), jnp.bfloat16),) * 2,
         compiler_params=params,
         cost_estimate=pl.CostEstimate(flops=0, bytes_accessed=8 * half * features, transcendentals=0),
-    )(*evens)
+    )(*came, pieces[0])
     odds = lax.ppermute(handed, "grp", apart(groups, 1))
 
     own_sq = jnp.sum(jnp.square(points.astype(jnp.float32)), axis=1)[None, :]
 
     total_old = groups * group_slots
-    held, minima_old = pl.pallas_call(
-        functools.partial(near_kernel, groups, group_slots),
+    old_cost = pl.CostEstimate(
+        flops=2 * total_old * rows * features, bytes_accessed=2 * (total_old + rows) * features, transcendentals=0
+    )
+    minima_old = pl.pallas_call(
+        functools.partial(minima_old_kernel, groups, group_slots),
         in_specs=[vmem] * 5 + [smem],
-        out_specs=(pl.BlockSpec(memory_space=pltpu.HBM), vmem),
-        out_shape=(
-            pltpu.HBM((16 * SUBLANES, rows), jnp.float32),
-            jax.ShapeDtypeStruct((groups, 1, group_slots), jnp.bfloat16),
-        ),
-        scratch_shapes=[
-            pltpu.VMEM((total_old, rows), jnp.float32),
-            pltpu.VMEM((16 * SUBLANES, rows), jnp.float32),
-            pltpu.SemaphoreType.DMA((2,)),
-        ],
-        compiler_params=params,
-        cost_estimate=pl.CostEstimate(
-            flops=2 * total_old * rows * features, bytes_accessed=2 * (total_old + rows) * features, transcendentals=0
-        ),
+        out_shape=jax.ShapeDtypeStruct((groups, 1, group_slots), jnp.bfloat16),
+        compiler_params=params,
+        cost_estimate=old_cost,
     )(evens, odds, points, own_sq, counts_old, place)
     pulled_new, minima_old = lax.optimization_barrier((pulled_new, minima_old))
     back_old = lax.all_to_all(minima_old, "grp", split_axis=0, concat_axis=0, tiled=True)
@@ -380,7 +379,16 @@
     )(pulled_new, points, own_sq, counts_new)
     back_new = lax.all_to_all(minima_new, "shard", split_axis=0, concat_axis=0, tiled=True)
 
-    pulled_new, _ = lax.optimization_barrier((pulled_new, minima_new))
+    evens, _ = lax.optimization_barrier((evens, pulled_new))
+    held = pl.pallas_call(
+        functools.partial(held_kernel, groups, group_slots),
+        in_specs=[vmem] * 5 + [smem],
+        out_shape=pltpu.HBM((16 * SUBLANES, rows), jnp.float32),
+        scratch_shapes=[pltpu.VMEM((total_old, rows), jnp.float32)],
+        compiler_params=params,
+        cost_estimate=old_cost,
+    )(evens, odds, points, own_sq, counts_old, place)
+    pulled_new, back_old, _ = lax.optimization_barrier((pulled_new, back_old, minima_new))
     nearest = pl.pallas_call(
         functools.partial(select_kernel, peers, slots, 256),
         in_specs=[vmem] * 4 + [pl.BlockSpec(memory_space=pltpu.HBM)],
@@ -396,11 +404,20 @@
         ),
     )(pulled_new, points, own_sq, counts_new, pltpu.with_memory_space_constraint(held, pltpu.HBM))
 
+    nearest, back_old = lax.optimization_barrier((nearest, back_old))
+    best, wide = pl.pallas_call(
+        ready_kernel,
+        out_shape=(
+            jax.ShapeDtypeStruct((SUBLANES, rows), jnp.float32),
+            jax.ShapeDtypeStruct((total_new, LANES), jnp.int32),
+        ),
+        compiler_params=params,
+    )(serve_old, back_old, serve_new)
     reverse = pl.pallas_call(
         reverse_kernel,
         out_shape=jax.ShapeDtypeStruct((SUBLANES, LANES), jnp.float32),
         compiler_params=params,
-    )(serve_new, serve_old, back_new, back_old)
+    )(back_new, best, wide)
     return nearest.T, reverse.reshape(rows)
 
 

time: 109 us -> 104 us (0.954)
  waiting for transfers between devices: 20.9 us -> 10.1 us
  starting transfers between devices: 65.1 us -> 68.5 us
  Pallas kernels: 21.1 us -> 23.2 us
    ppermute x7, waiting for transfers between devices: 9.33 us -> 3.87 us  [body(): came = [lax.ppermute(pieces[k], 'grp', apart(groups, 2 * k)) for k in order]]
    all_to_all x1, waiting for transfers between devices: 4.66 us -> 0.28 us  [body(): lax.all_to_all(minima_old, 'grp', split_axis=0, concat_axis=0, tiled=True)]
    all_to_all x1, starting transfers between devices: 11.4 us -> 7.13 us  [body(): lax.all_to_all(minima_new, 'shard', split_axis=0, concat_axis=0, tiled=True)]
    all_to_all x1, starting transfers between devices: 5.81 us -> 10 us  [body(): lax.all_to_all(minima_old, 'grp', split_axis=0, concat_axis=0, tiled=True)]
    ppermute x1, starting transfers between devices: 3.35 us -> 6.94 us  [body(): odds = lax.ppermute(handed, 'grp', apart(groups, 1))]
    pallas_call x2 -> x4, Pallas kernels: 5.92 us -> 8.91 us  [the longest x1 4.41 us: body(): pl.pallas_call(functools.partial(held_kernel, groups, group_slots), in_sp...]
  transfers between devices with their start and end apart: 11 -> 11, of which waited for: 5 -> 4; matrix products, arithmetic and copies ran while one was open for 0% -> 0% of each run, Pallas kernels for 14% -> 17%
where the time goes in v6:
time: 104 us; the launch traced here: 103 us
  starting transfers between devices  68.5 us (66%)
  Pallas kernels  23.2 us (22%)
  waiting for transfers between devices  10.1 us (10%)
    ppermute x7, starting transfers between devices, body(): came = [lax.ppermute(pieces[k], 'grp', apart(groups, 2 * k)) for k in order]  25.5 us
    all_to_all x1, starting transfers between devices, body(): lax.all_to_all(offered_new.reshape(peers, slots, features), 'shard', spli...  19 us
    all_to_all x1, starting transfers between devices, body(): lax.all_to_all(minima_old, 'grp', split_axis=0, concat_axis=0, tiled=True)  10 us
    all_to_all x1, starting transfers between devices, body(): lax.all_to_all(minima_new, 'shard', split_axis=0, concat_axis=0, tiled=True)  7.13 us
    ppermute x1, starting transfers between devices, body(): odds = lax.ppermute(handed, 'grp', apart(groups, 1))  6.94 us
    pallas_call x1, Pallas kernels, body(): pl.pallas_call(functools.partial(select_kernel, peers, slots, 256), in_sp...  5.24 us
    all_to_all x1, waiting for transfers between devices, body(): lax.all_to_all(minima_new, 'shard', split_axis=0, concat_axis=0, tiled=True)  4.78 us
    pallas_call x1, Pallas kernels, body(): pl.pallas_call(functools.partial(held_kernel, groups, group_slots), in_sp...  4.41 us
  transfers between devices with their start and end apart: 11, of which 4 were waited for; matrix products, arithmetic and copies ran while one was open for 0% of the time, Pallas kernels for 17%

profile of v6, /device:TPU:1, one launch (start us, length us, event | category | flops | bytes accessed | tf_op | source)
XLA Modules:
  0.0 103.2 jit_solution(2568169080987394020)
XLA Ops:
  0.6 3.7 %shard_map.68 = bf16[768,768]{1,0:T(8,128)(2,1)} custom-call(bf16[1024,768]{1,0:T(8,128)(2,1)} %points_ref.11, s32[16,48]{1,0:T(8,128)} %bitcast.20), custom_call_target="tpu_custom_call" | custom-call | flops 1207959552 | bytes 2752512 | tf_op jit(solution)/shard_map/pallas_call | solution.py:101
  4.3 0.0 copy-start
  4.3 0.0 copy-start.1
  4.3 19.0 %all-to-all-start = ((bf16[48,16,768]{2,1,0:T(8,128)(2,1)}), bf16[48,16,768]{2,1,0:T(8,128)(2,1)S(1)}, u32[]{:S(2)}, u32[]{:S(2)}) async-start(bf16[48,16,768]{2,1,0:T(8,128)(2,1)} %bitcast.19), calls=%async_computation | async-start | bytes 2359296 | tf_op jit(solution)/shard_map/all_to_all | solution.py:338
  23.3 0.0 copy-done
  23.3 0.0 copy-done.1
  23.3 0.0 copy-start.4
  23.3 1.5 %shard_map.69 = (bf16[64,768]{1,0:T(8,128)(2,1)S(1)}, bf16[64,768]{1,0:T(8,128)(2,1)S(1)}, bf16[64,768]{1,0:T(8,128)(2,1)S(1)}, bf16[64,768]{1,0:T(8,128)(2,1)S(...) custom-call(bf16[1024,768]{1,0:T(8,128)(2,1)S(1)} %copy-done, ...), custom_call_target="tpu_custom_call" | custom-call | flops 805306368 | bytes 2359296 | tf_op jit(solution)/shard_map/pallas_call | solution.py:135
  24.8 0.0 copy-start.2
  24.9 7.5 %collective-permute-start = (bf16[64,768]{1,0:T(8,128)(2,1)S(1)}, bf16[64,768]{1,0:T(8,128)(2,1)S(1)}, u32[]{:S(2)}, u32[]{:S(2)}) collective-permute-start(bf16[64,768]{1,0:T(8,128)(2,1)S(1)} %get-tuple-element.21), channel_id=1, source_target_pairs={{0,384},{48,432},{96,480},{144,528},{192,576},{240,624},{288,672},... | collective-permute-start | bytes 294920 | tf_op jit(solution)/shard_map/ppermute | solution.py:345
  32.3 2.4 %collective-permute-start.1 = (bf16[64,768]{1,0:T(8,128)(2,1)S(1)}, bf16[64,768]{1,0:T(8,128)(2,1)S(1)}, u32[]{:S(2)}, u32[]{:S(2)}) collective-permute-start(bf16[64,768]{1,0:T(8,128)(2,1)S(1)} %get-tuple-element.22), channel_id=1, source_target_pairs={{0,192},{48,240},{96,288},{144,336},{192,0},{240,48},{288,96},{336... | collective-permute-start | bytes 294920 | tf_op jit(solution)/shard_map/ppermute | solution.py:345
  34.7 1.9 %collective-permute-start.2 = (bf16[64,768]{1,0:T(8,128)(2,1)S(1)}, bf16[64,768]{1,0:T(8,128)(2,1)S(1)}, u32[]{:S(2)}, u32[]{:S(2)}) collective-permute-start(bf16[64,768]{1,0:T(8,128)(2,1)S(1)} %get-tuple-element.23), channel_id=1, source_target_pairs={{0,576},{48,624},{96,672},{144,720},{192,384},{240,432},{288,480},... | collective-permute-start | bytes 294920 | tf_op jit(solution)/shard_map/ppermute | solution.py:345
  36.7 4.8 %collective-permute-start.3 = (bf16[64,768]{1,0:T(8,128)(2,1)S(1)}, bf16[64,768]{1,0:T(8,128)(2,1)S(1)}, u32[]{:S(2)}, u32[]{:S(2)}) collective-permute-start(bf16[64,768]{1,0:T(8,128)(2,1)S(1)} %get-tuple-element.24), channel_id=1, source_target_pairs={{0,288},{48,336},{96,192},{144,240},{192,96},{240,144},{288,0},{33... | collective-permute-start | bytes 294920 | tf_op jit(solution)/shard_map/ppermute | solution.py:345
  41.5 4.4 %collective-permute-start.4 = (bf16[64,768]{1,0:T(8,128)(2,1)S(1)}, bf16[64,768]{1,0:T(8,128)(2,1)S(1)}, u32[]{:S(2)}, u32[]{:S(2)}) collective-permute-start(bf16[64,768]{1,0:T(8,128)(2,1)S(1)} %get-tuple-element.25), channel_id=1, source_target_pairs={{0,672},{48,720},{96,576},{144,624},{192,480},{240,528},{288,384},... | collective-permute-start | bytes 294920 | tf_op jit(solution)/shard_map/ppermute | solution.py:345
  45.9 0.0 collective-permute-done.refs_0_
  45.9 1.9 %collective-permute-start.5 = (bf16[64,768]{1,0:T(8,128)(2,1)S(1)}, bf16[64,768]{1,0:T(8,128)(2,1)S(1)}, u32[]{:S(2)}, u32[]{:S(2)}) collective-permute-start(bf16[64,768]{1,0:T(8,128)(2,1)S(1)} %get-tuple-element.26), channel_id=1, source_target_pairs={{0,480},{48,528},{96,384},{144,432},{192,672},{240,720},{288,576},... | collective-permute-start | bytes 294920 | tf_op jit(solution)/shard_map/ppermute | solution.py:345
  47.9 0.0 collective-permute-done.1.refs_1_
  47.9 2.5 %collective-permute-start.6 = (bf16[64,768]{1,0:T(8,128)(2,1)S(1)}, bf16[64,768]{1,0:T(8,128)(2,1)S(1)}, u32[]{:S(2)}, u32[]{:S(2)}) collective-permute-start(bf16[64,768]{1,0:T(8,128)(2,1)S(1)} %get-tuple-element.27), channel_id=1, source_target_pairs={{0,96},{48,144},{96,0},{144,48},{192,288},{240,336},{288,192},{336... | collective-permute-start | bytes 294920 | tf_op jit(solution)/shard_map/ppermute | solution.py:345
  50.4 0.0 collective-permute-done.2.refs_2_
  50.4 0.0 collective-permute-done.3.refs_3_
  50.4 0.0 collective-permute-done.4.refs_4_
  50.4 3.9 %collective-permute-done.5.refs_5_ = bf16[64,768]{1,0:T(8,128)(2,1)S(1)} collective-permute-done((bf16[64,768]{1,0:T(8,128)(2,1)S(1)}, bf16[64,768]{1,0:T(8,128)(2,1)S(1)}, u32[]{:S(2)}, u32[]{:S(2)}) %collective-permute-start.5) | collective-permute-done | bytes 98336 | tf_op jit(solution)/shard_map/ppermute | solution.py:345
  54.3 0.0 collective-permute-done.6.refs_6_
  54.3 0.8 shard_map.70
  55.1 6.9 %collective-permute-start.7 = (bf16[256,768]{1,0:T(8,128)(2,1)}, bf16[256,768]{1,0:T(8,128)(2,1)}, u32[]{:S(2)}, u32[]{:S(2)}) collective-permute-start(bf16[256,768]{1,0:T(8,128)(2,1)} %get-tuple-element.30), channel_id=1, source_target_pairs={{0,48},{48,0},{96,144},{144,96},{192,240},{240,192},{288,336},{336... | collective-permute-start | bytes 1179656 | tf_op jit(solution)/shard_map/ppermute | solution.py:353
  62.1 0.0 copy-done.4
  62.1 0.1 copy.7.new_lists_ref
  62.1 0.4 multiply_reduce_fusion
  62.5 0.0 copy-start.3
  62.5 1.2 %collective-permute-done.7.odd_ref = bf16[256,768]{1,0:T(8,128)(2,1)} collective-permute-done((bf16[256,768]{1,0:T(8,128)(2,1)}, bf16[256,768]{1,0:T(8,128)(2,1)}, u32[]{:S(2)}, u32[]{:S(2)}) %collective-permute-start.7) | collective-permute-done | bytes 393248 | tf_op jit(solution)/shard_map/ppermute | solution.py:353
  63.7 0.0 copy-done.2
  63.7 2.8 %shard_map.71 = bf16[16,1,32]{2,1,0:T(2,128)(2,1)} custom-call(bf16[256,768]{1,0:T(8,128)(2,1)S(1)} %get-tuple-element.34.even_ref, bf16[256,768]{1,0:T(8,128)(2,1)} %collective-permute-done.7.odd_ref, bf16[1024,768]{1,0:T(8,128)(2,1)S(1)} %copy-done, f32[1,1024]{1,0:T(1,128)S(1)} %bitcast.11, s32[1,16]{1,0:T(1,128)S(1)} %bitcast.15, s32[1]{0:T(128)} %bitcast.3.place_ref), custom_call_target="tpu_custom_call" | custom-call | flops 805306368 | bytes 2359296 | tf_op jit(solution)/shard_map/pallas_call | solution.py:361
  66.5 0.0 all-to-all-done
  66.5 10.0 %all-to-all-start.1 = ((bf16[16,1,32]{2,1,0:T(2,128)(2,1)}), bf16[16,1,32]{2,1,0:T(2,128)(2,1)S(1)}, u32[]{:S(2)}, u32[]{:S(2)}) async-start(bf16[16,1,32]{2,1,0:T(2,128)(2,1)} %shard_map.71), calls=%async_computation.1 | async-start | bytes 16384 | tf_op jit(solution)/shard_map/all_to_all | solution.py:369
  76.5 0.0 copy-done.3
  76.5 2.3 %shard_map.72 = bf16[48,1,16]{2,1,0:T(2,128)(2,1)} custom-call(bf16[768,768]{1,0:T(8,128)(2,1)S(1)} %bitcast.9, bf16[1024,768]{1,0:T(8,128)(2,1)S(1)} %copy-done, f32[1,1024]{1,0:T(1,128)S(1)} %bitcast.12, s32[1,48]{1,0:T(1,128)S(1)} %bitcast.17), custom_call_target="tpu_custom_call" | custom-call | flops 1207959552 | bytes 2359296 | tf_op jit(solution)/shard_map/pallas_call | solution.py:372
  78.8 4.4 %shard_map.73.held_hbm_ref = f32[128,1024]{1,0:T(8,128)} custom-call(bf16[256,768]{1,0:T(8,128)(2,1)S(1)} %get-tuple-element.34.even_ref, bf16[256,768]{1,0:T(8,128)(2,1)} %collective-permute-done.7.odd_ref, bf16[1024,768]{1,0:T(8,128)(2,1)S(1)} %copy-done, f32[1,1024]{1,0:T(1,128)S(1)} %bitcast.13, s32[1,16]{1,0:T(1,128)S(1)} %bitcast.16, s32[1]{0:T(128)} %bitcast.3.place_ref), custom_call_target="tpu_custom_call" | custom-call | flops 805306368 | bytes 2359296 | tf_op jit(solution)/shard_map/pallas_call | solution.py:383
  83.2 0.3 all-to-all-done.1.old_back_ref
  83.5 7.1 %all-to-all-start.2 = ((bf16[48,1,16]{2,1,0:T(2,128)(2,1)}), bf16[48,1,16]{2,1,0:T(2,128)(2,1)S(1)}, u32[]{:S(2)}, u32[]{:S(2)}) async-start(bf16[48,1,16]{2,1,0:T(2,128)(2,1)} %shard_map.72), calls=%async_computation.2 | async-start | bytes 49152 | tf_op jit(solution)/shard_map/all_to_all | solution.py:380
  90.6 5.2 %shard_map.74 = f32[16,1024]{1,0:T(8,128)} custom-call(bf16[768,768]{1,0:T(8,128)(2,1)S(1)} %bitcast.10, bf16[1024,768]{1,0:T(8,128)(2,1)S(1)} %copy-done, f32[1,1024]{1,0:T(1,128)S(1)} %bitcast.14, s32[1,48]{1,0:T(1,128)S(1)} %bitcast.18, f32[128,1024]{1,0:T(8,128)} %shard_map.73.held_hbm_ref), custom_call_target="tpu_custom_call" | custom-call | flops 2415919104 | bytes 2359296 | tf_op jit(solution)/shard_map/pallas_call | solution.py:392
  95.9 0.9 shard_map.75
  96.8 4.8 %all-to-all-done.2.back_ref = bf16[48,1,16]{2,1,0:T(2,128)(2,1)S(1)} async-done(((bf16[48,1,16]{2,1,0:T(2,128)(2,1)}), bf16[48,1,16]{2,1,0:T(2,128)(2,1)S(1)}, u32[]{:S(2)}, u32[]{:S(2)}) %all-to-all-start.2) | async-done | bytes 1568 | tf_op jit(solution)/shard_map/all_to_all | solution.py:380
  101.5 1.6 %shard_map.76 = f32[8,128]{1,0:T(8,128)} custom-call(bf16[48,1,16]{2,1,0:T(2,128)(2,1)S(1)} %all-to-all-done.2.back_ref, f32[8,1024]{1,0:T(8,128)S(1)} %get-tuple-element.38.best_ref, s32[768,128]{1,0:T(8,128)S(1)} %get-tuple-element.39.wide_ref), custom_call_target="tpu_custom_call" | custom-call | tf_op jit(solution)/shard_map/pallas_call | solution.py:416
Async XLA Ops:
  4.3 19.0 %copy-start = (bf16[1024,768]{1,0:T(8,128)(2,1)S(1)}, bf16[1024,768]{1,0:T(8,128)(2,1)}, u32[]{:S(2)}) copy-start(bf16[1024,768]{1,0:T(8,128)(2,1)} %points_ref.11) | copy-start | bytes 4718596
  4.3 19.0 %copy-start.1 = (s32[16,32]{1,0:T(8,128)S(1)}, s32[16,32]{1,0:T(8,128)}, u32[]{:S(2)}) copy-start(s32[16,32]{1,0:T(8,128)} %old_lists_ref.1) | copy-start | bytes 6148
  4.3 62.2 %all-to-all-start = ((bf16[48,16,768]{2,1,0:T(8,128)(2,1)}), bf16[48,16,768]{2,1,0:T(8,128)(2,1)S(1)}, u32[]{:S(2)}, u32[]{:S(2)}) async-start(bf16[48,16,768]{2,1,0:T(8,128)(2,1)} %bitcast.19), calls=%async_computation | async-start | bytes 2359296 | tf_op jit(solution)/shard_map/all_to_all | solution.py:338
  23.3 38.7 %copy-start.4 = (s32[48,16]{0,1:T(8,128)S(1)}, s32[48,16]{0,1:T(8,128)}, u32[]{:S(2)}) copy-start(s32[48,16]{0,1:T(8,128)} %param.6) | copy-start | bytes 9220
  24.8 38.9 %copy-start.2 = (s32[16,1]{0,1:T(1,128)S(1)}, s32[16,1]{0,1:T(1,128)}, u32[]{:S(2)}) copy-start(s32[16,1]{0,1:T(1,128)} %param.9) | copy-start | bytes 196
  24.9 21.1 %collective-permute-start = (bf16[64,768]{1,0:T(8,128)(2,1)S(1)}, bf16[64,768]{1,0:T(8,128)(2,1)S(1)}, u32[]{:S(2)}, u32[]{:S(2)}) collective-permute-start(bf16[64,768]{1,0:T(8,128)(2,1)S(1)} %get-tuple-element.21), channel_id=1, source_target_pairs={{0,384},{48,432},{96,480},{144,528},{192,576},{240,624},{288,672},... | collective-permute-start | bytes 294920 | tf_op jit(solution)/shard_map/ppermute | solution.py:345
  32.3 15.5 %collective-permute-start.1 = (bf16[64,768]{1,0:T(8,128)(2,1)S(1)}, bf16[64,768]{1,0:T(8,128)(2,1)S(1)}, u32[]{:S(2)}, u32[]{:S(2)}) collective-permute-start(bf16[64,768]{1,0:T(8,128)(2,1)S(1)} %get-tuple-element.22), channel_id=1, source_target_pairs={{0,192},{48,240},{96,288},{144,336},{192,0},{240,48},{288,96},{336... | collective-permute-start | bytes 294920 | tf_op jit(solution)/shard_map/ppermute | solution.py:345
  34.7 15.7 %collective-permute-start.2 = (bf16[64,768]{1,0:T(8,128)(2,1)S(1)}, bf16[64,768]{1,0:T(8,128)(2,1)S(1)}, u32[]{:S(2)}, u32[]{:S(2)}) collective-permute-start(bf16[64,768]{1,0:T(8,128)(2,1)S(1)} %get-tuple-element.23), channel_id=1, source_target_pairs={{0,576},{48,624},{96,672},{144,720},{192,384},{240,432},{288,480},... | collective-permute-start | bytes 294920 | tf_op jit(solution)/shard_map/ppermute | solution.py:345
  36.7 13.8 %collective-permute-start.3 = (bf16[64,768]{1,0:T(8,128)(2,1)S(1)}, bf16[64,768]{1,0:T(8,128)(2,1)S(1)}, u32[]{:S(2)}, u32[]{:S(2)}) collective-permute-start(bf16[64,768]{1,0:T(8,128)(2,1)S(1)} %get-tuple-element.24), channel_id=1, source_target_pairs={{0,288},{48,336},{96,192},{144,240},{192,96},{240,144},{288,0},{33... | collective-permute-start | bytes 294920 | tf_op jit(solution)/shard_map/ppermute | solution.py:345
  41.5 8.9 %collective-permute-start.4 = (bf16[64,768]{1,0:T(8,128)(2,1)S(1)}, bf16[64,768]{1,0:T(8,128)(2,1)S(1)}, u32[]{:S(2)}, u32[]{:S(2)}) collective-permute-start(bf16[64,768]{1,0:T(8,128)(2,1)S(1)} %get-tuple-element.25), channel_id=1, source_target_pairs={{0,672},{48,720},{96,576},{144,624},{192,480},{240,528},{288,384},... | collective-permute-start | bytes 294920 | tf_op jit(solution)/shard_map/ppermute | solution.py:345
  45.9 8.4 %collective-permute-start.5 = (bf16[64,768]{1,0:T(8,128)(2,1)S(1)}, bf16[64,768]{1,0:T(8,128)(2,1)S(1)}, u32[]{:S(2)}, u32[]{:S(2)}) collective-permute-start(bf16[64,768]{1,0:T(8,128)(2,1)S(1)} %get-tuple-element.26), channel_id=1, source_target_pairs={{0,480},{48,528},{96,384},{144,432},{192,672},{240,720},{288,576},... | collective-permute-start | bytes 294920 | tf_op jit(solution)/shard_map/ppermute | solution.py:345
  47.9 6.4 %collective-permute-start.6 = (bf16[64,768]{1,0:T(8,128)(2,1)S(1)}, bf16[64,768]{1,0:T(8,128)(2,1)S(1)}, u32[]{:S(2)}, u32[]{:S(2)}) collective-permute-start(bf16[64,768]{1,0:T(8,128)(2,1)S(1)} %get-tuple-element.27), channel_id=1, source_target_pairs={{0,96},{48,144},{96,0},{144,48},{192,288},{240,336},{288,192},{336... | collective-permute-start | bytes 294920 | tf_op jit(solution)/shard_map/ppermute | solution.py:345
  55.1 8.6 %collective-permute-start.7 = (bf16[256,768]{1,0:T(8,128)(2,1)}, bf16[256,768]{1,0:T(8,128)(2,1)}, u32[]{:S(2)}, u32[]{:S(2)}) collective-permute-start(bf16[256,768]{1,0:T(8,128)(2,1)} %get-tuple-element.30), channel_id=1, source_target_pairs={{0,48},{48,0},{96,144},{144,96},{192,240},{240,192},{288,336},{336... | collective-permute-start | bytes 1179656 | tf_op jit(solution)/shard_map/ppermute | solution.py:353
  62.5 14.0 %copy-start.3 = (s32[48,1]{0,1:T(1,128)S(1)}, s32[48,1]{0,1:T(1,128)}, u32[]{:S(2)}) copy-start(s32[48,1]{0,1:T(1,128)} %param.8) | copy-start | bytes 580
  66.5 16.9 %all-to-all-start.1 = ((bf16[16,1,32]{2,1,0:T(2,128)(2,1)}), bf16[16,1,32]{2,1,0:T(2,128)(2,1)S(1)}, u32[]{:S(2)}, u32[]{:S(2)}) async-start(bf16[16,1,32]{2,1,0:T(2,128)(2,1)} %shard_map.71), calls=%async_computation.1 | async-start | bytes 16384 | tf_op jit(solution)/shard_map/all_to_all | solution.py:369
  83.5 18.1 %all-to-all-start.2 = ((bf16[48,1,16]{2,1,0:T(2,128)(2,1)}), bf16[48,1,16]{2,1,0:T(2,128)(2,1)S(1)}, u32[]{:S(2)}, u32[]{:S(2)}) async-start(bf16[48,1,16]{2,1,0:T(2,128)(2,1)} %shard_map.72), calls=%async_computation.2 | async-start | bytes 49152 | tf_op jit(solution)/shard_map/all_to_all | solution.py:380

commit v7 on v6

--- a/solution.py
+++ b/solution.py
@@ -228,31 +228,49 @@
     return jnp.min(least, axis=1, keepdims=True)
 
 
-def minima_old_kernel(groups, slots, even_ref, odd_ref, points_ref, own_sq_ref, counts_ref, place_ref, minima_ref):
-    half = groups // 2 * slots
-    order = source_of(groups // 2, place_ref)
-    for start, cand_ref in ((0, even_ref), (half, odd_ref)):
-        usable = usable_slots(counts_ref, start, half, groups, slots, order)
-        minima = jnp.where(usable, least_distances(cand_ref[...], points_ref, own_sq_ref), cap_value)
-        for k, row in enumerate(slot_rows(minima, slots)):
-            minima_ref[order(start // slots + k)] = row.astype(jnp.bfloat16)
-
-
-def held_kernel(groups, slots, even_ref, odd_ref, points_ref, own_sq_ref, counts_ref, place_ref, held_ref, dist_ref):
-    half = groups // 2 * slots
-    order = source_of(groups // 2, place_ref)
-    for start, cand_ref in ((0, even_ref), (half, odd_ref)):
-        usable = usable_slots(counts_ref, start, half, groups, slots, order)
-        dist = distances(cand_ref[...], points_ref, own_sq_ref)
-        dist_ref[start : start + half, :] = jnp.where(usable, dist, far_value)
-
+def hold(dist_ref, before_ref, held_ref):
     def block(t, _):
         lanes = pl.ds(pl.multiple_of(t * LANES, LANES), LANES)
-        for k, value in enumerate(smallest16(dist_ref, lanes, None)):
+        before = None if before_ref is None else block16(before_ref, 0, lanes)
+        for k, value in enumerate(smallest16(dist_ref, lanes, before)):
             held_ref[SUBLANES * k : SUBLANES * (k + 1), lanes] = value
         return 0
 
     lax.fori_loop(0, dist_ref.shape[1] // LANES, block, 0)
+
+
+def even_kernel(groups, slots, cand_ref, points_ref, own_sq_ref, counts_ref, place_ref, rows_ref, held_ref, dist_ref):
+    half = groups // 2 * slots
+    usable = usable_slots(counts_ref, 0, half, groups, slots, source_of(groups // 2, place_ref))
+    dist = distances(cand_ref[...], points_ref, own_sq_ref)
+    dist_ref[...] = jnp.where(usable, dist, far_value)
+    minima = jnp.where(usable, jnp.min(dist, axis=1, keepdims=True), cap_value)
+    for k, row in enumerate(slot_rows(minima, slots)):
+        rows_ref[k : k + 1, :] = row
+    hold(dist_ref, None, held_ref)
+
+
+def minima_old_kernel(groups, slots, cand_ref, points_ref, own_sq_ref, counts_ref, rows_ref, place_ref, minima_ref):
+    count = groups // 2
+    order = source_of(count, place_ref)
+    usable = usable_slots(counts_ref, count * slots, count * slots, groups, slots, order)
+    minima = jnp.where(usable, least_distances(cand_ref[...], points_ref, own_sq_ref), cap_value)
+    for k, row in enumerate(slot_rows(minima, slots)):
+        minima_ref[order(k)] = rows_ref[k : k + 1, :].astype(jnp.bfloat16)
+        minima_ref[order(count + k)] = row.astype(jnp.bfloat16)
+
+
+def odd_kernel(
+    groups, slots, cand_ref, points_ref, own_sq_ref, counts_ref, place_ref, before_hbm_ref, held_ref,
+    dist_ref, before_ref, sem,
+):
+    fetch = pltpu.make_async_copy(before_hbm_ref, before_ref, sem)
+    fetch.start()
+    half = groups // 2 * slots
+    usable = usable_slots(counts_ref, half, half, groups, slots, source_of(groups // 2, place_ref))
+    dist_ref[...] = jnp.where(usable, distances(cand_ref[...], points_ref, own_sq_ref), far_value)
+    fetch.wait()
+    hold(dist_ref, before_ref, held_ref)
 
 
 def minima_kernel(peers, slots, cand_ref, points_ref, own_sq_ref, counts_ref, minima_ref):
@@ -299,9 +317,17 @@
             value = old_back[at : at + SUBLANES, c : c + 1]
             best = jnp.where(index == iota(best.shape, 1), jnp.minimum(best, value), best)
     best_ref[...] = best
-    peers, slots = new_lists_ref.shape
+    slots, peers = new_lists_ref.shape
+    same = onehot(iota((slots, slots), 0) == iota((slots, slots), 1))
+
+    def upright(values):
+        return lax.dot_general(
+            values.astype(jnp.bfloat16), same, (((0,), (0,)), ((), ())), preferred_element_type=jnp.float32
+        ).astype(jnp.int32)
+
+    lists = upright(new_lists_ref[...] // 32) * 32 + upright(new_lists_ref[...] % 32)
     for c in range(slots):
-        wide_ref[c * peers : (c + 1) * peers, :] = jnp.broadcast_to(new_lists_ref[:, c : c + 1], (peers, LANES))
+        wide_ref[c * peers : (c + 1) * peers, :] = jnp.broadcast_to(lists[:, c : c + 1], (peers, LANES))
 
 
 def reverse_kernel(back_ref, best_ref, wide_ref, out_ref):
@@ -343,28 +369,41 @@
     spread = (4, 2, 6, 3, 7, 5, 1)
     order = tuple(k for k in spread if k < groups // 2) + tuple(range(len(spread) + 1, groups // 2))
     came = [lax.ppermute(pieces[k], "grp", apart(groups, 2 * k)) for k in order]
+    own_sq = jnp.sum(jnp.square(points.astype(jnp.float32)), axis=1)[None, :]
+    own_sq, own_piece = lax.optimization_barrier((own_sq, pieces[0]))
+
     half = groups // 2 * group_slots
     evens, handed = pl.pallas_call(
         functools.partial(halves_kernel, group_slots, order + (0,)),
         out_shape=(jax.ShapeDtypeStruct((half, features), jnp.bfloat16),) * 2,
         compiler_params=params,
         cost_estimate=pl.CostEstimate(flops=0, bytes_accessed=8 * half * features, transcendentals=0),
-    )(*came, pieces[0])
+    )(*came, own_piece)
     odds = lax.ppermute(handed, "grp", apart(groups, 1))
 
-    own_sq = jnp.sum(jnp.square(points.astype(jnp.float32)), axis=1)[None, :]
-
-    total_old = groups * group_slots
     old_cost = pl.CostEstimate(
-        flops=2 * total_old * rows * features, bytes_accessed=2 * (total_old + rows) * features, transcendentals=0
+        flops=2 * half * rows * features, bytes_accessed=2 * (half + rows) * features, transcendentals=0
     )
+    held_shape = (16 * SUBLANES, rows)
+    minima_even, held = pl.pallas_call(
+        functools.partial(even_kernel, groups, group_slots),
+        in_specs=[vmem] * 4 + [smem],
+        out_shape=(
+            jax.ShapeDtypeStruct((groups // 2, group_slots), jnp.float32),
+            pltpu.HBM(held_shape, jnp.float32),
+        ),
+        scratch_shapes=[pltpu.VMEM((half, rows), jnp.float32)],
+        compiler_params=params,
+        cost_estimate=old_cost,
+    )(evens, points, own_sq, counts_old, place)
     minima_old = pl.pallas_call(
         functools.partial(minima_old_kernel, groups, group_slots),
         in_specs=[vmem] * 5 + [smem],
         out_shape=jax.ShapeDtypeStruct((groups, 1, group_slots), jnp.bfloat16),
         compiler_params=params,
         cost_estimate=old_cost,
-    )(evens, odds, points, own_sq, counts_old, place)
+    )(odds, points, own_sq, counts_old, minima_even, place)
+
     pulled_new, minima_old = lax.optimization_barrier((pulled_new, minima_old))
     back_old = lax.all_to_all(minima_old, "grp", split_axis=0, concat_axis=0, tiled=True)
 
@@ -379,23 +418,28 @@
     )(pulled_new, points, own_sq, counts_new)
     back_new = lax.all_to_all(minima_new, "shard", split_axis=0, concat_axis=0, tiled=True)
 
-    evens, _ = lax.optimization_barrier((evens, pulled_new))
+    odds, _ = lax.optimization_barrier((odds, pulled_new))
+    hbm = pl.BlockSpec(memory_space=pltpu.HBM)
     held = pl.pallas_call(
-        functools.partial(held_kernel, groups, group_slots),
-        in_specs=[vmem] * 5 + [smem],
-        out_shape=pltpu.HBM((16 * SUBLANES, rows), jnp.float32),
-        scratch_shapes=[pltpu.VMEM((total_old, rows), jnp.float32)],
+        functools.partial(odd_kernel, groups, group_slots),
+        in_specs=[vmem] * 4 + [smem, hbm],
+        out_shape=pltpu.HBM(held_shape, jnp.float32),
+        scratch_shapes=[
+            pltpu.VMEM((half, rows), jnp.float32),
+            pltpu.VMEM(held_shape, jnp.float32),
+            pltpu.SemaphoreType.DMA,
+        ],
         compiler_params=params,
         cost_estimate=old_cost,
-    )(evens, odds, points, own_sq, counts_old, place)
+    )(odds, points, own_sq, counts_old, place, pltpu.with_memory_space_constraint(held, pltpu.HBM))
     pulled_new, back_old, _ = lax.optimization_barrier((pulled_new, back_old, minima_new))
     nearest = pl.pallas_call(
         functools.partial(select_kernel, peers, slots, 256),
-        in_specs=[vmem] * 4 + [pl.BlockSpec(memory_space=pltpu.HBM)],
+        in_specs=[vmem] * 4 + [hbm],
         out_shape=jax.ShapeDtypeStruct((NEAR, rows), jnp.float32),
         scratch_shapes=[
             pltpu.VMEM((total_new, rows), jnp.float32),
-            pltpu.VMEM((16 * SUBLANES, rows), jnp.float32),
+            pltpu.VMEM(held_shape, jnp.float32),
             pltpu.SemaphoreType.DMA,
         ],
         compiler_params=params,
@@ -412,7 +456,7 @@
             jax.ShapeDtypeStruct((total_new, LANES), jnp.int32),
         ),
         compiler_params=params,
-    )(serve_old, back_old, serve_new)
+    )(serve_old, back_old, lists_new)
     reverse = pl.pallas_call(
         reverse_kernel,
         out_shape=jax.ShapeDtypeStruct((SUBLANES, LANES), jnp.float32),

time: 104 us -> 104 us (level)
  starting transfers between devices: 68.5 us -> 70.4 us
  Pallas kernels: 23.2 us -> 21.4 us
    all_to_all x1, starting transfers between devices: 10 us -> 11.8 us  [body(): lax.all_to_all(minima_old, 'grp', split_axis=0, concat_axis=0, tiled=True)]
    all_to_all x1, waiting for transfers between devices: 0.28 us -> 1.77 us  [body(): lax.all_to_all(minima_old, 'grp', split_axis=0, concat_axis=0, tiled=True)]
    pallas_call x1, Pallas kernels: 2.79 us -> 1.33 us  [body(): pl.pallas_call(functools.partial(minima_old_kernel, groups, group_slots),...]
    ppermute x1, waiting for transfers between devices: 1.19 us -> 0.01 us  [body(): odds = lax.ppermute(handed, 'grp', apart(groups, 1))]
    pallas_call x1 -> x2, Pallas kernels: 4.41 us -> 4.89 us  [the longest x1 2.89 us: body(): pl.pallas_call(functools.partial(odd_kernel, groups, group_slots), in_spe...]
  transfers between devices with their start and end apart: 11 -> 11, of which waited for: 4 -> 3; matrix products, arithmetic and copies ran while one was open for 0% -> 0% of each run, Pallas kernels for 17% -> 16%
where the time goes in v7:
time: 104 us; the launch traced here: 103 us
  starting transfers between devices  70.4 us (68%)
  Pallas kernels  21.4 us (21%)
  waiting for transfers between devices  10 us (10%)
    ppermute x7, starting transfers between devices, body(): came = [lax.ppermute(pieces[k], 'grp', apart(groups, 2 * k)) for k in order]  25.5 us
    all_to_all x1, starting transfers between devices, body(): lax.all_to_all(offered_new.reshape(peers, slots, features), 'shard', spli...  19 us
    all_to_all x1, starting transfers between devices, body(): lax.all_to_all(minima_old, 'grp', split_axis=0, concat_axis=0, tiled=True)  11.8 us
    all_to_all x1, starting transfers between devices, body(): lax.all_to_all(minima_new, 'shard', split_axis=0, concat_axis=0, tiled=True)  7.13 us
    ppermute x1, starting transfers between devices, body(): odds = lax.ppermute(handed, 'grp', apart(groups, 1))  7.05 us
    pallas_call x1, Pallas kernels, body(): pl.pallas_call(functools.partial(select_kernel, peers, slots, 256), in_sp...  5.2 us
    all_to_all x1, waiting for transfers between devices, body(): lax.all_to_all(minima_new, 'shard', split_axis=0, concat_axis=0, tiled=True)  4.76 us
    pallas_call x1, Pallas kernels, gather_new(): pl.pallas_call(functools.partial(gather_new_kernel, peers, slots, chunk),...  3.66 us
  transfers between devices with their start and end apart: 11, of which 3 were waited for; matrix products, arithmetic and copies ran while one was open for 0% of the time, Pallas kernels for 16%

profile of v7, /device:TPU:1, one launch (start us, length us, event | category | flops | bytes accessed | tf_op | source)
XLA Modules:
  0.0 103.2 jit_solution(7403668461196686313)
XLA Ops:
  0.6 3.7 %shard_map.68 = bf16[768,768]{1,0:T(8,128)(2,1)} custom-call(bf16[1024,768]{1,0:T(8,128)(2,1)} %points_ref.13, s32[16,48]{1,0:T(8,128)} %bitcast.16), custom_call_target="tpu_custom_call" | custom-call | flops 1207959552 | bytes 2752512 | tf_op jit(solution)/shard_map/pallas_call | solution.py:101
  4.3 0.0 copy-start
  4.3 0.0 copy-start.2
  4.3 19.0 %all-to-all-start = ((bf16[48,16,768]{2,1,0:T(8,128)(2,1)}), bf16[48,16,768]{2,1,0:T(8,128)(2,1)S(1)}, u32[]{:S(2)}, u32[]{:S(2)}) async-start(bf16[48,16,768]{2,1,0:T(8,128)(2,1)} %bitcast.23), calls=%async_computation | async-start | bytes 2359296 | tf_op jit(solution)/shard_map/all_to_all | solution.py:364
  23.3 0.0 copy-done
  23.3 0.0 copy-done.2
  23.3 1.5 %shard_map.69 = (bf16[64,768]{1,0:T(8,128)(2,1)S(1)}, bf16[64,768]{1,0:T(8,128)(2,1)S(1)}, bf16[64,768]{1,0:T(8,128)(2,1)S(1)}, bf16[64,768]{1,0:T(8,128)(2,1)S(...) custom-call(bf16[1024,768]{1,0:T(8,128)(2,1)S(1)} %copy-done, ...), custom_call_target="tpu_custom_call" | custom-call | flops 805306368 | bytes 2359296 | tf_op jit(solution)/shard_map/pallas_call | solution.py:135
  24.8 0.0 copy-start.3
  24.8 7.5 %collective-permute-start = (bf16[64,768]{1,0:T(8,128)(2,1)S(1)}, bf16[64,768]{1,0:T(8,128)(2,1)S(1)}, u32[]{:S(2)}, u32[]{:S(2)}) collective-permute-start(bf16[64,768]{1,0:T(8,128)(2,1)S(1)} %get-tuple-element.25), channel_id=1, source_target_pairs={{0,384},{48,432},{96,480},{144,528},{192,576},{240,624},{288,672},... | collective-permute-start | bytes 294920 | tf_op jit(solution)/shard_map/ppermute | solution.py:371
  32.3 2.4 %collective-permute-start.1 = (bf16[64,768]{1,0:T(8,128)(2,1)S(1)}, bf16[64,768]{1,0:T(8,128)(2,1)S(1)}, u32[]{:S(2)}, u32[]{:S(2)}) collective-permute-start(bf16[64,768]{1,0:T(8,128)(2,1)S(1)} %get-tuple-element.26), channel_id=1, source_target_pairs={{0,192},{48,240},{96,288},{144,336},{192,0},{240,48},{288,96},{336... | collective-permute-start | bytes 294920 | tf_op jit(solution)/shard_map/ppermute | solution.py:371
  34.7 1.9 %collective-permute-start.2 = (bf16[64,768]{1,0:T(8,128)(2,1)S(1)}, bf16[64,768]{1,0:T(8,128)(2,1)S(1)}, u32[]{:S(2)}, u32[]{:S(2)}) collective-permute-start(bf16[64,768]{1,0:T(8,128)(2,1)S(1)} %get-tuple-element.27), channel_id=1, source_target_pairs={{0,576},{48,624},{96,672},{144,720},{192,384},{240,432},{288,480},... | collective-permute-start | bytes 294920 | tf_op jit(solution)/shard_map/ppermute | solution.py:371
  36.7 4.8 %collective-permute-start.3 = (bf16[64,768]{1,0:T(8,128)(2,1)S(1)}, bf16[64,768]{1,0:T(8,128)(2,1)S(1)}, u32[]{:S(2)}, u32[]{:S(2)}) collective-permute-start(bf16[64,768]{1,0:T(8,128)(2,1)S(1)} %get-tuple-element.28), channel_id=1, source_target_pairs={{0,288},{48,336},{96,192},{144,240},{192,96},{240,144},{288,0},{33... | collective-permute-start | bytes 294920 | tf_op jit(solution)/shard_map/ppermute | solution.py:371
  41.5 4.4 %collective-permute-start.4 = (bf16[64,768]{1,0:T(8,128)(2,1)S(1)}, bf16[64,768]{1,0:T(8,128)(2,1)S(1)}, u32[]{:S(2)}, u32[]{:S(2)}) collective-permute-start(bf16[64,768]{1,0:T(8,128)(2,1)S(1)} %get-tuple-element.29), channel_id=1, source_target_pairs={{0,672},{48,720},{96,576},{144,624},{192,480},{240,528},{288,384},... | collective-permute-start | bytes 294920 | tf_op jit(solution)/shard_map/ppermute | solution.py:371
  45.9 0.0 collective-permute-done.refs_0_
  45.9 1.9 %collective-permute-start.5 = (bf16[64,768]{1,0:T(8,128)(2,1)S(1)}, bf16[64,768]{1,0:T(8,128)(2,1)S(1)}, u32[]{:S(2)}, u32[]{:S(2)}) collective-permute-start(bf16[64,768]{1,0:T(8,128)(2,1)S(1)} %get-tuple-element.30), channel_id=1, source_target_pairs={{0,480},{48,528},{96,384},{144,432},{192,672},{240,720},{288,576},... | collective-permute-start | bytes 294920 | tf_op jit(solution)/shard_map/ppermute | solution.py:371
  47.8 0.0 collective-permute-done.1.refs_1_
  47.9 2.5 %collective-permute-start.6 = (bf16[64,768]{1,0:T(8,128)(2,1)S(1)}, bf16[64,768]{1,0:T(8,128)(2,1)S(1)}, u32[]{:S(2)}, u32[]{:S(2)}) collective-permute-start(bf16[64,768]{1,0:T(8,128)(2,1)S(1)} %get-tuple-element.31), channel_id=1, source_target_pairs={{0,96},{48,144},{96,0},{144,48},{192,288},{240,336},{288,192},{336... | collective-permute-start | bytes 294920 | tf_op jit(solution)/shard_map/ppermute | solution.py:371
  50.4 0.4 multiply_reduce_fusion
  50.8 0.0 collective-permute-done.2.refs_2_
  50.8 0.0 collective-permute-done.3.refs_3_
  50.8 0.0 collective-permute-done.4.refs_4_
  50.8 3.5 %collective-permute-done.5.refs_5_ = bf16[64,768]{1,0:T(8,128)(2,1)S(1)} collective-permute-done((bf16[64,768]{1,0:T(8,128)(2,1)S(1)}, bf16[64,768]{1,0:T(8,128)(2,1)S(1)}, u32[]{:S(2)}, u32[]{:S(2)}) %collective-permute-start.5) | collective-permute-done | bytes 98336 | tf_op jit(solution)/shard_map/ppermute | solution.py:371
  54.3 0.0 collective-permute-done.6.refs_6_
  54.3 0.1 shard_map.70
  54.3 7.0 %collective-permute-start.7 = (bf16[256,768]{1,0:T(8,128)(2,1)S(1)}, bf16[256,768]{1,0:T(8,128)(2,1)S(1)}, u32[]{:S(2)}, u32[]{:S(2)}) collective-permute-start(bf16[256,768]{1,0:T(8,128)(2,1)S(1)} %get-tuple-element.34), channel_id=1, source_target_pairs={{0,48},{48,0},{96,144},{144,96},{192,240},{240,192},{288,336},{336... | collective-permute-start | bytes 1179656 | tf_op jit(solution)/shard_map/ppermute | solution.py:382
  61.4 0.0 copy-done.3
  61.4 0.0 copy-start.4
  61.4 2.0 %shard_map.71 = (f32[8,32]{1,0:T(8,128)S(1)}, f32[128,1024]{1,0:T(8,128)}) custom-call(bf16[256,768]{1,0:T(8,128)(2,1)S(1)} %get-tuple-element.36.cand_ref, bf16[1024,768]{1,0:T(8,128)(2,1)S(1)} %copy-done, f32[1,1024]{1,0:T(1,128)S(1)} %bitcast.11, s32[1,16]{1,0:T(1,128)S(1)} %bitcast.18, s32[1]{0:T(128)} %bitcast.3.place_ref), custom_call_target="tpu_custom_call" | custom-call | flops 402653184 | bytes 1966080 | tf_op jit(solution)/shard_map/pallas_call | solution.py:388
  63.4 0.0 collective-permute-done.7.cand_ref
  63.4 1.3 %shard_map.72 = bf16[16,1,32]{2,1,0:T(2,128)(2,1)} custom-call(bf16[256,768]{1,0:T(8,128)(2,1)S(1)} %collective-permute-done.7.cand_ref, bf16[1024,768]{1,0:T(8,128)(2,1)S(1)} %copy-done, f32[1,1024]{1,0:T(1,128)S(1)} %bitcast.12, s32[1,16]{1,0:T(1,128)S(1)} %bitcast.19, f32[8,32]{1,0:T(8,128)S(1)} %get-tuple-element.37.rows_ref, s32[1]{0:T(128)} %bitcast.3.place_ref), custom_call_target="tpu_custom_call" | custom-call | flops 402653184 | bytes 1966080 | tf_op jit(solution)/shard_map/pallas_call | solution.py:399
  64.8 0.0 all-to-all-done
  64.8 11.8 %all-to-all-start.1 = ((bf16[16,1,32]{2,1,0:T(2,128)(2,1)}), bf16[16,1,32]{2,1,0:T(2,128)(2,1)S(1)}, u32[]{:S(2)}, u32[]{:S(2)}) async-start(bf16[16,1,32]{2,1,0:T(2,128)(2,1)} %shard_map.72), calls=%async_computation.1 | async-start | bytes 16384 | tf_op jit(solution)/shard_map/all_to_all | solution.py:408
  76.5 0.0 copy-done.4
  76.5 2.3 %shard_map.73 = bf16[48,1,16]{2,1,0:T(2,128)(2,1)} custom-call(bf16[768,768]{1,0:T(8,128)(2,1)S(1)} %bitcast.9, bf16[1024,768]{1,0:T(8,128)(2,1)S(1)} %copy-done, f32[1,1024]{1,0:T(1,128)S(1)} %bitcast.13, s32[1,48]{1,0:T(1,128)S(1)} %bitcast.21), custom_call_target="tpu_custom_call" | custom-call | flops 1207959552 | bytes 2359296 | tf_op jit(solution)/shard_map/pallas_call | solution.py:411
  78.8 2.9 %shard_map.74.held_hbm_ref = f32[128,1024]{1,0:T(8,128)} custom-call(bf16[256,768]{1,0:T(8,128)(2,1)S(1)} %collective-permute-done.7.cand_ref, bf16[1024,768]{1,0:T(8,128)(2,1)S(1)} %copy-done, f32[1,1024]{1,0:T(1,128)S(1)} %bitcast.14, s32[1,16]{1,0:T(1,128)S(1)} %bitcast.20, s32[1]{0:T(128)} %bitcast.3.place_ref, f32[128,1024]{1,0:T(8,128)} %get-tuple-element.42.before_hbm_ref), custom_call_target="tpu_custom_call" | custom-call | flops 402653184 | bytes 1966080 | tf_op jit(solution)/shard_map/pallas_call | solution.py:423
  81.7 1.8 %all-to-all-done.1.old_back_ref = bf16[16,1,32]{2,1,0:T(2,128)(2,1)S(1)} async-done(((bf16[16,1,32]{2,1,0:T(2,128)(2,1)}), bf16[16,1,32]{2,1,0:T(2,128)(2,1)S(1)}, u32[]{:S(2)}, u32[]{:S(2)}) %all-to-all-start.1) | async-done | bytes 1056 | tf_op jit(solution)/shard_map/all_to_all | solution.py:408
  83.5 7.1 %all-to-all-start.2 = ((bf16[48,1,16]{2,1,0:T(2,128)(2,1)}), bf16[48,1,16]{2,1,0:T(2,128)(2,1)S(1)}, u32[]{:S(2)}, u32[]{:S(2)}) async-start(bf16[48,1,16]{2,1,0:T(2,128)(2,1)} %shard_map.73), calls=%async_computation.2 | async-start | bytes 49152 | tf_op jit(solution)/shard_map/all_to_all | solution.py:419
  90.6 0.0 copy-start.1
  90.6 5.2 %shard_map.75 = f32[16,1024]{1,0:T(8,128)} custom-call(bf16[768,768]{1,0:T(8,128)(2,1)S(1)} %bitcast.10, bf16[1024,768]{1,0:T(8,128)(2,1)S(1)} %copy-done, f32[1,1024]{1,0:T(1,128)S(1)} %bitcast.15, s32[1,48]{1,0:T(1,128)S(1)} %bitcast.22, f32[128,1024]{1,0:T(8,128)} %shard_map.74.held_hbm_ref), custom_call_target="tpu_custom_call" | custom-call | flops 2415919104 | bytes 2359296 | tf_op jit(solution)/shard_map/pallas_call | solution.py:436
  95.8 0.0 copy-done.1
  95.8 0.9 shard_map.76
  96.8 4.8 %all-to-all-done.2.back_ref = bf16[48,1,16]{2,1,0:T(2,128)(2,1)S(1)} async-done(((bf16[48,1,16]{2,1,0:T(2,128)(2,1)}), bf16[48,1,16]{2,1,0:T(2,128)(2,1)S(1)}, u32[]{:S(2)}, u32[]{:S(2)}) %all-to-all-start.2) | async-done | bytes 1568 | tf_op jit(solution)/shard_map/all_to_all | solution.py:419
  101.5 1.6 %shard_map.77 = f32[8,128]{1,0:T(8,128)} custom-call(bf16[48,1,16]{2,1,0:T(2,128)(2,1)S(1)} %all-to-all-done.2.back_ref, f32[8,1024]{1,0:T(8,128)S(1)} %get-tuple-element.46.best_ref, s32[768,128]{1,0:T(8,128)S(1)} %get-tuple-element.47.wide_ref), custom_call_target="tpu_custom_call" | custom-call | tf_op jit(solution)/shard_map/pallas_call | solution.py:460
Async XLA Ops:
  4.3 19.0 %copy-start = (bf16[1024,768]{1,0:T(8,128)(2,1)S(1)}, bf16[1024,768]{1,0:T(8,128)(2,1)}, u32[]{:S(2)}) copy-start(bf16[1024,768]{1,0:T(8,128)(2,1)} %points_ref.13) | copy-start | bytes 4718596
  4.3 19.0 %copy-start.2 = (s32[16,32]{1,0:T(8,128)S(1)}, s32[16,32]{1,0:T(8,128)}, u32[]{:S(2)}) copy-start(s32[16,32]{1,0:T(8,128)} %old_lists_ref.1) | copy-start | bytes 6148
  4.3 60.4 %all-to-all-start = ((bf16[48,16,768]{2,1,0:T(8,128)(2,1)}), bf16[48,16,768]{2,1,0:T(8,128)(2,1)S(1)}, u32[]{:S(2)}, u32[]{:S(2)}) async-start(bf16[48,16,768]{2,1,0:T(8,128)(2,1)} %bitcast.23), calls=%async_computation | async-start | bytes 2359296 | tf_op jit(solution)/shard_map/all_to_all | solution.py:364
  24.8 36.6 %copy-start.3 = (s32[16,1]{0,1:T(1,128)S(1)}, s32[16,1]{0,1:T(1,128)}, u32[]{:S(2)}) copy-start(s32[16,1]{0,1:T(1,128)} %param.9) | copy-start | bytes 196
  24.8 21.1 %collective-permute-start = (bf16[64,768]{1,0:T(8,128)(2,1)S(1)}, bf16[64,768]{1,0:T(8,128)(2,1)S(1)}, u32[]{:S(2)}, u32[]{:S(2)}) collective-permute-start(bf16[64,768]{1,0:T(8,128)(2,1)S(1)} %get-tuple-element.25), channel_id=1, source_target_pairs={{0,384},{48,432},{96,480},{144,528},{192,576},{240,624},{288,672},... | collective-permute-start | bytes 294920 | tf_op jit(solution)/shard_map/ppermute | solution.py:371
  32.3 15.5 %collective-permute-start.1 = (bf16[64,768]{1,0:T(8,128)(2,1)S(1)}, bf16[64,768]{1,0:T(8,128)(2,1)S(1)}, u32[]{:S(2)}, u32[]{:S(2)}) collective-permute-start(bf16[64,768]{1,0:T(8,128)(2,1)S(1)} %get-tuple-element.26), channel_id=1, source_target_pairs={{0,192},{48,240},{96,288},{144,336},{192,0},{240,48},{288,96},{336... | collective-permute-start | bytes 294920 | tf_op jit(solution)/shard_map/ppermute | solution.py:371
  34.7 16.1 %collective-permute-start.2 = (bf16[64,768]{1,0:T(8,128)(2,1)S(1)}, bf16[64,768]{1,0:T(8,128)(2,1)S(1)}, u32[]{:S(2)}, u32[]{:S(2)}) collective-permute-start(bf16[64,768]{1,0:T(8,128)(2,1)S(1)} %get-tuple-element.27), channel_id=1, source_target_pairs={{0,576},{48,624},{96,672},{144,720},{192,384},{240,432},{288,480},... | collective-permute-start | bytes 294920 | tf_op jit(solution)/shard_map/ppermute | solution.py:371
  36.7 14.1 %collective-permute-start.3 = (bf16[64,768]{1,0:T(8,128)(2,1)S(1)}, bf16[64,768]{1,0:T(8,128)(2,1)S(1)}, u32[]{:S(2)}, u32[]{:S(2)}) collective-permute-start(bf16[64,768]{1,0:T(8,128)(2,1)S(1)} %get-tuple-element.28), channel_id=1, source_target_pairs={{0,288},{48,336},{96,192},{144,240},{192,96},{240,144},{288,0},{33... | collective-permute-start | bytes 294920 | tf_op jit(solution)/shard_map/ppermute | solution.py:371
  41.5 9.3 %collective-permute-start.4 = (bf16[64,768]{1,0:T(8,128)(2,1)S(1)}, bf16[64,768]{1,0:T(8,128)(2,1)S(1)}, u32[]{:S(2)}, u32[]{:S(2)}) collective-permute-start(bf16[64,768]{1,0:T(8,128)(2,1)S(1)} %get-tuple-element.29), channel_id=1, source_target_pairs={{0,672},{48,720},{96,576},{144,624},{192,480},{240,528},{288,384},... | collective-permute-start | bytes 294920 | tf_op jit(solution)/shard_map/ppermute | solution.py:371
  45.9 8.4 %collective-permute-start.5 = (bf16[64,768]{1,0:T(8,128)(2,1)S(1)}, bf16[64,768]{1,0:T(8,128)(2,1)S(1)}, u32[]{:S(2)}, u32[]{:S(2)}) collective-permute-start(bf16[64,768]{1,0:T(8,128)(2,1)S(1)} %get-tuple-element.30), channel_id=1, source_target_pairs={{0,480},{48,528},{96,384},{144,432},{192,672},{240,720},{288,576},... | collective-permute-start | bytes 294920 | tf_op jit(solution)/shard_map/ppermute | solution.py:371
  47.9 6.4 %collective-permute-start.6 = (bf16[64,768]{1,0:T(8,128)(2,1)S(1)}, bf16[64,768]{1,0:T(8,128)(2,1)S(1)}, u32[]{:S(2)}, u32[]{:S(2)}) collective-permute-start(bf16[64,768]{1,0:T(8,128)(2,1)S(1)} %get-tuple-element.31), channel_id=1, source_target_pairs={{0,96},{48,144},{96,0},{144,48},{192,288},{240,336},{288,192},{336... | collective-permute-start | bytes 294920 | tf_op jit(solution)/shard_map/ppermute | solution.py:371
  54.3 9.1 %collective-permute-start.7 = (bf16[256,768]{1,0:T(8,128)(2,1)S(1)}, bf16[256,768]{1,0:T(8,128)(2,1)S(1)}, u32[]{:S(2)}, u32[]{:S(2)}) collective-permute-start(bf16[256,768]{1,0:T(8,128)(2,1)S(1)} %get-tuple-element.34), channel_id=1, source_target_pairs={{0,48},{48,0},{96,144},{144,96},{192,240},{240,192},{288,336},{336... | collective-permute-start | bytes 1179656 | tf_op jit(solution)/shard_map/ppermute | solution.py:382
  61.4 15.1 %copy-start.4 = (s32[48,1]{0,1:T(1,128)S(1)}, s32[48,1]{0,1:T(1,128)}, u32[]{:S(2)}) copy-start(s32[48,1]{0,1:T(1,128)} %param.8) | copy-start | bytes 580
  64.8 18.7 %all-to-all-start.1 = ((bf16[16,1,32]{2,1,0:T(2,128)(2,1)}), bf16[16,1,32]{2,1,0:T(2,128)(2,1)S(1)}, u32[]{:S(2)}, u32[]{:S(2)}) async-start(bf16[16,1,32]{2,1,0:T(2,128)(2,1)} %shard_map.72), calls=%async_computation.1 | async-start | bytes 16384 | tf_op jit(solution)/shard_map/all_to_all | solution.py:408
  83.5 18.1 %all-to-all-start.2 = ((bf16[48,1,16]{2,1,0:T(2,128)(2,1)}), bf16[48,1,16]{2,1,0:T(2,128)(2,1)S(1)}, u32[]{:S(2)}, u32[]{:S(2)}) async-start(bf16[48,1,16]{2,1,0:T(2,128)(2,1)} %shard_map.73), calls=%async_computation.2 | async-start | bytes 49152 | tf_op jit(solution)/shard_map/all_to_all | solution.py:419
  90.6 5.2 %copy-start.1 = (s32[48,16]{0,1:T(8,128)S(1)}, s32[48,16]{0,1:T(8,128)}, u32[]{:S(2)}) copy-start(s32[48,16]{0,1:T(8,128)} %param.6) | copy-start | bytes 9220

commit v8 on v7

--- a/solution.py
+++ b/solution.py
@@ -62,40 +62,46 @@
 
 
 def index_column(lists, parts):
-    high = column(*parts, (lists // 32).astype(jnp.bfloat16))
-    low = column(*parts, (lists % 32).astype(jnp.bfloat16))
-    return high.astype(jnp.int32) * 32 + low.astype(jnp.int32)
-
-
-def gather_new_kernel(peers, slots, chunk, points_ref, lists_ref, out_ref, points, lists, picked, in_sems, out_sems):
-    total, rows = peers * slots, points.shape[0]
+    rows_of, lane_of = parts
+    rows_of = onehot(rows_of)
+    high = dot(rows_of, (lists // 32).astype(jnp.bfloat16))
+    low = dot(rows_of, (lists % 32).astype(jnp.bfloat16))
+    return jnp.sum(jnp.where(lane_of, high * 32.0 + low, 0.0), axis=1, keepdims=True).astype(jnp.int32)
+
+
+def gather_new_kernel(
+    peers, slots, chunk, points_ref, lists_ref, out_ref, points, lists, picked, first, in_sems, out_sems
+):
+    total, rows = peers * slots, points_ref.shape[0]
     loads = [pltpu.make_async_copy(lists_ref, lists, in_sems.at[0])]
-    for k, start in enumerate(range(0, rows, chunk)):
-        part = pl.ds(start, chunk)
+    for k in range(4):
+        part = pl.ds(k * (rows // 4), rows // 4)
         loads.append(pltpu.make_async_copy(points_ref.at[part, :], points.at[part, :], in_sems.at[k + 1]))
     for load in loads:
         load.start()
     loads[0].wait()
     index = index_column(lists[...], flat_parts(0, total, peers, slots, straight, True))
+    half = rows // 2
     stores = []
-    for c, at in enumerate(range(0, total, chunk)):
-        acc = None
-        for k, start in enumerate(range(0, rows, chunk)):
-            if c == 0:
-                loads[k + 1].wait()
-            picks = onehot(index[at : at + chunk, :] == iota((chunk, chunk), 1) + start)
-            term = dot(picks, points[start : start + chunk, :])
-            acc = term if acc is None else acc + term
-        picked[at : at + chunk, :] = acc.astype(jnp.bfloat16)
-        part = pl.ds(at, chunk)
-        stores.append(pltpu.make_async_copy(picked.at[part, :], out_ref.at[part, :], out_sems.at[c]))
-        stores[-1].start()
+    for h in range(2):
+        loads[1 + 2 * h].wait()
+        loads[2 + 2 * h].wait()
+        for c, at in enumerate(range(0, total, chunk)):
+            picks = onehot(index[at : at + chunk, :] == iota((chunk, half), 1) + h * half)
+            term = dot(picks, points[h * half : (h + 1) * half, :])
+            if h == 0:
+                first[at : at + chunk, :] = term
+                continue
+            picked[at : at + chunk, :] = (first[at : at + chunk, :] + term).astype(jnp.bfloat16)
+            part = pl.ds(at, chunk)
+            stores.append(pltpu.make_async_copy(picked.at[part, :], out_ref.at[part, :], out_sems.at[c]))
+            stores[-1].start()
     for store in stores:
         store.wait()
 
 
 def gather_new(points, lists, peers, slots):
-    total, chunk = peers * slots, 256
+    total, chunk = peers * slots, 128
     rows, features = points.shape
     hbm = pl.BlockSpec(memory_space=pltpu.HBM)
     return pl.pallas_call(
@@ -107,7 +113,8 @@
             pltpu.VMEM((rows, features), jnp.bfloat16),
             pltpu.VMEM(lists.shape, jnp.int32),
             pltpu.VMEM((total, features), jnp.bfloat16),
-            pltpu.SemaphoreType.DMA((rows // chunk + 1,)),
+            pltpu.VMEM((total, features), jnp.float32),
+            pltpu.SemaphoreType.DMA((5,)),
             pltpu.SemaphoreType.DMA((total // chunk,)),
         ],
         compiler_params=pltpu.CompilerParams(vmem_limit_bytes=VMEM_LIMIT),
@@ -307,16 +314,7 @@
     lax.fori_loop(0, dist_ref.shape[1] // LANES, block, 0)
 
 
-def ready_kernel(old_lists_ref, old_back_ref, new_lists_ref, best_ref, wide_ref):
-    best = jnp.full(best_ref.shape, cap_value, jnp.float32)
-    old_back = old_back_ref[...].reshape(old_lists_ref.shape).astype(jnp.float32)
-    peers, slots = old_lists_ref.shape
-    for c in range(slots):
-        for at in range(0, peers, SUBLANES):
-            index = old_lists_ref[at : at + SUBLANES, c : c + 1]
-            value = old_back[at : at + SUBLANES, c : c + 1]
-            best = jnp.where(index == iota(best.shape, 1), jnp.minimum(best, value), best)
-    best_ref[...] = best
+def wide_kernel(new_lists_ref, old_lists_ref, new_wide_ref, old_wide_ref):
     slots, peers = new_lists_ref.shape
     same = onehot(iota((slots, slots), 0) == iota((slots, slots), 1))
 
@@ -325,22 +323,37 @@
             values.astype(jnp.bfloat16), same, (((0,), (0,)), ((), ())), preferred_element_type=jnp.float32
         ).astype(jnp.int32)
 
-    lists = upright(new_lists_ref[...] // 32) * 32 + upright(new_lists_ref[...] % 32)
-    for c in range(slots):
-        wide_ref[c * peers : (c + 1) * peers, :] = jnp.broadcast_to(lists[:, c : c + 1], (peers, LANES))
-
-
-def reverse_kernel(back_ref, best_ref, wide_ref, out_ref):
+    new_lists = upright(new_lists_ref[...] // 32) * 32 + upright(new_lists_ref[...] % 32)
+    for lists, wide_ref in ((new_lists, new_wide_ref), (old_lists_ref[...], old_wide_ref)):
+        peers, slots = lists.shape
+        for c in range(slots):
+            wide_ref[c * peers : (c + 1) * peers, :] = jnp.broadcast_to(lists[:, c : c + 1], (peers, LANES))
+
+
+def fold(best, back_ref, wide_ref):
     peers, _, slots = back_ref.shape
-    back = back_ref[...].reshape(peers, slots).astype(jnp.float32)
+    total = peers * slots
+    of_peer = onehot(iota((total, peers), 1) == iota((total, peers), 0) % peers)
+    rows = dot(of_peer, back_ref[...].reshape(peers, slots))
+    chosen = jnp.where(iota((total, slots), 1) == iota((total, slots), 0) // peers, rows, 0.0)
+    values = dot(chosen.astype(jnp.bfloat16), jnp.ones((slots, LANES), jnp.bfloat16))
     lane = iota((SUBLANES, LANES), 1)
-    best = [best_ref[:, LANES * k : LANES * (k + 1)] for k in range(SUBLANES)]
-    for c in range(slots):
-        for at in range(0, peers, SUBLANES):
-            index = wide_ref[c * peers + at : c * peers + at + SUBLANES, :]
-            value = back[at : at + SUBLANES, c : c + 1]
-            for k in range(SUBLANES):
-                best[k] = jnp.minimum(best[k], jnp.where(index == lane + k * LANES, value, cap_value))
+    best = list(best)
+    for at in range(0, total, SUBLANES):
+        index, value = wide_ref[at : at + SUBLANES, :], values[at : at + SUBLANES, :]
+        for k in range(SUBLANES):
+            best[k] = jnp.minimum(best[k], jnp.where(index == lane + k * LANES, value, cap_value))
+    return best
+
+
+def fold_new_kernel(back_ref, wide_ref, best_ref):
+    best = fold([jnp.full((SUBLANES, LANES), cap_value, jnp.float32)] * SUBLANES, back_ref, wide_ref)
+    for k in range(SUBLANES):
+        best_ref[:, k * LANES : (k + 1) * LANES] = best[k]
+
+
+def reverse_kernel(back_ref, wide_ref, best_ref, out_ref):
+    best = fold([best_ref[:, k * LANES : (k + 1) * LANES] for k in range(SUBLANES)], back_ref, wide_ref)
     for k in range(SUBLANES):
         out_ref[k : k + 1, :] = jnp.min(best[k], axis=0, keepdims=True)
 
@@ -404,9 +417,6 @@
         cost_estimate=old_cost,
     )(odds, points, own_sq, counts_old, minima_even, place)
 
-    pulled_new, minima_old = lax.optimization_barrier((pulled_new, minima_old))
-    back_old = lax.all_to_all(minima_old, "grp", split_axis=0, concat_axis=0, tiled=True)
-
     total_new = peers * slots
     minima_new = pl.pallas_call(
         functools.partial(minima_kernel, peers, slots),
@@ -416,9 +426,17 @@
             flops=2 * total_new * rows * features, bytes_accessed=4 * total_new * features, transcendentals=0
         ),
     )(pulled_new, points, own_sq, counts_new)
+
+    odds, wait_lists, minima_new = lax.optimization_barrier((odds, lists_new, minima_new))
     back_new = lax.all_to_all(minima_new, "shard", split_axis=0, concat_axis=0, tiled=True)
-
-    odds, _ = lax.optimization_barrier((odds, pulled_new))
+    wide_new, wide_old = pl.pallas_call(
+        wide_kernel,
+        out_shape=(
+            jax.ShapeDtypeStruct((total_new, LANES), jnp.int32),
+            jax.ShapeDtypeStruct((groups * group_slots, LANES), jnp.int32),
+        ),
+        compiler_params=params,
+    )(wait_lists, serve_old)
     hbm = pl.BlockSpec(memory_space=pltpu.HBM)
     held = pl.pallas_call(
         functools.partial(odd_kernel, groups, group_slots),
@@ -432,7 +450,8 @@
         compiler_params=params,
         cost_estimate=old_cost,
     )(odds, points, own_sq, counts_old, place, pltpu.with_memory_space_constraint(held, pltpu.HBM))
-    pulled_new, back_old, _ = lax.optimization_barrier((pulled_new, back_old, minima_new))
+    pulled_new, minima_old, back_new = lax.optimization_barrier((pulled_new, minima_old, back_new))
+    back_old = lax.all_to_all(minima_old, "grp", split_axis=0, concat_axis=0, tiled=True)
     nearest = pl.pallas_call(
         functools.partial(select_kernel, peers, slots, 256),
         in_specs=[vmem] * 4 + [hbm],
@@ -448,20 +467,16 @@
         ),
     )(pulled_new, points, own_sq, counts_new, pltpu.with_memory_space_constraint(held, pltpu.HBM))
 
-    nearest, back_old = lax.optimization_barrier((nearest, back_old))
-    best, wide = pl.pallas_call(
-        ready_kernel,
-        out_shape=(
-            jax.ShapeDtypeStruct((SUBLANES, rows), jnp.float32),
-            jax.ShapeDtypeStruct((total_new, LANES), jnp.int32),
-        ),
-        compiler_params=params,
-    )(serve_old, back_old, lists_new)
+    best = pl.pallas_call(
+        fold_new_kernel,
+        out_shape=jax.ShapeDtypeStruct((SUBLANES, rows), jnp.float32),
+        compiler_params=params,
+    )(back_new, wide_new)
     reverse = pl.pallas_call(
         reverse_kernel,
         out_shape=jax.ShapeDtypeStruct((SUBLANES, LANES), jnp.float32),
         compiler_params=params,
-    )(back_new, best, wide)
+    )(back_old, wide_old, best)
     return nearest.T, reverse.reshape(rows)
 
 

time: 104 us -> 107 us (1.029)
  waiting for transfers between devices: 10 us -> 12.4 us
  starting transfers between devices: 70.4 us -> 71.8 us
    all_to_all x1, starting transfers between devices: 7.13 us -> 12.1 us  [body(): lax.all_to_all(minima_new, 'shard', split_axis=0, concat_axis=0, tiled=True)]
    all_to_all x1, starting transfers between devices: 11.8 us -> 8.16 us  [body(): lax.all_to_all(minima_old, 'grp', split_axis=0, concat_axis=0, tiled=True)]
    all_to_all x1, waiting for transfers between devices: 4.76 us -> 7.68 us  [body(): lax.all_to_all(minima_new, 'shard', split_axis=0, concat_axis=0, tiled=True)]
  transfers between devices with their start and end apart: 11 -> 11, of which waited for: 3 -> 3; matrix products, arithmetic and copies ran while one was open for 0% -> 0% of each run, Pallas kernels for 16% -> 13%
where the time goes in v8:
time: 107 us; the launch traced here: 106 us
  starting transfers between devices  71.8 us (67%)
  Pallas kernels  20.8 us (19%)
  waiting for transfers between devices  12.4 us (12%)
    ppermute x7, starting transfers between devices, body(): came = [lax.ppermute(pieces[k], 'grp', apart(groups, 2 * k)) for k in order]  25.5 us
    all_to_all x1, starting transfers between devices, body(): lax.all_to_all(offered_new.reshape(peers, slots, features), 'shard', spli...  19 us
    all_to_all x1, starting transfers between devices, body(): lax.all_to_all(minima_new, 'shard', split_axis=0, concat_axis=0, tiled=True)  12.1 us
    all_to_all x1, starting transfers between devices, body(): lax.all_to_all(minima_old, 'grp', split_axis=0, concat_axis=0, tiled=True)  8.16 us
    all_to_all x1, waiting for transfers between devices, body(): lax.all_to_all(minima_new, 'shard', split_axis=0, concat_axis=0, tiled=True)  7.68 us
    ppermute x1, starting transfers between devices, body(): odds = lax.ppermute(handed, 'grp', apart(groups, 1))  7.05 us
    pallas_call x1, Pallas kernels, body(): pl.pallas_call(functools.partial(select_kernel, peers, slots, 256), in_sp...  5.11 us
    ppermute x7, waiting for transfers between devices, body(): came = [lax.ppermute(pieces[k], 'grp', apart(groups, 2 * k)) for k in order]  3.5 us
  transfers between devices with their start and end apart: 11, of which 3 were waited for; matrix products, arithmetic and copies ran while one was open for 0% of the time, Pallas kernels for 13%

profile of v8, /device:TPU:1, one launch (start us, length us, event | category | flops | bytes accessed | tf_op | source)
XLA Modules:
  0.0 106.2 jit_solution(18393341254385556082)
XLA Ops:
  0.6 3.4 %shard_map.68 = bf16[768,768]{1,0:T(8,128)(2,1)} custom-call(bf16[1024,768]{1,0:T(8,128)(2,1)} %points_ref.13, s32[16,48]{1,0:T(8,128)} %bitcast.16), custom_call_target="tpu_custom_call" | custom-call | flops 1207959552 | bytes 2752512 | tf_op jit(solution)/shard_map/pallas_call | solution.py:107
  4.0 0.0 copy-start
  4.0 0.0 copy-start.2
  4.1 19.0 %all-to-all-start = ((bf16[48,16,768]{2,1,0:T(8,128)(2,1)}), bf16[48,16,768]{2,1,0:T(8,128)(2,1)S(1)}, u32[]{:S(2)}, u32[]{:S(2)}) async-start(bf16[48,16,768]{2,1,0:T(8,128)(2,1)} %bitcast.23), calls=%async_computation | async-start | bytes 2359296 | tf_op jit(solution)/shard_map/all_to_all | solution.py:377
  23.0 0.0 copy-done
  23.0 0.0 copy-done.2
  23.1 1.4 %shard_map.69 = (bf16[64,768]{1,0:T(8,128)(2,1)S(1)}, bf16[64,768]{1,0:T(8,128)(2,1)S(1)}, bf16[64,768]{1,0:T(8,128)(2,1)S(1)}, bf16[64,768]{1,0:T(8,128)(2,1)S(...) custom-call(bf16[1024,768]{1,0:T(8,128)(2,1)S(1)} %copy-done, ...), custom_call_target="tpu_custom_call" | custom-call | flops 805306368 | bytes 2359296 | tf_op jit(solution)/shard_map/pallas_call | solution.py:142
  24.5 0.0 copy-start.3
  24.5 7.5 %collective-permute-start = (bf16[64,768]{1,0:T(8,128)(2,1)S(1)}, bf16[64,768]{1,0:T(8,128)(2,1)S(1)}, u32[]{:S(2)}, u32[]{:S(2)}) collective-permute-start(bf16[64,768]{1,0:T(8,128)(2,1)S(1)} %get-tuple-element.24), channel_id=1, source_target_pairs={{0,384},{48,432},{96,480},{144,528},{192,576},{240,624},{288,672},... | collective-permute-start | bytes 294920 | tf_op jit(solution)/shard_map/ppermute | solution.py:384
  32.0 2.4 %collective-permute-start.1 = (bf16[64,768]{1,0:T(8,128)(2,1)S(1)}, bf16[64,768]{1,0:T(8,128)(2,1)S(1)}, u32[]{:S(2)}, u32[]{:S(2)}) collective-permute-start(bf16[64,768]{1,0:T(8,128)(2,1)S(1)} %get-tuple-element.25), channel_id=1, source_target_pairs={{0,192},{48,240},{96,288},{144,336},{192,0},{240,48},{288,96},{336... | collective-permute-start | bytes 294920 | tf_op jit(solution)/shard_map/ppermute | solution.py:384
  34.4 1.9 %collective-permute-start.2 = (bf16[64,768]{1,0:T(8,128)(2,1)S(1)}, bf16[64,768]{1,0:T(8,128)(2,1)S(1)}, u32[]{:S(2)}, u32[]{:S(2)}) collective-permute-start(bf16[64,768]{1,0:T(8,128)(2,1)S(1)} %get-tuple-element.26), channel_id=1, source_target_pairs={{0,576},{48,624},{96,672},{144,720},{192,384},{240,432},{288,480},... | collective-permute-start | bytes 294920 | tf_op jit(solution)/shard_map/ppermute | solution.py:384
  36.4 4.8 %collective-permute-start.3 = (bf16[64,768]{1,0:T(8,128)(2,1)S(1)}, bf16[64,768]{1,0:T(8,128)(2,1)S(1)}, u32[]{:S(2)}, u32[]{:S(2)}) collective-permute-start(bf16[64,768]{1,0:T(8,128)(2,1)S(1)} %get-tuple-element.27), channel_id=1, source_target_pairs={{0,288},{48,336},{96,192},{144,240},{192,96},{240,144},{288,0},{33... | collective-permute-start | bytes 294920 | tf_op jit(solution)/shard_map/ppermute | solution.py:384
  41.2 4.4 %collective-permute-start.4 = (bf16[64,768]{1,0:T(8,128)(2,1)S(1)}, bf16[64,768]{1,0:T(8,128)(2,1)S(1)}, u32[]{:S(2)}, u32[]{:S(2)}) collective-permute-start(bf16[64,768]{1,0:T(8,128)(2,1)S(1)} %get-tuple-element.28), channel_id=1, source_target_pairs={{0,672},{48,720},{96,576},{144,624},{192,480},{240,528},{288,384},... | collective-permute-start | bytes 294920 | tf_op jit(solution)/shard_map/ppermute | solution.py:384
  45.6 0.0 collective-permute-done.refs_0_
  45.6 1.9 %collective-permute-start.5 = (bf16[64,768]{1,0:T(8,128)(2,1)S(1)}, bf16[64,768]{1,0:T(8,128)(2,1)S(1)}, u32[]{:S(2)}, u32[]{:S(2)}) collective-permute-start(bf16[64,768]{1,0:T(8,128)(2,1)S(1)} %get-tuple-element.29), channel_id=1, source_target_pairs={{0,480},{48,528},{96,384},{144,432},{192,672},{240,720},{288,576},... | collective-permute-start | bytes 294920 | tf_op jit(solution)/shard_map/ppermute | solution.py:384
  47.5 0.0 collective-permute-done.1.refs_1_
  47.6 2.5 %collective-permute-start.6 = (bf16[64,768]{1,0:T(8,128)(2,1)S(1)}, bf16[64,768]{1,0:T(8,128)(2,1)S(1)}, u32[]{:S(2)}, u32[]{:S(2)}) collective-permute-start(bf16[64,768]{1,0:T(8,128)(2,1)S(1)} %get-tuple-element.30), channel_id=1, source_target_pairs={{0,96},{48,144},{96,0},{144,48},{192,288},{240,336},{288,192},{336... | collective-permute-start | bytes 294920 | tf_op jit(solution)/shard_map/ppermute | solution.py:384
  50.1 0.4 multiply_reduce_fusion
  50.5 0.0 collective-permute-done.2.refs_2_
  50.5 0.0 collective-permute-done.3.refs_3_
  50.5 0.0 collective-permute-done.4.refs_4_
  50.5 3.5 %collective-permute-done.5.refs_5_ = bf16[64,768]{1,0:T(8,128)(2,1)S(1)} collective-permute-done((bf16[64,768]{1,0:T(8,128)(2,1)S(1)}, bf16[64,768]{1,0:T(8,128)(2,1)S(1)}, u32[]{:S(2)}, u32[]{:S(2)}) %collective-permute-start.5) | collective-permute-done | bytes 98336 | tf_op jit(solution)/shard_map/ppermute | solution.py:384
  54.0 0.0 collective-permute-done.6.refs_6_
  54.0 0.1 shard_map.70
  54.0 7.0 %collective-permute-start.7 = (bf16[256,768]{1,0:T(8,128)(2,1)S(1)}, bf16[256,768]{1,0:T(8,128)(2,1)S(1)}, u32[]{:S(2)}, u32[]{:S(2)}) collective-permute-start(bf16[256,768]{1,0:T(8,128)(2,1)S(1)} %get-tuple-element.33), channel_id=1, source_target_pairs={{0,48},{48,0},{96,144},{144,96},{192,240},{240,192},{288,336},{336... | collective-permute-start | bytes 1179656 | tf_op jit(solution)/shard_map/ppermute | solution.py:395
  61.1 0.0 copy-done.3
  61.1 0.0 copy-start.4
  61.1 2.0 %shard_map.71 = (f32[8,32]{1,0:T(8,128)S(1)}, f32[128,1024]{1,0:T(8,128)}) custom-call(bf16[256,768]{1,0:T(8,128)(2,1)S(1)} %get-tuple-element.35.cand_ref, bf16[1024,768]{1,0:T(8,128)(2,1)S(1)} %copy-done, f32[1,1024]{1,0:T(1,128)S(1)} %bitcast.11, s32[1,16]{1,0:T(1,128)S(1)} %bitcast.18, s32[1]{0:T(128)} %bitcast.3.place_ref), custom_call_target="tpu_custom_call" | custom-call | flops 402653184 | bytes 1966080 | tf_op jit(solution)/shard_map/pallas_call | solution.py:401
  63.1 0.0 collective-permute-done.7.cand_ref
  63.1 1.3 %shard_map.72 = bf16[16,1,32]{2,1,0:T(2,128)(2,1)} custom-call(bf16[256,768]{1,0:T(8,128)(2,1)S(1)} %collective-permute-done.7.cand_ref, bf16[1024,768]{1,0:T(8,128)(2,1)S(1)} %copy-done, f32[1,1024]{1,0:T(1,128)S(1)} %bitcast.12, s32[1,16]{1,0:T(1,128)S(1)} %bitcast.19, f32[8,32]{1,0:T(8,128)S(1)} %get-tuple-element.36.rows_ref, s32[1]{0:T(128)} %bitcast.3.place_ref), custom_call_target="tpu_custom_call" | custom-call | flops 402653184 | bytes 1966080 | tf_op jit(solution)/shard_map/pallas_call | solution.py:412
  64.4 0.0 all-to-all-done
  64.4 0.0 copy-done.4
  64.4 2.3 %shard_map.73 = bf16[48,1,16]{2,1,0:T(2,128)(2,1)} custom-call(bf16[768,768]{1,0:T(8,128)(2,1)S(1)} %bitcast.9, bf16[1024,768]{1,0:T(8,128)(2,1)S(1)} %copy-done, f32[1,1024]{1,0:T(1,128)S(1)} %bitcast.13, s32[1,48]{1,0:T(1,128)S(1)} %bitcast.21), custom_call_target="tpu_custom_call" | custom-call | flops 1207959552 | bytes 2359296 | tf_op jit(solution)/shard_map/pallas_call | solution.py:421
  66.7 0.0 copy-start.1
  66.7 12.1 %all-to-all-start.1 = ((bf16[48,1,16]{2,1,0:T(2,128)(2,1)}), bf16[48,1,16]{2,1,0:T(2,128)(2,1)S(1)}, u32[]{:S(2)}, u32[]{:S(2)}) async-start(bf16[48,1,16]{2,1,0:T(2,128)(2,1)} %shard_map.73), calls=%async_computation.1 | async-start | bytes 49152 | tf_op jit(solution)/shard_map/all_to_all | solution.py:431
  78.8 2.9 %shard_map.74.held_hbm_ref = f32[128,1024]{1,0:T(8,128)} custom-call(bf16[256,768]{1,0:T(8,128)(2,1)S(1)} %collective-permute-done.7.cand_ref, bf16[1024,768]{1,0:T(8,128)(2,1)S(1)} %copy-done, f32[1,1024]{1,0:T(1,128)S(1)} %bitcast.14, s32[1,16]{1,0:T(1,128)S(1)} %bitcast.20, s32[1]{0:T(128)} %bitcast.3.place_ref, f32[128,1024]{1,0:T(8,128)} %get-tuple-element.40.before_hbm_ref), custom_call_target="tpu_custom_call" | custom-call | flops 402653184 | bytes 1966080 | tf_op jit(solution)/shard_map/pallas_call | solution.py:441
  81.7 0.0 copy-done.1
  81.8 0.5 shard_map.76
  82.2 7.7 %all-to-all-done.1.back_ref = bf16[48,1,16]{2,1,0:T(2,128)(2,1)S(1)} async-done(((bf16[48,1,16]{2,1,0:T(2,128)(2,1)}), bf16[48,1,16]{2,1,0:T(2,128)(2,1)S(1)}, u32[]{:S(2)}, u32[]{:S(2)}) %all-to-all-start.1) | async-done | bytes 1568 | tf_op jit(solution)/shard_map/all_to_all | solution.py:431
  89.9 8.2 %all-to-all-start.2 = ((bf16[16,1,32]{2,1,0:T(2,128)(2,1)}), bf16[16,1,32]{2,1,0:T(2,128)(2,1)S(1)}, u32[]{:S(2)}, u32[]{:S(2)}) async-start(bf16[16,1,32]{2,1,0:T(2,128)(2,1)} %shard_map.72), calls=%async_computation.2 | async-start | bytes 16384 | tf_op jit(solution)/shard_map/all_to_all | solution.py:454
  98.0 5.1 %shard_map.75 = f32[16,1024]{1,0:T(8,128)} custom-call(bf16[768,768]{1,0:T(8,128)(2,1)S(1)} %bitcast.10, bf16[1024,768]{1,0:T(8,128)(2,1)S(1)} %copy-done, f32[1,1024]{1,0:T(1,128)S(1)} %bitcast.15, s32[1,48]{1,0:T(1,128)S(1)} %bitcast.22, f32[128,1024]{1,0:T(8,128)} %shard_map.74.held_hbm_ref), custom_call_target="tpu_custom_call" | custom-call | flops 2415919104 | bytes 2359296 | tf_op jit(solution)/shard_map/pallas_call | solution.py:455
  103.2 0.7 shard_map.77.best_ref
  103.9 1.1 %all-to-all-done.2.back_ref = bf16[16,1,32]{2,1,0:T(2,128)(2,1)S(1)} async-done(((bf16[16,1,32]{2,1,0:T(2,128)(2,1)}), bf16[16,1,32]{2,1,0:T(2,128)(2,1)S(1)}, u32[]{:S(2)}, u32[]{:S(2)}) %all-to-all-start.2) | async-done | bytes 1056 | tf_op jit(solution)/shard_map/all_to_all | solution.py:454
  105.1 1.1 %shard_map.78 = f32[8,128]{1,0:T(8,128)} custom-call(bf16[16,1,32]{2,1,0:T(2,128)(2,1)S(1)} %all-to-all-done.2.back_ref, s32[512,128]{1,0:T(8,128)S(1)} %get-tuple-element.43.wide_ref, f32[8,1024]{1,0:T(8,128)S(1)} %shard_map.77.best_ref), custom_call_target="tpu_custom_call" | custom-call | tf_op jit(solution)/shard_map/pallas_call | solution.py:475
Async XLA Ops:
  4.0 19.0 %copy-start = (bf16[1024,768]{1,0:T(8,128)(2,1)S(1)}, bf16[1024,768]{1,0:T(8,128)(2,1)}, u32[]{:S(2)}) copy-start(bf16[1024,768]{1,0:T(8,128)(2,1)} %points_ref.13) | copy-start | bytes 4718596
  4.0 19.0 %copy-start.2 = (s32[16,32]{1,0:T(8,128)S(1)}, s32[16,32]{1,0:T(8,128)}, u32[]{:S(2)}) copy-start(s32[16,32]{1,0:T(8,128)} %old_lists_ref.1) | copy-start | bytes 6148
  4.1 60.4 %all-to-all-start = ((bf16[48,16,768]{2,1,0:T(8,128)(2,1)}), bf16[48,16,768]{2,1,0:T(8,128)(2,1)S(1)}, u32[]{:S(2)}, u32[]{:S(2)}) async-start(bf16[48,16,768]{2,1,0:T(8,128)(2,1)} %bitcast.23), calls=%async_computation | async-start | bytes 2359296 | tf_op jit(solution)/shard_map/all_to_all | solution.py:377
  24.5 36.6 %copy-start.3 = (s32[16,1]{0,1:T(1,128)S(1)}, s32[16,1]{0,1:T(1,128)}, u32[]{:S(2)}) copy-start(s32[16,1]{0,1:T(1,128)} %param.9) | copy-start | bytes 196
  24.5 21.1 %collective-permute-start = (bf16[64,768]{1,0:T(8,128)(2,1)S(1)}, bf16[64,768]{1,0:T(8,128)(2,1)S(1)}, u32[]{:S(2)}, u32[]{:S(2)}) collective-permute-start(bf16[64,768]{1,0:T(8,128)(2,1)S(1)} %get-tuple-element.24), channel_id=1, source_target_pairs={{0,384},{48,432},{96,480},{144,528},{192,576},{240,624},{288,672},... | collective-permute-start | bytes 294920 | tf_op jit(solution)/shard_map/ppermute | solution.py:384
  32.0 15.5 %collective-permute-start.1 = (bf16[64,768]{1,0:T(8,128)(2,1)S(1)}, bf16[64,768]{1,0:T(8,128)(2,1)S(1)}, u32[]{:S(2)}, u32[]{:S(2)}) collective-permute-start(bf16[64,768]{1,0:T(8,128)(2,1)S(1)} %get-tuple-element.25), channel_id=1, source_target_pairs={{0,192},{48,240},{96,288},{144,336},{192,0},{240,48},{288,96},{336... | collective-permute-start | bytes 294920 | tf_op jit(solution)/shard_map/ppermute | solution.py:384
  34.4 16.0 %collective-permute-start.2 = (bf16[64,768]{1,0:T(8,128)(2,1)S(1)}, bf16[64,768]{1,0:T(8,128)(2,1)S(1)}, u32[]{:S(2)}, u32[]{:S(2)}) collective-permute-start(bf16[64,768]{1,0:T(8,128)(2,1)S(1)} %get-tuple-element.26), channel_id=1, source_target_pairs={{0,576},{48,624},{96,672},{144,720},{192,384},{240,432},{288,480},... | collective-permute-start | bytes 294920 | tf_op jit(solution)/shard_map/ppermute | solution.py:384
  36.4 14.1 %collective-permute-start.3 = (bf16[64,768]{1,0:T(8,128)(2,1)S(1)}, bf16[64,768]{1,0:T(8,128)(2,1)S(1)}, u32[]{:S(2)}, u32[]{:S(2)}) collective-permute-start(bf16[64,768]{1,0:T(8,128)(2,1)S(1)} %get-tuple-element.27), channel_id=1, source_target_pairs={{0,288},{48,336},{96,192},{144,240},{192,96},{240,144},{288,0},{33... | collective-permute-start | bytes 294920 | tf_op jit(solution)/shard_map/ppermute | solution.py:384
  41.2 9.3 %collective-permute-start.4 = (bf16[64,768]{1,0:T(8,128)(2,1)S(1)}, bf16[64,768]{1,0:T(8,128)(2,1)S(1)}, u32[]{:S(2)}, u32[]{:S(2)}) collective-permute-start(bf16[64,768]{1,0:T(8,128)(2,1)S(1)} %get-tuple-element.28), channel_id=1, source_target_pairs={{0,672},{48,720},{96,576},{144,624},{192,480},{240,528},{288,384},... | collective-permute-start | bytes 294920 | tf_op jit(solution)/shard_map/ppermute | solution.py:384
  45.6 8.4 %collective-permute-start.5 = (bf16[64,768]{1,0:T(8,128)(2,1)S(1)}, bf16[64,768]{1,0:T(8,128)(2,1)S(1)}, u32[]{:S(2)}, u32[]{:S(2)}) collective-permute-start(bf16[64,768]{1,0:T(8,128)(2,1)S(1)} %get-tuple-element.29), channel_id=1, source_target_pairs={{0,480},{48,528},{96,384},{144,432},{192,672},{240,720},{288,576},... | collective-permute-start | bytes 294920 | tf_op jit(solution)/shard_map/ppermute | solution.py:384
  47.6 6.4 %collective-permute-start.6 = (bf16[64,768]{1,0:T(8,128)(2,1)S(1)}, bf16[64,768]{1,0:T(8,128)(2,1)S(1)}, u32[]{:S(2)}, u32[]{:S(2)}) collective-permute-start(bf16[64,768]{1,0:T(8,128)(2,1)S(1)} %get-tuple-element.30), channel_id=1, source_target_pairs={{0,96},{48,144},{96,0},{144,48},{192,288},{240,336},{288,192},{336... | collective-permute-start | bytes 294920 | tf_op jit(solution)/shard_map/ppermute | solution.py:384
  54.0 9.1 %collective-permute-start.7 = (bf16[256,768]{1,0:T(8,128)(2,1)S(1)}, bf16[256,768]{1,0:T(8,128)(2,1)S(1)}, u32[]{:S(2)}, u32[]{:S(2)}) collective-permute-start(bf16[256,768]{1,0:T(8,128)(2,1)S(1)} %get-tuple-element.33), channel_id=1, source_target_pairs={{0,48},{48,0},{96,144},{144,96},{192,240},{240,192},{288,336},{336... | collective-permute-start | bytes 1179656 | tf_op jit(solution)/shard_map/ppermute | solution.py:395
  61.1 3.3 %copy-start.4 = (s32[48,1]{0,1:T(1,128)S(1)}, s32[48,1]{0,1:T(1,128)}, u32[]{:S(2)}) copy-start(s32[48,1]{0,1:T(1,128)} %param.8) | copy-start | bytes 580
  66.7 15.1 %copy-start.1 = (s32[48,16]{0,1:T(8,128)S(1)}, s32[48,16]{0,1:T(8,128)}, u32[]{:S(2)}) copy-start(s32[48,16]{0,1:T(8,128)} %param.6) | copy-start | bytes 9220
  66.7 23.2 %all-to-all-start.1 = ((bf16[48,1,16]{2,1,0:T(2,128)(2,1)}), bf16[48,1,16]{2,1,0:T(2,128)(2,1)S(1)}, u32[]{:S(2)}, u32[]{:S(2)}) async-start(bf16[48,1,16]{2,1,0:T(2,128)(2,1)} %shard_map.73), calls=%async_computation.1 | async-start | bytes 49152 | tf_op jit(solution)/shard_map/all_to_all | solution.py:431
  89.9 15.2 %all-to-all-start.2 = ((bf16[16,1,32]{2,1,0:T(2,128)(2,1)}), bf16[16,1,32]{2,1,0:T(2,128)(2,1)S(1)}, u32[]{:S(2)}, u32[]{:S(2)}) async-start(bf16[16,1,32]{2,1,0:T(2,128)(2,1)} %shard_map.72), calls=%async_computation.2 | async-start | bytes 16384 | tf_op jit(solution)/shard_map/all_to_all | solution.py:454

commit v9 on v8

--- a/solution.py
+++ b/solution.py
@@ -54,11 +54,6 @@
 
 def straight(block):
     return block
-
-
-def column(rows_of, lane_of, values):
-    picked = dot(onehot(rows_of), values)
-    return jnp.sum(jnp.where(lane_of, picked, 0.0), axis=1, keepdims=True)
 
 
 def index_column(lists, parts):
@@ -257,25 +252,21 @@
     hold(dist_ref, None, held_ref)
 
 
-def minima_old_kernel(groups, slots, cand_ref, points_ref, own_sq_ref, counts_ref, rows_ref, place_ref, minima_ref):
+def odd_kernel(
+    groups, slots, cand_ref, points_ref, own_sq_ref, counts_ref, rows_ref, place_ref, before_hbm_ref,
+    minima_ref, held_ref, dist_ref, before_ref, sem,
+):
+    fetch = pltpu.make_async_copy(before_hbm_ref, before_ref, sem)
+    fetch.start()
     count = groups // 2
     order = source_of(count, place_ref)
     usable = usable_slots(counts_ref, count * slots, count * slots, groups, slots, order)
-    minima = jnp.where(usable, least_distances(cand_ref[...], points_ref, own_sq_ref), cap_value)
+    dist = distances(cand_ref[...], points_ref, own_sq_ref)
+    dist_ref[...] = jnp.where(usable, dist, far_value)
+    minima = jnp.where(usable, jnp.min(dist, axis=1, keepdims=True), cap_value)
     for k, row in enumerate(slot_rows(minima, slots)):
         minima_ref[order(k)] = rows_ref[k : k + 1, :].astype(jnp.bfloat16)
         minima_ref[order(count + k)] = row.astype(jnp.bfloat16)
-
-
-def odd_kernel(
-    groups, slots, cand_ref, points_ref, own_sq_ref, counts_ref, place_ref, before_hbm_ref, held_ref,
-    dist_ref, before_ref, sem,
-):
-    fetch = pltpu.make_async_copy(before_hbm_ref, before_ref, sem)
-    fetch.start()
-    half = groups // 2 * slots
-    usable = usable_slots(counts_ref, half, half, groups, slots, source_of(groups // 2, place_ref))
-    dist_ref[...] = jnp.where(usable, distances(cand_ref[...], points_ref, own_sq_ref), far_value)
     fetch.wait()
     hold(dist_ref, before_ref, held_ref)
 
@@ -314,7 +305,16 @@
     lax.fori_loop(0, dist_ref.shape[1] // LANES, block, 0)
 
 
-def wide_kernel(new_lists_ref, old_lists_ref, new_wide_ref, old_wide_ref):
+def ready_kernel(old_lists_ref, old_back_ref, new_lists_ref, best_ref, wide_ref):
+    best = jnp.full(best_ref.shape, cap_value, jnp.float32)
+    old_back = old_back_ref[...].reshape(old_lists_ref.shape).astype(jnp.float32)
+    peers, slots = old_lists_ref.shape
+    for c in range(slots):
+        for at in range(0, peers, SUBLANES):
+            index = old_lists_ref[at : at + SUBLANES, c : c + 1]
+            value = old_back[at : at + SUBLANES, c : c + 1]
+            best = jnp.where(index == iota(best.shape, 1), jnp.minimum(best, value), best)
+    best_ref[...] = best
     slots, peers = new_lists_ref.shape
     same = onehot(iota((slots, slots), 0) == iota((slots, slots), 1))
 
@@ -323,14 +323,12 @@
             values.astype(jnp.bfloat16), same, (((0,), (0,)), ((), ())), preferred_element_type=jnp.float32
         ).astype(jnp.int32)
 
-    new_lists = upright(new_lists_ref[...] // 32) * 32 + upright(new_lists_ref[...] % 32)
-    for lists, wide_ref in ((new_lists, new_wide_ref), (old_lists_ref[...], old_wide_ref)):
-        peers, slots = lists.shape
-        for c in range(slots):
-            wide_ref[c * peers : (c + 1) * peers, :] = jnp.broadcast_to(lists[:, c : c + 1], (peers, LANES))
-
-
-def fold(best, back_ref, wide_ref):
+    lists = upright(new_lists_ref[...] // 32) * 32 + upright(new_lists_ref[...] % 32)
+    for c in range(slots):
+        wide_ref[c * peers : (c + 1) * peers, :] = jnp.broadcast_to(lists[:, c : c + 1], (peers, LANES))
+
+
+def reverse_kernel(back_ref, best_ref, wide_ref, out_ref):
     peers, _, slots = back_ref.shape
     total = peers * slots
     of_peer = onehot(iota((total, peers), 1) == iota((total, peers), 0) % peers)
@@ -338,22 +336,11 @@
     chosen = jnp.where(iota((total, slots), 1) == iota((total, slots), 0) // peers, rows, 0.0)
     values = dot(chosen.astype(jnp.bfloat16), jnp.ones((slots, LANES), jnp.bfloat16))
     lane = iota((SUBLANES, LANES), 1)
-    best = list(best)
+    best = [best_ref[:, LANES * k : LANES * (k + 1)] for k in range(SUBLANES)]
     for at in range(0, total, SUBLANES):
         index, value = wide_ref[at : at + SUBLANES, :], values[at : at + SUBLANES, :]
         for k in range(SUBLANES):
             best[k] = jnp.minimum(best[k], jnp.where(index == lane + k * LANES, value, cap_value))
-    return best
-
-
-def fold_new_kernel(back_ref, wide_ref, best_ref):
-    best = fold([jnp.full((SUBLANES, LANES), cap_value, jnp.float32)] * SUBLANES, back_ref, wide_ref)
-    for k in range(SUBLANES):
-        best_ref[:, k * LANES : (k + 1) * LANES] = best[k]
-
-
-def reverse_kernel(back_ref, wide_ref, best_ref, out_ref):
-    best = fold([best_ref[:, k * LANES : (k + 1) * LANES] for k in range(SUBLANES)], back_ref, wide_ref)
     for k in range(SUBLANES):
         out_ref[k : k + 1, :] = jnp.min(best[k], axis=0, keepdims=True)
 
@@ -409,39 +396,14 @@
         compiler_params=params,
         cost_estimate=old_cost,
     )(evens, points, own_sq, counts_old, place)
-    minima_old = pl.pallas_call(
-        functools.partial(minima_old_kernel, groups, group_slots),
-        in_specs=[vmem] * 5 + [smem],
-        out_shape=jax.ShapeDtypeStruct((groups, 1, group_slots), jnp.bfloat16),
-        compiler_params=params,
-        cost_estimate=old_cost,
-    )(odds, points, own_sq, counts_old, minima_even, place)
-
-    total_new = peers * slots
-    minima_new = pl.pallas_call(
-        functools.partial(minima_kernel, peers, slots),
-        out_shape=jax.ShapeDtypeStruct((peers, 1, slots), jnp.bfloat16),
-        compiler_params=params,
-        cost_estimate=pl.CostEstimate(
-            flops=2 * total_new * rows * features, bytes_accessed=4 * total_new * features, transcendentals=0
-        ),
-    )(pulled_new, points, own_sq, counts_new)
-
-    odds, wait_lists, minima_new = lax.optimization_barrier((odds, lists_new, minima_new))
-    back_new = lax.all_to_all(minima_new, "shard", split_axis=0, concat_axis=0, tiled=True)
-    wide_new, wide_old = pl.pallas_call(
-        wide_kernel,
+    hbm = pl.BlockSpec(memory_space=pltpu.HBM)
+    minima_old, held = pl.pallas_call(
+        functools.partial(odd_kernel, groups, group_slots),
+        in_specs=[vmem] * 5 + [smem, hbm],
         out_shape=(
-            jax.ShapeDtypeStruct((total_new, LANES), jnp.int32),
-            jax.ShapeDtypeStruct((groups * group_slots, LANES), jnp.int32),
-        ),
-        compiler_params=params,
-    )(wait_lists, serve_old)
-    hbm = pl.BlockSpec(memory_space=pltpu.HBM)
-    held = pl.pallas_call(
-        functools.partial(odd_kernel, groups, group_slots),
-        in_specs=[vmem] * 4 + [smem, hbm],
-        out_shape=pltpu.HBM(held_shape, jnp.float32),
+            jax.ShapeDtypeStruct((groups, 1, group_slots), jnp.bfloat16),
+            pltpu.HBM(held_shape, jnp.float32),
+        ),
         scratch_shapes=[
             pltpu.VMEM((half, rows), jnp.float32),
             pltpu.VMEM(held_shape, jnp.float32),
@@ -449,9 +411,23 @@
         ],
         compiler_params=params,
         cost_estimate=old_cost,
-    )(odds, points, own_sq, counts_old, place, pltpu.with_memory_space_constraint(held, pltpu.HBM))
-    pulled_new, minima_old, back_new = lax.optimization_barrier((pulled_new, minima_old, back_new))
+    )(odds, points, own_sq, counts_old, minima_even, place, pltpu.with_memory_space_constraint(held, pltpu.HBM))
+
+    pulled_new, minima_old = lax.optimization_barrier((pulled_new, minima_old))
     back_old = lax.all_to_all(minima_old, "grp", split_axis=0, concat_axis=0, tiled=True)
+
+    total_new = peers * slots
+    minima_new = pl.pallas_call(
+        functools.partial(minima_kernel, peers, slots),
+        out_shape=jax.ShapeDtypeStruct((peers, 1, slots), jnp.bfloat16),
+        compiler_params=params,
+        cost_estimate=pl.CostEstimate(
+            flops=2 * total_new * rows * features, bytes_accessed=4 * total_new * features, transcendentals=0
+        ),
+    )(pulled_new, points, own_sq, counts_new)
+    back_new = lax.all_to_all(minima_new, "shard", split_axis=0, concat_axis=0, tiled=True)
+
+    pulled_new, back_old, _ = lax.optimization_barrier((pulled_new, back_old, minima_new))
     nearest = pl.pallas_call(
         functools.partial(select_kernel, peers, slots, 256),
         in_specs=[vmem] * 4 + [hbm],
@@ -467,16 +443,20 @@
         ),
     )(pulled_new, points, own_sq, counts_new, pltpu.with_memory_space_constraint(held, pltpu.HBM))
 
-    best = pl.pallas_call(
-        fold_new_kernel,
-        out_shape=jax.ShapeDtypeStruct((SUBLANES, rows), jnp.float32),
-        compiler_params=params,
-    )(back_new, wide_new)
+    nearest, back_old = lax.optimization_barrier((nearest, back_old))
+    best, wide = pl.pallas_call(
+        ready_kernel,
+        out_shape=(
+            jax.ShapeDtypeStruct((SUBLANES, rows), jnp.float32),
+            jax.ShapeDtypeStruct((total_new, LANES), jnp.int32),
+        ),
+        compiler_params=params,
+    )(serve_old, back_old, lists_new)
     reverse = pl.pallas_call(
         reverse_kernel,
         out_shape=jax.ShapeDtypeStruct((SUBLANES, LANES), jnp.float32),
         compiler_params=params,
-    )(back_old, wide_old, best)
+    )(back_new, best, wide)
     return nearest.T, reverse.reshape(rows)
 
 

time: 107 us -> 103 us (0.963)
  starting transfers between devices: 71.8 us -> 68.3 us
    all_to_all x1, starting transfers between devices: 12.1 us -> 6.95 us  [body(): lax.all_to_all(minima_new, 'shard', split_axis=0, concat_axis=0, tiled=True)]
    all_to_all x1, waiting for transfers between devices: 1.15 us -> 4.68 us  [body(): lax.all_to_all(minima_old, 'grp', split_axis=0, concat_axis=0, tiled=True)]
    all_to_all x1, waiting for transfers between devices: 7.68 us -> 4.93 us  [body(): lax.all_to_all(minima_new, 'shard', split_axis=0, concat_axis=0, tiled=True)]
    all_to_all x1, starting transfers between devices: 8.16 us -> 9.95 us  [body(): lax.all_to_all(minima_old, 'grp', split_axis=0, concat_axis=0, tiled=True)]
    pallas_call x3 -> x1, Pallas kernels: 2.5 us -> 0.93 us  [body(): pl.pallas_call(ready_kernel, out_shape=(jax.ShapeDtypeStruct((SUBLANES, r...]
  transfers between devices with their start and end apart: 11 -> 11, of which waited for: 3 -> 3; matrix products, arithmetic and copies ran while one was open for 0% -> 0% of each run, Pallas kernels for 13% -> 15%
where the time goes in v9:
time: 103 us
  starting transfers between devices  68.3 us (66%)
  Pallas kernels  19.9 us (19%)
  waiting for transfers between devices  13.1 us (13%)
    ppermute x7, starting transfers between devices, body(): came = [lax.ppermute(pieces[k], 'grp', apart(groups, 2 * k)) for k in order]  25.5 us
    all_to_all x1, starting transfers between devices, body(): lax.all_to_all(offered_new.reshape(peers, slots, features), 'shard', spli...  19 us
    all_to_all x1, starting transfers between devices, body(): lax.all_to_all(minima_old, 'grp', split_axis=0, concat_axis=0, tiled=True)  9.95 us
    ppermute x1, starting transfers between devices, body(): odds = lax.ppermute(handed, 'grp', apart(groups, 1))  6.96 us
    all_to_all x1, starting transfers between devices, body(): lax.all_to_all(minima_new, 'shard', split_axis=0, concat_axis=0, tiled=True)  6.95 us
    pallas_call x1, Pallas kernels, body(): pl.pallas_call(functools.partial(select_kernel, peers, slots, 256), in_sp...  5.22 us
    all_to_all x1, waiting for transfers between devices, body(): lax.all_to_all(minima_new, 'shard', split_axis=0, concat_axis=0, tiled=True)  4.93 us
    all_to_all x1, waiting for transfers between devices, body(): lax.all_to_all(minima_old, 'grp', split_axis=0, concat_axis=0, tiled=True)  4.68 us
  transfers between devices with their start and end apart: 11, of which 3 were waited for; matrix products, arithmetic and copies ran while one was open for 0% of the time, Pallas kernels for 15%

profile of v9, /device:TPU:1, one launch (start us, length us, event | category | flops | bytes accessed | tf_op | source)
XLA Modules:
  0.0 102.6 jit_solution(13590295547118671077)
XLA Ops:
  0.6 3.4 %shard_map.68 = bf16[768,768]{1,0:T(8,128)(2,1)} custom-call(bf16[1024,768]{1,0:T(8,128)(2,1)} %points_ref.11, s32[16,48]{1,0:T(8,128)} %bitcast.15), custom_call_target="tpu_custom_call" | custom-call | flops 1207959552 | bytes 2752512 | tf_op jit(solution)/shard_map/pallas_call | solution.py:102
  4.0 0.0 copy-start
  4.0 0.0 copy-start.2
  4.0 19.0 %all-to-all-start = ((bf16[48,16,768]{2,1,0:T(8,128)(2,1)}), bf16[48,16,768]{2,1,0:T(8,128)(2,1)S(1)}, u32[]{:S(2)}, u32[]{:S(2)}) async-start(bf16[48,16,768]{2,1,0:T(8,128)(2,1)} %bitcast.21), calls=%async_computation | async-start | bytes 2359296 | tf_op jit(solution)/shard_map/all_to_all | solution.py:364
  23.0 0.0 copy-done
  23.0 0.0 copy-done.2
  23.1 1.5 %shard_map.69 = (bf16[64,768]{1,0:T(8,128)(2,1)S(1)}, bf16[64,768]{1,0:T(8,128)(2,1)S(1)}, bf16[64,768]{1,0:T(8,128)(2,1)S(1)}, bf16[64,768]{1,0:T(8,128)(2,1)S(...) custom-call(bf16[1024,768]{1,0:T(8,128)(2,1)S(1)} %copy-done, ...), custom_call_target="tpu_custom_call" | custom-call | flops 805306368 | bytes 2359296 | tf_op jit(solution)/shard_map/pallas_call | solution.py:137
  24.5 0.0 copy-start.3
  24.5 7.4 %collective-permute-start = (bf16[64,768]{1,0:T(8,128)(2,1)S(1)}, bf16[64,768]{1,0:T(8,128)(2,1)S(1)}, u32[]{:S(2)}, u32[]{:S(2)}) collective-permute-start(bf16[64,768]{1,0:T(8,128)(2,1)S(1)} %get-tuple-element.26), channel_id=1, source_target_pairs={{0,384},{48,432},{96,480},{144,528},{192,576},{240,624},{288,672},... | collective-permute-start | bytes 294920 | tf_op jit(solution)/shard_map/ppermute | solution.py:371
  32.0 2.4 %collective-permute-start.1 = (bf16[64,768]{1,0:T(8,128)(2,1)S(1)}, bf16[64,768]{1,0:T(8,128)(2,1)S(1)}, u32[]{:S(2)}, u32[]{:S(2)}) collective-permute-start(bf16[64,768]{1,0:T(8,128)(2,1)S(1)} %get-tuple-element.27), channel_id=1, source_target_pairs={{0,192},{48,240},{96,288},{144,336},{192,0},{240,48},{288,96},{336... | collective-permute-start | bytes 294920 | tf_op jit(solution)/shard_map/ppermute | solution.py:371
  34.4 1.9 %collective-permute-start.2 = (bf16[64,768]{1,0:T(8,128)(2,1)S(1)}, bf16[64,768]{1,0:T(8,128)(2,1)S(1)}, u32[]{:S(2)}, u32[]{:S(2)}) collective-permute-start(bf16[64,768]{1,0:T(8,128)(2,1)S(1)} %get-tuple-element.28), channel_id=1, source_target_pairs={{0,576},{48,624},{96,672},{144,720},{192,384},{240,432},{288,480},... | collective-permute-start | bytes 294920 | tf_op jit(solution)/shard_map/ppermute | solution.py:371
  36.4 4.8 %collective-permute-start.3 = (bf16[64,768]{1,0:T(8,128)(2,1)S(1)}, bf16[64,768]{1,0:T(8,128)(2,1)S(1)}, u32[]{:S(2)}, u32[]{:S(2)}) collective-permute-start(bf16[64,768]{1,0:T(8,128)(2,1)S(1)} %get-tuple-element.29), channel_id=1, source_target_pairs={{0,288},{48,336},{96,192},{144,240},{192,96},{240,144},{288,0},{33... | collective-permute-start | bytes 294920 | tf_op jit(solution)/shard_map/ppermute | solution.py:371
  41.2 4.4 %collective-permute-start.4 = (bf16[64,768]{1,0:T(8,128)(2,1)S(1)}, bf16[64,768]{1,0:T(8,128)(2,1)S(1)}, u32[]{:S(2)}, u32[]{:S(2)}) collective-permute-start(bf16[64,768]{1,0:T(8,128)(2,1)S(1)} %get-tuple-element.30), channel_id=1, source_target_pairs={{0,672},{48,720},{96,576},{144,624},{192,480},{240,528},{288,384},... | collective-permute-start | bytes 294920 | tf_op jit(solution)/shard_map/ppermute | solution.py:371
  45.6 0.0 collective-permute-done.refs_0_
  45.6 1.9 %collective-permute-start.5 = (bf16[64,768]{1,0:T(8,128)(2,1)S(1)}, bf16[64,768]{1,0:T(8,128)(2,1)S(1)}, u32[]{:S(2)}, u32[]{:S(2)}) collective-permute-start(bf16[64,768]{1,0:T(8,128)(2,1)S(1)} %get-tuple-element.31), channel_id=1, source_target_pairs={{0,480},{48,528},{96,384},{144,432},{192,672},{240,720},{288,576},... | collective-permute-start | bytes 294920 | tf_op jit(solution)/shard_map/ppermute | solution.py:371
  47.5 0.0 collective-permute-done.1.refs_1_
  47.6 2.5 %collective-permute-start.6 = (bf16[64,768]{1,0:T(8,128)(2,1)S(1)}, bf16[64,768]{1,0:T(8,128)(2,1)S(1)}, u32[]{:S(2)}, u32[]{:S(2)}) collective-permute-start(bf16[64,768]{1,0:T(8,128)(2,1)S(1)} %get-tuple-element.32), channel_id=1, source_target_pairs={{0,96},{48,144},{96,0},{144,48},{192,288},{240,336},{288,192},{336... | collective-permute-start | bytes 294920 | tf_op jit(solution)/shard_map/ppermute | solution.py:371
  50.1 0.4 multiply_reduce_fusion
  50.5 0.0 collective-permute-done.2.refs_2_
  50.5 0.0 collective-permute-done.3.refs_3_
  50.5 0.0 collective-permute-done.4.refs_4_
  50.5 3.5 %collective-permute-done.5.refs_5_ = bf16[64,768]{1,0:T(8,128)(2,1)S(1)} collective-permute-done((bf16[64,768]{1,0:T(8,128)(2,1)S(1)}, bf16[64,768]{1,0:T(8,128)(2,1)S(1)}, u32[]{:S(2)}, u32[]{:S(2)}) %collective-permute-start.5) | collective-permute-done | bytes 98336 | tf_op jit(solution)/shard_map/ppermute | solution.py:371
  54.0 0.0 collective-permute-done.6.refs_6_
  54.0 0.1 shard_map.70
  54.0 7.0 %collective-permute-start.7 = (bf16[256,768]{1,0:T(8,128)(2,1)S(1)}, bf16[256,768]{1,0:T(8,128)(2,1)S(1)}, u32[]{:S(2)}, u32[]{:S(2)}) collective-permute-start(bf16[256,768]{1,0:T(8,128)(2,1)S(1)} %get-tuple-element.35), channel_id=1, source_target_pairs={{0,48},{48,0},{96,144},{144,96},{192,240},{240,192},{288,336},{336... | collective-permute-start | bytes 1179656 | tf_op jit(solution)/shard_map/ppermute | solution.py:382
  61.0 0.0 copy-done.3
  61.0 2.0 %shard_map.71 = (f32[8,32]{1,0:T(8,128)S(1)}, f32[128,1024]{1,0:T(8,128)}) custom-call(bf16[256,768]{1,0:T(8,128)(2,1)S(1)} %get-tuple-element.37.cand_ref, bf16[1024,768]{1,0:T(8,128)(2,1)S(1)} %copy-done, f32[1,1024]{1,0:T(1,128)S(1)} %bitcast.11, s32[1,16]{1,0:T(1,128)S(1)} %bitcast.17, s32[1]{0:T(128)} %bitcast.3.place_ref), custom_call_target="tpu_custom_call" | custom-call | flops 402653184 | bytes 1966080 | tf_op jit(solution)/shard_map/pallas_call | solution.py:388
  63.0 0.0 copy-start.4
  63.0 0.0 collective-permute-done.7.cand_ref
  63.0 3.2 %shard_map.72 = (bf16[16,1,32]{2,1,0:T(2,128)(2,1)}, f32[128,1024]{1,0:T(8,128)}) custom-call(bf16[256,768]{1,0:T(8,128)(2,1)S(1)} %collective-permute-done.7.cand_ref, bf16[1024,768]{1,0:T(8,128)(2,1)S(1)} %copy-done, f32[1,1024]{1,0:T(1,128)S(1)} %bitcast.12, s32[1,16]{1,0:T(1,128)S(1)} %bitcast.18, f32[8,32]{1,0:T(8,128)S(1)} %get-tuple-element.38.rows_ref, ...), custom_call_target="tpu_custom_call" | custom-call | flops 402653184 | bytes 1966080 | tf_op jit(solution)/shard_map/pallas_call | solution.py:400
  66.3 0.0 all-to-all-done
  66.3 9.9 %all-to-all-start.1 = ((bf16[16,1,32]{2,1,0:T(2,128)(2,1)}), bf16[16,1,32]{2,1,0:T(2,128)(2,1)S(1)}, u32[]{:S(2)}, u32[]{:S(2)}) async-start(bf16[16,1,32]{2,1,0:T(2,128)(2,1)} %get-tuple-element.42), calls=%async_computation.1 | async-start | bytes 16384 | tf_op jit(solution)/shard_map/all_to_all | solution.py:417
  76.2 0.0 copy-done.4
  76.3 2.3 %shard_map.73 = bf16[48,1,16]{2,1,0:T(2,128)(2,1)} custom-call(bf16[768,768]{1,0:T(8,128)(2,1)S(1)} %bitcast.9, bf16[1024,768]{1,0:T(8,128)(2,1)S(1)} %copy-done, f32[1,1024]{1,0:T(1,128)S(1)} %bitcast.13, s32[1,48]{1,0:T(1,128)S(1)} %bitcast.19), custom_call_target="tpu_custom_call" | custom-call | flops 1207959552 | bytes 2359296 | tf_op jit(solution)/shard_map/pallas_call | solution.py:420
  78.5 4.7 %all-to-all-done.1.old_back_ref = bf16[16,1,32]{2,1,0:T(2,128)(2,1)S(1)} async-done(((bf16[16,1,32]{2,1,0:T(2,128)(2,1)}), bf16[16,1,32]{2,1,0:T(2,128)(2,1)S(1)}, u32[]{:S(2)}, u32[]{:S(2)}) %all-to-all-start.1) | async-done | bytes 1056 | tf_op jit(solution)/shard_map/all_to_all | solution.py:417
  83.2 6.9 %all-to-all-start.2 = ((bf16[48,1,16]{2,1,0:T(2,128)(2,1)}), bf16[48,1,16]{2,1,0:T(2,128)(2,1)S(1)}, u32[]{:S(2)}, u32[]{:S(2)}) async-start(bf16[48,1,16]{2,1,0:T(2,128)(2,1)} %shard_map.73), calls=%async_computation.2 | async-start | bytes 49152 | tf_op jit(solution)/shard_map/all_to_all | solution.py:428
  90.1 0.0 copy-start.1
  90.2 5.2 %shard_map.74 = f32[16,1024]{1,0:T(8,128)} custom-call(bf16[768,768]{1,0:T(8,128)(2,1)S(1)} %bitcast.10, bf16[1024,768]{1,0:T(8,128)(2,1)S(1)} %copy-done, f32[1,1024]{1,0:T(1,128)S(1)} %bitcast.14, s32[1,48]{1,0:T(1,128)S(1)} %bitcast.20, f32[128,1024]{1,0:T(8,128)} %get-tuple-element.44.held_hbm_ref), custom_call_target="tpu_custom_call" | custom-call | flops 2415919104 | bytes 2359296 | tf_op jit(solution)/shard_map/pallas_call | solution.py:431
  95.4 0.0 copy-done.1
  95.4 0.9 shard_map.75
  96.3 4.9 %all-to-all-done.2.back_ref = bf16[48,1,16]{2,1,0:T(2,128)(2,1)S(1)} async-done(((bf16[48,1,16]{2,1,0:T(2,128)(2,1)}), bf16[48,1,16]{2,1,0:T(2,128)(2,1)S(1)}, u32[]{:S(2)}, u32[]{:S(2)}) %all-to-all-start.2) | async-done | bytes 1568 | tf_op jit(solution)/shard_map/all_to_all | solution.py:428
  101.3 1.3 %shard_map.76 = f32[8,128]{1,0:T(8,128)} custom-call(bf16[48,1,16]{2,1,0:T(2,128)(2,1)S(1)} %all-to-all-done.2.back_ref, f32[8,1024]{1,0:T(8,128)S(1)} %get-tuple-element.48.best_ref, s32[768,128]{1,0:T(8,128)S(1)} %get-tuple-element.49.wide_ref), custom_call_target="tpu_custom_call" | custom-call | tf_op jit(solution)/shard_map/pallas_call | solution.py:455
Async XLA Ops:
  4.0 19.0 %copy-start = (bf16[1024,768]{1,0:T(8,128)(2,1)S(1)}, bf16[1024,768]{1,0:T(8,128)(2,1)}, u32[]{:S(2)}) copy-start(bf16[1024,768]{1,0:T(8,128)(2,1)} %points_ref.11) | copy-start | bytes 4718596
  4.0 19.0 %copy-start.2 = (s32[16,32]{1,0:T(8,128)S(1)}, s32[16,32]{1,0:T(8,128)}, u32[]{:S(2)}) copy-start(s32[16,32]{1,0:T(8,128)} %old_lists_ref.1) | copy-start | bytes 6148
  4.0 62.3 %all-to-all-start = ((bf16[48,16,768]{2,1,0:T(8,128)(2,1)}), bf16[48,16,768]{2,1,0:T(8,128)(2,1)S(1)}, u32[]{:S(2)}, u32[]{:S(2)}) async-start(bf16[48,16,768]{2,1,0:T(8,128)(2,1)} %bitcast.21), calls=%async_computation | async-start | bytes 2359296 | tf_op jit(solution)/shard_map/all_to_all | solution.py:364
  24.5 36.5 %copy-start.3 = (s32[16,1]{0,1:T(1,128)S(1)}, s32[16,1]{0,1:T(1,128)}, u32[]{:S(2)}) copy-start(s32[16,1]{0,1:T(1,128)} %param.9) | copy-start | bytes 196
  24.5 21.1 %collective-permute-start = (bf16[64,768]{1,0:T(8,128)(2,1)S(1)}, bf16[64,768]{1,0:T(8,128)(2,1)S(1)}, u32[]{:S(2)}, u32[]{:S(2)}) collective-permute-start(bf16[64,768]{1,0:T(8,128)(2,1)S(1)} %get-tuple-element.26), channel_id=1, source_target_pairs={{0,384},{48,432},{96,480},{144,528},{192,576},{240,624},{288,672},... | collective-permute-start | bytes 294920 | tf_op jit(solution)/shard_map/ppermute | solution.py:371
  32.0 15.5 %collective-permute-start.1 = (bf16[64,768]{1,0:T(8,128)(2,1)S(1)}, bf16[64,768]{1,0:T(8,128)(2,1)S(1)}, u32[]{:S(2)}, u32[]{:S(2)}) collective-permute-start(bf16[64,768]{1,0:T(8,128)(2,1)S(1)} %get-tuple-element.27), channel_id=1, source_target_pairs={{0,192},{48,240},{96,288},{144,336},{192,0},{240,48},{288,96},{336... | collective-permute-start | bytes 294920 | tf_op jit(solution)/shard_map/ppermute | solution.py:371
  34.4 16.0 %collective-permute-start.2 = (bf16[64,768]{1,0:T(8,128)(2,1)S(1)}, bf16[64,768]{1,0:T(8,128)(2,1)S(1)}, u32[]{:S(2)}, u32[]{:S(2)}) collective-permute-start(bf16[64,768]{1,0:T(8,128)(2,1)S(1)} %get-tuple-element.28), channel_id=1, source_target_pairs={{0,576},{48,624},{96,672},{144,720},{192,384},{240,432},{288,480},... | collective-permute-start | bytes 294920 | tf_op jit(solution)/shard_map/ppermute | solution.py:371
  36.4 14.1 %collective-permute-start.3 = (bf16[64,768]{1,0:T(8,128)(2,1)S(1)}, bf16[64,768]{1,0:T(8,128)(2,1)S(1)}, u32[]{:S(2)}, u32[]{:S(2)}) collective-permute-start(bf16[64,768]{1,0:T(8,128)(2,1)S(1)} %get-tuple-element.29), channel_id=1, source_target_pairs={{0,288},{48,336},{96,192},{144,240},{192,96},{240,144},{288,0},{33... | collective-permute-start | bytes 294920 | tf_op jit(solution)/shard_map/ppermute | solution.py:371
  41.2 9.3 %collective-permute-start.4 = (bf16[64,768]{1,0:T(8,128)(2,1)S(1)}, bf16[64,768]{1,0:T(8,128)(2,1)S(1)}, u32[]{:S(2)}, u32[]{:S(2)}) collective-permute-start(bf16[64,768]{1,0:T(8,128)(2,1)S(1)} %get-tuple-element.30), channel_id=1, source_target_pairs={{0,672},{48,720},{96,576},{144,624},{192,480},{240,528},{288,384},... | collective-permute-start | bytes 294920 | tf_op jit(solution)/shard_map/ppermute | solution.py:371
  45.6 8.4 %collective-permute-start.5 = (bf16[64,768]{1,0:T(8,128)(2,1)S(1)}, bf16[64,768]{1,0:T(8,128)(2,1)S(1)}, u32[]{:S(2)}, u32[]{:S(2)}) collective-permute-start(bf16[64,768]{1,0:T(8,128)(2,1)S(1)} %get-tuple-element.31), channel_id=1, source_target_pairs={{0,480},{48,528},{96,384},{144,432},{192,672},{240,720},{288,576},... | collective-permute-start | bytes 294920 | tf_op jit(solution)/shard_map/ppermute | solution.py:371
  47.6 6.4 %collective-permute-start.6 = (bf16[64,768]{1,0:T(8,128)(2,1)S(1)}, bf16[64,768]{1,0:T(8,128)(2,1)S(1)}, u32[]{:S(2)}, u32[]{:S(2)}) collective-permute-start(bf16[64,768]{1,0:T(8,128)(2,1)S(1)} %get-tuple-element.32), channel_id=1, source_target_pairs={{0,96},{48,144},{96,0},{144,48},{192,288},{240,336},{288,192},{336... | collective-permute-start | bytes 294920 | tf_op jit(solution)/shard_map/ppermute | solution.py:371
  54.0 9.0 %collective-permute-start.7 = (bf16[256,768]{1,0:T(8,128)(2,1)S(1)}, bf16[256,768]{1,0:T(8,128)(2,1)S(1)}, u32[]{:S(2)}, u32[]{:S(2)}) collective-permute-start(bf16[256,768]{1,0:T(8,128)(2,1)S(1)} %get-tuple-element.35), channel_id=1, source_target_pairs={{0,48},{48,0},{96,144},{144,96},{192,240},{240,192},{288,336},{336... | collective-permute-start | bytes 1179656 | tf_op jit(solution)/shard_map/ppermute | solution.py:382
  63.0 13.2 %copy-start.4 = (s32[48,1]{0,1:T(1,128)S(1)}, s32[48,1]{0,1:T(1,128)}, u32[]{:S(2)}) copy-start(s32[48,1]{0,1:T(1,128)} %param.8) | copy-start | bytes 580
  66.3 16.9 %all-to-all-start.1 = ((bf16[16,1,32]{2,1,0:T(2,128)(2,1)}), bf16[16,1,32]{2,1,0:T(2,128)(2,1)S(1)}, u32[]{:S(2)}, u32[]{:S(2)}) async-start(bf16[16,1,32]{2,1,0:T(2,128)(2,1)} %get-tuple-element.42), calls=%async_computation.1 | async-start | bytes 16384 | tf_op jit(solution)/shard_map/all_to_all | solution.py:417
  83.2 18.1 %all-to-all-start.2 = ((bf16[48,1,16]{2,1,0:T(2,128)(2,1)}), bf16[48,1,16]{2,1,0:T(2,128)(2,1)S(1)}, u32[]{:S(2)}, u32[]{:S(2)}) async-start(bf16[48,1,16]{2,1,0:T(2,128)(2,1)} %shard_map.73), calls=%async_computation.2 | async-start | bytes 49152 | tf_op jit(solution)/shard_map/all_to_all | solution.py:428
  90.1 5.2 %copy-start.1 = (s32[48,16]{0,1:T(8,128)S(1)}, s32[48,16]{0,1:T(8,128)}, u32[]{:S(2)}) copy-start(s32[48,16]{0,1:T(8,128)} %param.6) | copy-start | bytes 9220

commit v10 on v9

--- a/solution.py
+++ b/solution.py
@@ -252,21 +252,25 @@
     hold(dist_ref, None, held_ref)
 
 
+def minima_old_kernel(groups, slots, cand_ref, points_ref, own_sq_ref, counts_ref, rows_ref, place_ref, minima_ref):
+    count = groups // 2
+    order = source_of(count, place_ref)
+    usable = usable_slots(counts_ref, count * slots, count * slots, groups, slots, order)
+    minima = jnp.where(usable, least_distances(cand_ref[...], points_ref, own_sq_ref), cap_value)
+    for k, row in enumerate(slot_rows(minima, slots)):
+        minima_ref[order(k)] = rows_ref[k : k + 1, :].astype(jnp.bfloat16)
+        minima_ref[order(count + k)] = row.astype(jnp.bfloat16)
+
+
 def odd_kernel(
-    groups, slots, cand_ref, points_ref, own_sq_ref, counts_ref, rows_ref, place_ref, before_hbm_ref,
-    minima_ref, held_ref, dist_ref, before_ref, sem,
+    groups, slots, cand_ref, points_ref, own_sq_ref, counts_ref, place_ref, before_hbm_ref, held_ref,
+    dist_ref, before_ref, sem,
 ):
     fetch = pltpu.make_async_copy(before_hbm_ref, before_ref, sem)
     fetch.start()
-    count = groups // 2
-    order = source_of(count, place_ref)
-    usable = usable_slots(counts_ref, count * slots, count * slots, groups, slots, order)
-    dist = distances(cand_ref[...], points_ref, own_sq_ref)
-    dist_ref[...] = jnp.where(usable, dist, far_value)
-    minima = jnp.where(usable, jnp.min(dist, axis=1, keepdims=True), cap_value)
-    for k, row in enumerate(slot_rows(minima, slots)):
-        minima_ref[order(k)] = rows_ref[k : k + 1, :].astype(jnp.bfloat16)
-        minima_ref[order(count + k)] = row.astype(jnp.bfloat16)
+    half = groups // 2 * slots
+    usable = usable_slots(counts_ref, half, half, groups, slots, source_of(groups // 2, place_ref))
+    dist_ref[...] = jnp.where(usable, distances(cand_ref[...], points_ref, own_sq_ref), far_value)
     fetch.wait()
     hold(dist_ref, before_ref, held_ref)
 
@@ -396,14 +400,34 @@
         compiler_params=params,
         cost_estimate=old_cost,
     )(evens, points, own_sq, counts_old, place)
+    minima_old = pl.pallas_call(
+        functools.partial(minima_old_kernel, groups, group_slots),
+        in_specs=[vmem] * 5 + [smem],
+        out_shape=jax.ShapeDtypeStruct((groups, 1, group_slots), jnp.bfloat16),
+        compiler_params=params,
+        cost_estimate=old_cost,
+    )(odds, points, own_sq, counts_old, minima_even, place)
+
+    pulled_new, minima_old = lax.optimization_barrier((pulled_new, minima_old))
+    back_old = lax.all_to_all(minima_old, "grp", split_axis=0, concat_axis=0, tiled=True)
+
+    total_new = peers * slots
+    minima_new = pl.pallas_call(
+        functools.partial(minima_kernel, peers, slots),
+        out_shape=jax.ShapeDtypeStruct((peers, 1, slots), jnp.bfloat16),
+        compiler_params=params,
+        cost_estimate=pl.CostEstimate(
+            flops=2 * total_new * rows * features, bytes_accessed=4 * total_new * features, transcendentals=0
+        ),
+    )(pulled_new, points, own_sq, counts_new)
+    back_new = lax.all_to_all(minima_new, "shard", split_axis=0, concat_axis=0, tiled=True)
+
+    odds, _ = lax.optimization_barrier((odds, pulled_new))
     hbm = pl.BlockSpec(memory_space=pltpu.HBM)
-    minima_old, held = pl.pallas_call(
+    held = pl.pallas_call(
         functools.partial(odd_kernel, groups, group_slots),
-        in_specs=[vmem] * 5 + [smem, hbm],
-        out_shape=(
-            jax.ShapeDtypeStruct((groups, 1, group_slots), jnp.bfloat16),
-            pltpu.HBM(held_shape, jnp.float32),
-        ),
+        in_specs=[vmem] * 4 + [smem, hbm],
+        out_shape=pltpu.HBM(held_shape, jnp.float32),
         scratch_shapes=[
             pltpu.VMEM((half, rows), jnp.float32),
             pltpu.VMEM(held_shape, jnp.float32),
@@ -411,22 +435,7 @@
         ],
         compiler_params=params,
         cost_estimate=old_cost,
-    )(odds, points, own_sq, counts_old, minima_even, place, pltpu.with_memory_space_constraint(held, pltpu.HBM))
-
-    pulled_new, minima_old = lax.optimization_barrier((pulled_new, minima_old))
-    back_old = lax.all_to_all(minima_old, "grp", split_axis=0, concat_axis=0, tiled=True)
-
-    total_new = peers * slots
-    minima_new = pl.pallas_call(
-        functools.partial(minima_kernel, peers, slots),
-        out_shape=jax.ShapeDtypeStruct((peers, 1, slots), jnp.bfloat16),
-        compiler_params=params,
-        cost_estimate=pl.CostEstimate(
-            flops=2 * total_new * rows * features, bytes_accessed=4 * total_new * features, transcendentals=0
-        ),
-    )(pulled_new, points, own_sq, counts_new)
-    back_new = lax.all_to_all(minima_new, "shard", split_axis=0, concat_axis=0, tiled=True)
-
+    )(odds, points, own_sq, counts_old, place, pltpu.with_memory_space_constraint(held, pltpu.HBM))
     pulled_new, back_old, _ = lax.optimization_barrier((pulled_new, back_old, minima_new))
     nearest = pl.pallas_call(
         functools.partial(select_kernel, peers, slots, 256),

time: 103 us -> 103 us (level)
  waiting for transfers between devices: 13.1 us -> 10.1 us
  starting transfers between devices: 68.3 us -> 70.4 us
    all_to_all x1, waiting for transfers between devices: 4.68 us -> 1.77 us  [body(): lax.all_to_all(minima_old, 'grp', split_axis=0, concat_axis=0, tiled=True)]
    all_to_all x1, starting transfers between devices: 9.95 us -> 11.8 us  [body(): lax.all_to_all(minima_old, 'grp', split_axis=0, concat_axis=0, tiled=True)]
    pallas_call x0 -> x1, Pallas kernels: none -> 1.33 us  [body(): pl.pallas_call(functools.partial(minima_old_kernel, groups, group_slots),...]
  transfers between devices with their start and end apart: 11 -> 11, of which waited for: 3 -> 4; matrix products, arithmetic and copies ran while one was open for 0% -> 0% of each run, Pallas kernels for 15% -> 16%
where the time goes in v10:
time: 103 us
  starting transfers between devices  70.4 us (68%)
  Pallas kernels  20.8 us (20%)
  waiting for transfers between devices  10.1 us (10%)
    ppermute x7, starting transfers between devices, body(): came = [lax.ppermute(pieces[k], 'grp', apart(groups, 2 * k)) for k in order]  25.5 us
    all_to_all x1, starting transfers between devices, body(): lax.all_to_all(offered_new.reshape(peers, slots, features), 'shard', spli...  19 us
    all_to_all x1, starting transfers between devices, body(): lax.all_to_all(minima_old, 'grp', split_axis=0, concat_axis=0, tiled=True)  11.8 us
    all_to_all x1, starting transfers between devices, body(): lax.all_to_all(minima_new, 'shard', split_axis=0, concat_axis=0, tiled=True)  7.13 us
    ppermute x1, starting transfers between devices, body(): odds = lax.ppermute(handed, 'grp', apart(groups, 1))  6.96 us
    pallas_call x1, Pallas kernels, body(): pl.pallas_call(functools.partial(select_kernel, peers, slots, 256), in_sp...  5.2 us
    all_to_all x1, waiting for transfers between devices, body(): lax.all_to_all(minima_new, 'shard', split_axis=0, concat_axis=0, tiled=True)  4.76 us
    ppermute x7, waiting for transfers between devices, body(): came = [lax.ppermute(pieces[k], 'grp', apart(groups, 2 * k)) for k in order]  3.5 us
  transfers between devices with their start and end apart: 11, of which 4 were waited for; matrix products, arithmetic and copies ran while one was open for 0% of the time, Pallas kernels for 16%

profile of v10, /device:TPU:1, one launch (start us, length us, event | category | flops | bytes accessed | tf_op | source)
XLA Modules:
  0.0 102.6 jit_solution(2724298591953072743)
XLA Ops:
  0.6 3.4 %shard_map.68 = bf16[768,768]{1,0:T(8,128)(2,1)} custom-call(bf16[1024,768]{1,0:T(8,128)(2,1)} %points_ref.13, s32[16,48]{1,0:T(8,128)} %bitcast.16), custom_call_target="tpu_custom_call" | custom-call | flops 1207959552 | bytes 2752512 | tf_op jit(solution)/shard_map/pallas_call | solution.py:102
  4.0 0.0 copy-start
  4.0 0.0 copy-start.2
  4.1 19.0 %all-to-all-start = ((bf16[48,16,768]{2,1,0:T(8,128)(2,1)}), bf16[48,16,768]{2,1,0:T(8,128)(2,1)S(1)}, u32[]{:S(2)}, u32[]{:S(2)}) async-start(bf16[48,16,768]{2,1,0:T(8,128)(2,1)} %bitcast.23), calls=%async_computation | async-start | bytes 2359296 | tf_op jit(solution)/shard_map/all_to_all | solution.py:368
  23.0 0.0 copy-done
  23.0 0.0 copy-done.2
  23.1 1.5 %shard_map.69 = (bf16[64,768]{1,0:T(8,128)(2,1)S(1)}, bf16[64,768]{1,0:T(8,128)(2,1)S(1)}, bf16[64,768]{1,0:T(8,128)(2,1)S(1)}, bf16[64,768]{1,0:T(8,128)(2,1)S(...) custom-call(bf16[1024,768]{1,0:T(8,128)(2,1)S(1)} %copy-done, ...), custom_call_target="tpu_custom_call" | custom-call | flops 805306368 | bytes 2359296 | tf_op jit(solution)/shard_map/pallas_call | solution.py:137
  24.5 0.0 copy-start.3
  24.6 7.5 %collective-permute-start = (bf16[64,768]{1,0:T(8,128)(2,1)S(1)}, bf16[64,768]{1,0:T(8,128)(2,1)S(1)}, u32[]{:S(2)}, u32[]{:S(2)}) collective-permute-start(bf16[64,768]{1,0:T(8,128)(2,1)S(1)} %get-tuple-element.25), channel_id=1, source_target_pairs={{0,384},{48,432},{96,480},{144,528},{192,576},{240,624},{288,672},... | collective-permute-start | bytes 294920 | tf_op jit(solution)/shard_map/ppermute | solution.py:375
  32.0 2.4 %collective-permute-start.1 = (bf16[64,768]{1,0:T(8,128)(2,1)S(1)}, bf16[64,768]{1,0:T(8,128)(2,1)S(1)}, u32[]{:S(2)}, u32[]{:S(2)}) collective-permute-start(bf16[64,768]{1,0:T(8,128)(2,1)S(1)} %get-tuple-element.26), channel_id=1, source_target_pairs={{0,192},{48,240},{96,288},{144,336},{192,0},{240,48},{288,96},{336... | collective-permute-start | bytes 294920 | tf_op jit(solution)/shard_map/ppermute | solution.py:375
  34.5 1.9 %collective-permute-start.2 = (bf16[64,768]{1,0:T(8,128)(2,1)S(1)}, bf16[64,768]{1,0:T(8,128)(2,1)S(1)}, u32[]{:S(2)}, u32[]{:S(2)}) collective-permute-start(bf16[64,768]{1,0:T(8,128)(2,1)S(1)} %get-tuple-element.27), channel_id=1, source_target_pairs={{0,576},{48,624},{96,672},{144,720},{192,384},{240,432},{288,480},... | collective-permute-start | bytes 294920 | tf_op jit(solution)/shard_map/ppermute | solution.py:375
  36.4 4.8 %collective-permute-start.3 = (bf16[64,768]{1,0:T(8,128)(2,1)S(1)}, bf16[64,768]{1,0:T(8,128)(2,1)S(1)}, u32[]{:S(2)}, u32[]{:S(2)}) collective-permute-start(bf16[64,768]{1,0:T(8,128)(2,1)S(1)} %get-tuple-element.28), channel_id=1, source_target_pairs={{0,288},{48,336},{96,192},{144,240},{192,96},{240,144},{288,0},{33... | collective-permute-start | bytes 294920 | tf_op jit(solution)/shard_map/ppermute | solution.py:375
  41.2 4.4 %collective-permute-start.4 = (bf16[64,768]{1,0:T(8,128)(2,1)S(1)}, bf16[64,768]{1,0:T(8,128)(2,1)S(1)}, u32[]{:S(2)}, u32[]{:S(2)}) collective-permute-start(bf16[64,768]{1,0:T(8,128)(2,1)S(1)} %get-tuple-element.29), channel_id=1, source_target_pairs={{0,672},{48,720},{96,576},{144,624},{192,480},{240,528},{288,384},... | collective-permute-start | bytes 294920 | tf_op jit(solution)/shard_map/ppermute | solution.py:375
  45.6 0.0 collective-permute-done.refs_0_
  45.6 1.9 %collective-permute-start.5 = (bf16[64,768]{1,0:T(8,128)(2,1)S(1)}, bf16[64,768]{1,0:T(8,128)(2,1)S(1)}, u32[]{:S(2)}, u32[]{:S(2)}) collective-permute-start(bf16[64,768]{1,0:T(8,128)(2,1)S(1)} %get-tuple-element.30), channel_id=1, source_target_pairs={{0,480},{48,528},{96,384},{144,432},{192,672},{240,720},{288,576},... | collective-permute-start | bytes 294920 | tf_op jit(solution)/shard_map/ppermute | solution.py:375
  47.6 0.0 collective-permute-done.1.refs_1_
  47.6 2.5 %collective-permute-start.6 = (bf16[64,768]{1,0:T(8,128)(2,1)S(1)}, bf16[64,768]{1,0:T(8,128)(2,1)S(1)}, u32[]{:S(2)}, u32[]{:S(2)}) collective-permute-start(bf16[64,768]{1,0:T(8,128)(2,1)S(1)} %get-tuple-element.31), channel_id=1, source_target_pairs={{0,96},{48,144},{96,0},{144,48},{192,288},{240,336},{288,192},{336... | collective-permute-start | bytes 294920 | tf_op jit(solution)/shard_map/ppermute | solution.py:375
  50.1 0.4 multiply_reduce_fusion
  50.5 0.0 collective-permute-done.2.refs_2_
  50.5 0.0 collective-permute-done.3.refs_3_
  50.5 0.0 collective-permute-done.4.refs_4_
  50.5 3.5 %collective-permute-done.5.refs_5_ = bf16[64,768]{1,0:T(8,128)(2,1)S(1)} collective-permute-done((bf16[64,768]{1,0:T(8,128)(2,1)S(1)}, bf16[64,768]{1,0:T(8,128)(2,1)S(1)}, u32[]{:S(2)}, u32[]{:S(2)}) %collective-permute-start.5) | collective-permute-done | bytes 98336 | tf_op jit(solution)/shard_map/ppermute | solution.py:375
  54.0 0.0 collective-permute-done.6.refs_6_
  54.0 0.1 shard_map.70
  54.1 7.0 %collective-permute-start.7 = (bf16[256,768]{1,0:T(8,128)(2,1)S(1)}, bf16[256,768]{1,0:T(8,128)(2,1)S(1)}, u32[]{:S(2)}, u32[]{:S(2)}) collective-permute-start(bf16[256,768]{1,0:T(8,128)(2,1)S(1)} %get-tuple-element.34), channel_id=1, source_target_pairs={{0,48},{48,0},{96,144},{144,96},{192,240},{240,192},{288,336},{336... | collective-permute-start | bytes 1179656 | tf_op jit(solution)/shard_map/ppermute | solution.py:386
  61.0 0.0 copy-done.3
  61.0 0.0 copy-start.4
  61.1 2.0 %shard_map.71 = (f32[8,32]{1,0:T(8,128)S(1)}, f32[128,1024]{1,0:T(8,128)}) custom-call(bf16[256,768]{1,0:T(8,128)(2,1)S(1)} %get-tuple-element.36.cand_ref, bf16[1024,768]{1,0:T(8,128)(2,1)S(1)} %copy-done, f32[1,1024]{1,0:T(1,128)S(1)} %bitcast.11, s32[1,16]{1,0:T(1,128)S(1)} %bitcast.18, s32[1]{0:T(128)} %bitcast.3.place_ref), custom_call_target="tpu_custom_call" | custom-call | flops 402653184 | bytes 1966080 | tf_op jit(solution)/shard_map/pallas_call | solution.py:392
  63.1 0.0 collective-permute-done.7.cand_ref
  63.1 1.3 %shard_map.72 = bf16[16,1,32]{2,1,0:T(2,128)(2,1)} custom-call(bf16[256,768]{1,0:T(8,128)(2,1)S(1)} %collective-permute-done.7.cand_ref, bf16[1024,768]{1,0:T(8,128)(2,1)S(1)} %copy-done, f32[1,1024]{1,0:T(1,128)S(1)} %bitcast.12, s32[1,16]{1,0:T(1,128)S(1)} %bitcast.19, f32[8,32]{1,0:T(8,128)S(1)} %get-tuple-element.37.rows_ref, s32[1]{0:T(128)} %bitcast.3.place_ref), custom_call_target="tpu_custom_call" | custom-call | flops 402653184 | bytes 1966080 | tf_op jit(solution)/shard_map/pallas_call | solution.py:403
  64.4 0.1 all-to-all-done
  64.4 11.8 %all-to-all-start.1 = ((bf16[16,1,32]{2,1,0:T(2,128)(2,1)}), bf16[16,1,32]{2,1,0:T(2,128)(2,1)S(1)}, u32[]{:S(2)}, u32[]{:S(2)}) async-start(bf16[16,1,32]{2,1,0:T(2,128)(2,1)} %shard_map.72), calls=%async_computation.1 | async-start | bytes 16384 | tf_op jit(solution)/shard_map/all_to_all | solution.py:412
  76.3 0.0 copy-done.4
  76.3 2.3 %shard_map.73 = bf16[48,1,16]{2,1,0:T(2,128)(2,1)} custom-call(bf16[768,768]{1,0:T(8,128)(2,1)S(1)} %bitcast.9, bf16[1024,768]{1,0:T(8,128)(2,1)S(1)} %copy-done, f32[1,1024]{1,0:T(1,128)S(1)} %bitcast.13, s32[1,48]{1,0:T(1,128)S(1)} %bitcast.21), custom_call_target="tpu_custom_call" | custom-call | flops 1207959552 | bytes 2359296 | tf_op jit(solution)/shard_map/pallas_call | solution.py:415
  78.5 2.9 %shard_map.74.held_hbm_ref = f32[128,1024]{1,0:T(8,128)} custom-call(bf16[256,768]{1,0:T(8,128)(2,1)S(1)} %collective-permute-done.7.cand_ref, bf16[1024,768]{1,0:T(8,128)(2,1)S(1)} %copy-done, f32[1,1024]{1,0:T(1,128)S(1)} %bitcast.14, s32[1,16]{1,0:T(1,128)S(1)} %bitcast.20, s32[1]{0:T(128)} %bitcast.3.place_ref, f32[128,1024]{1,0:T(8,128)} %get-tuple-element.42.before_hbm_ref), custom_call_target="tpu_custom_call" | custom-call | flops 402653184 | bytes 1966080 | tf_op jit(solution)/shard_map/pallas_call | solution.py:427
  81.4 1.8 %all-to-all-done.1.old_back_ref = bf16[16,1,32]{2,1,0:T(2,128)(2,1)S(1)} async-done(((bf16[16,1,32]{2,1,0:T(2,128)(2,1)}), bf16[16,1,32]{2,1,0:T(2,128)(2,1)S(1)}, u32[]{:S(2)}, u32[]{:S(2)}) %all-to-all-start.1) | async-done | bytes 1056 | tf_op jit(solution)/shard_map/all_to_all | solution.py:412
  83.2 7.1 %all-to-all-start.2 = ((bf16[48,1,16]{2,1,0:T(2,128)(2,1)}), bf16[48,1,16]{2,1,0:T(2,128)(2,1)S(1)}, u32[]{:S(2)}, u32[]{:S(2)}) async-start(bf16[48,1,16]{2,1,0:T(2,128)(2,1)} %shard_map.73), calls=%async_computation.2 | async-start | bytes 49152 | tf_op jit(solution)/shard_map/all_to_all | solution.py:423
  90.3 0.0 copy-start.1
  90.3 5.2 %shard_map.75 = f32[16,1024]{1,0:T(8,128)} custom-call(bf16[768,768]{1,0:T(8,128)(2,1)S(1)} %bitcast.10, bf16[1024,768]{1,0:T(8,128)(2,1)S(1)} %copy-done, f32[1,1024]{1,0:T(1,128)S(1)} %bitcast.15, s32[1,48]{1,0:T(1,128)S(1)} %bitcast.22, f32[128,1024]{1,0:T(8,128)} %shard_map.74.held_hbm_ref), custom_call_target="tpu_custom_call" | custom-call | flops 2415919104 | bytes 2359296 | tf_op jit(solution)/shard_map/pallas_call | solution.py:440
  95.6 0.0 copy-done.1
  95.6 0.9 shard_map.76
  96.5 4.8 %all-to-all-done.2.back_ref = bf16[48,1,16]{2,1,0:T(2,128)(2,1)S(1)} async-done(((bf16[48,1,16]{2,1,0:T(2,128)(2,1)}), bf16[48,1,16]{2,1,0:T(2,128)(2,1)S(1)}, u32[]{:S(2)}, u32[]{:S(2)}) %all-to-all-start.2) | async-done | bytes 1568 | tf_op jit(solution)/shard_map/all_to_all | solution.py:423
  101.3 1.3 %shard_map.77 = f32[8,128]{1,0:T(8,128)} custom-call(bf16[48,1,16]{2,1,0:T(2,128)(2,1)S(1)} %all-to-all-done.2.back_ref, f32[8,1024]{1,0:T(8,128)S(1)} %get-tuple-element.46.best_ref, s32[768,128]{1,0:T(8,128)S(1)} %get-tuple-element.47.wide_ref), custom_call_target="tpu_custom_call" | custom-call | tf_op jit(solution)/shard_map/pallas_call | solution.py:464
Async XLA Ops:
  4.0 19.0 %copy-start = (bf16[1024,768]{1,0:T(8,128)(2,1)S(1)}, bf16[1024,768]{1,0:T(8,128)(2,1)}, u32[]{:S(2)}) copy-start(bf16[1024,768]{1,0:T(8,128)(2,1)} %points_ref.13) | copy-start | bytes 4718596
  4.0 19.0 %copy-start.2 = (s32[16,32]{1,0:T(8,128)S(1)}, s32[16,32]{1,0:T(8,128)}, u32[]{:S(2)}) copy-start(s32[16,32]{1,0:T(8,128)} %old_lists_ref.1) | copy-start | bytes 6148
  4.1 60.4 %all-to-all-start = ((bf16[48,16,768]{2,1,0:T(8,128)(2,1)}), bf16[48,16,768]{2,1,0:T(8,128)(2,1)S(1)}, u32[]{:S(2)}, u32[]{:S(2)}) async-start(bf16[48,16,768]{2,1,0:T(8,128)(2,1)} %bitcast.23), calls=%async_computation | async-start | bytes 2359296 | tf_op jit(solution)/shard_map/all_to_all | solution.py:368
  24.5 36.5 %copy-start.3 = (s32[16,1]{0,1:T(1,128)S(1)}, s32[16,1]{0,1:T(1,128)}, u32[]{:S(2)}) copy-start(s32[16,1]{0,1:T(1,128)} %param.9) | copy-start | bytes 196
  24.6 21.1 %collective-permute-start = (bf16[64,768]{1,0:T(8,128)(2,1)S(1)}, bf16[64,768]{1,0:T(8,128)(2,1)S(1)}, u32[]{:S(2)}, u32[]{:S(2)}) collective-permute-start(bf16[64,768]{1,0:T(8,128)(2,1)S(1)} %get-tuple-element.25), channel_id=1, source_target_pairs={{0,384},{48,432},{96,480},{144,528},{192,576},{240,624},{288,672},... | collective-permute-start | bytes 294920 | tf_op jit(solution)/shard_map/ppermute | solution.py:375
  32.0 15.5 %collective-permute-start.1 = (bf16[64,768]{1,0:T(8,128)(2,1)S(1)}, bf16[64,768]{1,0:T(8,128)(2,1)S(1)}, u32[]{:S(2)}, u32[]{:S(2)}) collective-permute-start(bf16[64,768]{1,0:T(8,128)(2,1)S(1)} %get-tuple-element.26), channel_id=1, source_target_pairs={{0,192},{48,240},{96,288},{144,336},{192,0},{240,48},{288,96},{336... | collective-permute-start | bytes 294920 | tf_op jit(solution)/shard_map/ppermute | solution.py:375
  34.5 16.0 %collective-permute-start.2 = (bf16[64,768]{1,0:T(8,128)(2,1)S(1)}, bf16[64,768]{1,0:T(8,128)(2,1)S(1)}, u32[]{:S(2)}, u32[]{:S(2)}) collective-permute-start(bf16[64,768]{1,0:T(8,128)(2,1)S(1)} %get-tuple-element.27), channel_id=1, source_target_pairs={{0,576},{48,624},{96,672},{144,720},{192,384},{240,432},{288,480},... | collective-permute-start | bytes 294920 | tf_op jit(solution)/shard_map/ppermute | solution.py:375
  36.4 14.1 %collective-permute-start.3 = (bf16[64,768]{1,0:T(8,128)(2,1)S(1)}, bf16[64,768]{1,0:T(8,128)(2,1)S(1)}, u32[]{:S(2)}, u32[]{:S(2)}) collective-permute-start(bf16[64,768]{1,0:T(8,128)(2,1)S(1)} %get-tuple-element.28), channel_id=1, source_target_pairs={{0,288},{48,336},{96,192},{144,240},{192,96},{240,144},{288,0},{33... | collective-permute-start | bytes 294920 | tf_op jit(solution)/shard_map/ppermute | solution.py:375
  41.2 9.3 %collective-permute-start.4 = (bf16[64,768]{1,0:T(8,128)(2,1)S(1)}, bf16[64,768]{1,0:T(8,128)(2,1)S(1)}, u32[]{:S(2)}, u32[]{:S(2)}) collective-permute-start(bf16[64,768]{1,0:T(8,128)(2,1)S(1)} %get-tuple-element.29), channel_id=1, source_target_pairs={{0,672},{48,720},{96,576},{144,624},{192,480},{240,528},{288,384},... | collective-permute-start | bytes 294920 | tf_op jit(solution)/shard_map/ppermute | solution.py:375
  45.6 8.4 %collective-permute-start.5 = (bf16[64,768]{1,0:T(8,128)(2,1)S(1)}, bf16[64,768]{1,0:T(8,128)(2,1)S(1)}, u32[]{:S(2)}, u32[]{:S(2)}) collective-permute-start(bf16[64,768]{1,0:T(8,128)(2,1)S(1)} %get-tuple-element.30), channel_id=1, source_target_pairs={{0,480},{48,528},{96,384},{144,432},{192,672},{240,720},{288,576},... | collective-permute-start | bytes 294920 | tf_op jit(solution)/shard_map/ppermute | solution.py:375
  47.6 6.4 %collective-permute-start.6 = (bf16[64,768]{1,0:T(8,128)(2,1)S(1)}, bf16[64,768]{1,0:T(8,128)(2,1)S(1)}, u32[]{:S(2)}, u32[]{:S(2)}) collective-permute-start(bf16[64,768]{1,0:T(8,128)(2,1)S(1)} %get-tuple-element.31), channel_id=1, source_target_pairs={{0,96},{48,144},{96,0},{144,48},{192,288},{240,336},{288,192},{336... | collective-permute-start | bytes 294920 | tf_op jit(solution)/shard_map/ppermute | solution.py:375
  54.1 9.0 %collective-permute-start.7 = (bf16[256,768]{1,0:T(8,128)(2,1)S(1)}, bf16[256,768]{1,0:T(8,128)(2,1)S(1)}, u32[]{:S(2)}, u32[]{:S(2)}) collective-permute-start(bf16[256,768]{1,0:T(8,128)(2,1)S(1)} %get-tuple-element.34), channel_id=1, source_target_pairs={{0,48},{48,0},{96,144},{144,96},{192,240},{240,192},{288,336},{336... | collective-permute-start | bytes 1179656 | tf_op jit(solution)/shard_map/ppermute | solution.py:386
  61.0 15.2 %copy-start.4 = (s32[48,1]{0,1:T(1,128)S(1)}, s32[48,1]{0,1:T(1,128)}, u32[]{:S(2)}) copy-start(s32[48,1]{0,1:T(1,128)} %param.8) | copy-start | bytes 580
  64.4 18.8 %all-to-all-start.1 = ((bf16[16,1,32]{2,1,0:T(2,128)(2,1)}), bf16[16,1,32]{2,1,0:T(2,128)(2,1)S(1)}, u32[]{:S(2)}, u32[]{:S(2)}) async-start(bf16[16,1,32]{2,1,0:T(2,128)(2,1)} %shard_map.72), calls=%async_computation.1 | async-start | bytes 16384 | tf_op jit(solution)/shard_map/all_to_all | solution.py:412
  83.2 18.1 %all-to-all-start.2 = ((bf16[48,1,16]{2,1,0:T(2,128)(2,1)}), bf16[48,1,16]{2,1,0:T(2,128)(2,1)S(1)}, u32[]{:S(2)}, u32[]{:S(2)}) async-start(bf16[48,1,16]{2,1,0:T(2,128)(2,1)} %shard_map.73), calls=%async_computation.2 | async-start | bytes 49152 | tf_op jit(solution)/shard_map/all_to_all | solution.py:423
  90.3 5.2 %copy-start.1 = (s32[48,16]{0,1:T(8,128)S(1)}, s32[48,16]{0,1:T(8,128)}, u32[]{:S(2)}) copy-start(s32[48,16]{0,1:T(8,128)} %param.6) | copy-start | bytes 9220
